TPU v7x, 512 devices: a whole 4x8x8 slice. The times are simulated.
512 devices in a mesh: tm: 16 (over z, core), space: 32 (over x, y).
Axes of the slice: x: 4, y: 8, z: 8, core: 2. Of those that a mesh axis runs over, the one named last changes fastest.
Arguments:
- iterate: float32 [16, 32, 16, 16, 512], P('tm', 'space'), may hold values from -3 to 3
- source_term: float32 [16, 32, 16, 16, 512], P('tm', 'space'), may hold values from -6 to 6
- conductivity: float32 [32, 16, 16, 512], P('space'), may hold values from 0.5 to 4
Outputs:
- new_iterate: float32 [16, 32, 16, 16, 512], P('tm', 'space')
- residual: float32 [16, 32, 16, 16, 512], P('tm', 'space')
All inputs are finite; a program needn't handle non-finite values.
Results may differ from a plain program's by a relative error of at most 0.00002.
Values sent between devices are 32-bit elements; how exact they have to be, the bound alone decides.
No kernel may reach another device: no remote copies, remote signals or barrier semaphores. Data moves between devices by JAX's collectives and lax.ppermute only.
A program may use at most 64 MiB of HBM per device.

v0:
```python
import jax
import jax.numpy as jnp
from jax import lax
from jax.sharding import PartitionSpec as P

tau_step = 0.08
damping = 0.7


def shifted(block, axis, distance):
    devices = range(lax.axis_size(axis))
    route = [(i - distance, i) for i in devices if i - distance in devices]
    return lax.ppermute(block, axis, route)


def from_partner(value, axis, stride):
    mask = 2**stride
    pairs = [(source, source ^ mask) for source in range(lax.axis_size(axis))]
    return lax.ppermute(value, axis, pairs)


def neighbours(grid_field):
    below_rows = shifted(grid_field[..., -1:, :], "space", 1)
    above_rows = shifted(grid_field[..., :1, :], "space", -1)
    zero_col = jnp.zeros_like(grid_field[..., :1])
    zero_plane = jnp.zeros_like(grid_field[..., :1, :, :])
    return [
        jnp.concatenate([below_rows, grid_field[..., :-1, :]], axis=-2),
        jnp.concatenate([grid_field[..., 1:, :], above_rows], axis=-2),
        jnp.concatenate([zero_col, grid_field[..., :-1]], axis=-1),
        jnp.concatenate([grid_field[..., 1:], zero_col], axis=-1),
        jnp.concatenate([zero_plane, grid_field[..., :-1, :, :]], axis=-3),
        jnp.concatenate([grid_field[..., 1:, :, :], zero_plane], axis=-3),
    ]


def weights_from(conduct, conduct_near):
    weights = [0.5 * (conduct + other) for other in conduct_near]
    weight_sum = weights[0]
    for near_item in weights[1:]:
        weight_sum = weight_sum + near_item
    return (weights, weight_sum)


def earlier(grid_field, depth_level):
    if depth_level == 0:
        return shifted(grid_field, "tm", 1)
    if depth_level == 1:
        return shifted(grid_field, "tm", 2)
    return shifted(grid_field, "tm", 4)


def operator_from(update, near_list, previous, weights, weight_sum, step_size):
    flux_sum = weights[0] * near_list[0]
    for position in range(1, 6):
        flux_sum = flux_sum + weights[position] * near_list[position]
    return update - previous + step_size * (weight_sum * update - flux_sum)


def apply_operator(update, weights, weight_sum, step_size, depth_level):
    return operator_from(
        update, neighbours(update), earlier(update, depth_level), weights, weight_sum, step_size
    )


def smooth(rhs_field, weights, weight_sum, step_size, depth_level, want_left):
    diag_term = 1.0 + step_size * weight_sum
    update = damping * rhs_field / diag_term
    update = (
        update
        + damping
        * (rhs_field - apply_operator(update, weights, weight_sum, step_size, depth_level))
        / diag_term
    )
    if want_left:
        return (
            update,
            rhs_field - apply_operator(update, weights, weight_sum, step_size, depth_level),
        )
    return (update, update)


def level_weights(conduct):
    return weights_from(conduct, neighbours(conduct))


def shards(iterate, source_term, conductivity):
    state_here = iterate[0, 0]
    source_here = source_term[0, 0]
    conduct = conductivity[0] * (1.0 + state_here * state_here)
    both_near = neighbours(jnp.stack([state_here, conduct]))
    state_near = [near_item[0] for near_item in both_near]
    conduct_near = [near_item[1] for near_item in both_near]
    weights, weight_sum = weights_from(conduct, conduct_near)
    residual = source_here - operator_from(
        state_here, state_near, earlier(state_here, 0), weights, weight_sum, tau_step
    )
    fine_update, fine_left = smooth(residual, weights, weight_sum, tau_step, 0, True)
    partner = from_partner((fine_left, conduct), "tm", 0)
    mid_rhs = partner[0] + fine_left
    mid_conduct = 0.5 * (partner[1] + conduct)
    mid_weights, mid_sum = level_weights(mid_conduct)
    mid_update, mid_left = smooth(mid_rhs, mid_weights, mid_sum, 2.0 * tau_step, 1, True)
    partner_mid = from_partner((mid_left, mid_conduct), "tm", 1)
    top_rhs = partner_mid[0] + mid_left
    top_conduct = 0.5 * (partner_mid[1] + mid_conduct)
    top_weights, top_sum = level_weights(top_conduct)
    top_update, unused = smooth(top_rhs, top_weights, top_sum, 4.0 * tau_step, 2, False)
    mid_update = mid_update + top_update
    fine_update = fine_update + mid_update
    new_state = state_here + fine_update
    return (new_state[None, None], residual[None, None])


def solution(mesh):
    in_specs = (
        P("tm", "space", None, None, None),
        P("tm", "space", None, None, None),
        P("space", None, None, None),
    )
    out_specs = (P("tm", "space", None, None, None), P("tm", "space", None, None, None))
    return jax.shard_map(shards, mesh=mesh, in_specs=in_specs, out_specs=out_specs, check_vma=False)
```

profile of v0, /device:TPU:71, one launch (start us, length us, event | category | flops | bytes accessed | tf_op | source)
XLA Modules:
  0.0 152.1 jit_solution(8234664036856412608)
XLA Ops:
  0.6 1.4 add_multiply_fusion.10
  2.1 3.2 %collective-permute-start.1 = (f32[2,16,1,512]{3,2,1,0:T(1,128)S(1)}, f32[2,16,1,512]{3,2,1,0:T(1,128)S(1)}, u32[]{:S(2)}, u32[]{:S(2)}) collective-permute-start(f32[2,16,1,512]{3,2,1,0:T(1,128)S(1)} %get-tuple-element.17), channel_id=1, source_target_pairs={{0,1},{1,2},{2,3},{3,4},{4,5},{5,6},{6,7},{7,8},{8,9},{9,10},{10,1... | collective-permute-start | bytes 196616 | tf_op jit(solution)/shard_map/ppermute | solution.py:13
  5.3 4.2 %collective-permute-start.2 = (f32[2,16,1,512]{3,2,1,0:T(1,128)S(1)}, f32[2,16,1,512]{3,2,1,0:T(1,128)S(1)}, u32[]{:S(2)}, u32[]{:S(2)}) collective-permute-start(f32[2,16,1,512]{3,2,1,0:T(1,128)S(1)} %get-tuple-element.18), channel_id=1, source_target_pairs={{1,0},{2,1},{3,2},{4,3},{5,4},{6,5},{7,6},{8,7},{9,8},{10,9},{11,1... | collective-permute-start | bytes 196616 | tf_op jit(solution)/shard_map/ppermute | solution.py:13
  9.5 5.1 %collective-permute-start = (f32[16,16,512]{2,1,0:T(8,128)S(1)}, f32[16,16,512]{2,1,0:T(8,128)S(1)}, u32[]{:S(2)}, u32[]{:S(2)}) collective-permute-start(f32[16,16,512]{2,1,0:T(8,128)S(1)} %bitcast.118), channel_id=1, source_target_pairs={{0,32},{32,64},{64,96},{96,128},{128,160},{160,192},{192,224},{224... | collective-permute-start | bytes 1572872 | tf_op jit(solution)/shard_map/ppermute | solution.py:13
  14.8 0.2 fusion
  15.0 0.4 fusion.2
  15.5 5.3 %collective-permute-done = f32[16,16,512]{2,1,0:T(8,128)S(1)} collective-permute-done((f32[16,16,512]{2,1,0:T(8,128)S(1)}, f32[16,16,512]{2,1,0:T(8,128)S(1)}, u32[]{:S(2)}, u32[]{:S(2)}) %collective-permute-start) | collective-permute-done | bytes 524320 | tf_op jit(solution)/shard_map/ppermute | solution.py:13
  20.8 1.7 %fusion.107 = (f32[16,16,512]{2,1,0:T(8,128)S(1)}, f32[16,16,512]{2,1,0:T(8,128)S(1)}, f32[16,16,512]{2,1,0:T(8,128)S(1)}, f32[16,16,512]{2,1,0:T(8,128)S(1)}, f...) fusion(f32[2,16,16,512]{3,2,1,0:T(8,128)S(1)} %select_maximum_f, ...), kind=kLoop, calls=%fused_computation.165 | loop fusion | flops 5898240 | bytes 13037568 | tf_op jit(solution)/shard_map/div | solution.py:68
  22.8 4.4 %collective-permute-start.3 = (f32[16,16,512]{2,1,0:T(8,128)S(1)}, f32[16,16,512]{2,1,0:T(8,128)S(1)}, u32[]{:S(2)}, u32[]{:S(2)}) collective-permute-start(f32[16,16,512]{2,1,0:T(8,128)S(1)} %get-tuple-element.8), channel_id=1, source_target_pairs={{0,32},{32,64},{64,96},{96,128},{128,160},{160,192},{192,224},{224... | collective-permute-start | bytes 1572872 | tf_op jit(solution)/shard_map/ppermute | solution.py:13
  27.2 1.9 %collective-permute-start.4 = (f32[16,1,512]{2,1,0:T(1,128)S(1)}, f32[16,1,512]{2,1,0:T(1,128)S(1)}, u32[]{:S(2)}, u32[]{:S(2)}) collective-permute-start(f32[16,1,512]{2,1,0:T(1,128)S(1)} %get-tuple-element.80), channel_id=1, source_target_pairs={{0,1},{1,2},{2,3},{3,4},{4,5},{5,6},{6,7},{7,8},{8,9},{9,10},{10,1... | collective-permute-start | bytes 98312 | tf_op jit(solution)/shard_map/ppermute | solution.py:13
  29.1 5.5 %collective-permute-start.5 = (f32[16,1,512]{2,1,0:T(1,128)S(1)}, f32[16,1,512]{2,1,0:T(1,128)S(1)}, u32[]{:S(2)}, u32[]{:S(2)}) collective-permute-start(f32[16,1,512]{2,1,0:T(1,128)S(1)} %get-tuple-element.79), channel_id=1, source_target_pairs={{1,0},{2,1},{3,2},{4,3},{5,4},{6,5},{7,6},{8,7},{9,8},{10,9},{11,1... | collective-permute-start | bytes 98312 | tf_op jit(solution)/shard_map/ppermute | solution.py:13
  34.8 1.9 %collective-permute-start.10 = (f32[16,16,512]{2,1,0:T(8,128)S(1)}, f32[16,16,512]{2,1,0:T(8,128)S(1)}, u32[]{:S(2)}, u32[]{:S(2)}) collective-permute-start(f32[16,16,512]{2,1,0:T(8,128)S(1)} %get-tuple-element.16), channel_id=1, source_target_pairs={{0,32},{32,0},{64,96},{96,64},{128,160},{160,128},{192,224},{224,1... | collective-permute-start | bytes 1572872 | tf_op jit(solution)/shard_map/ppermute | solution.py:19
  36.8 1.0 fusion.55
  38.0 4.4 %collective-permute-start.6 = (f32[16,16,512]{2,1,0:T(8,128)S(1)}, f32[16,16,512]{2,1,0:T(8,128)S(1)}, u32[]{:S(2)}, u32[]{:S(2)}) collective-permute-start(f32[16,16,512]{2,1,0:T(8,128)S(1)} %fusion.55), channel_id=1, source_target_pairs={{0,32},{32,64},{64,96},{96,128},{128,160},{160,192},{192,224},{224... | collective-permute-start | bytes 1572872 | tf_op jit(solution)/shard_map/ppermute | solution.py:13
  42.4 1.9 %collective-permute-start.7 = (f32[16,1,512]{2,1,0:T(1,128)S(1)}, f32[16,1,512]{2,1,0:T(1,128)S(1)}, u32[]{:S(2)}, u32[]{:S(2)}) collective-permute-start(f32[16,1,512]{2,1,0:T(1,128)S(1)} %get-tuple-element.64), channel_id=1, source_target_pairs={{0,1},{1,2},{2,3},{3,4},{4,5},{5,6},{6,7},{7,8},{8,9},{9,10},{10,1... | collective-permute-start | bytes 98312 | tf_op jit(solution)/shard_map/ppermute | solution.py:13
  44.4 5.5 %collective-permute-start.8 = (f32[16,1,512]{2,1,0:T(1,128)S(1)}, f32[16,1,512]{2,1,0:T(1,128)S(1)}, u32[]{:S(2)}, u32[]{:S(2)}) collective-permute-start(f32[16,1,512]{2,1,0:T(1,128)S(1)} %get-tuple-element.63), channel_id=1, source_target_pairs={{1,0},{2,1},{3,2},{4,3},{5,4},{6,5},{7,6},{8,7},{9,8},{10,9},{11,1... | collective-permute-start | bytes 98312 | tf_op jit(solution)/shard_map/ppermute | solution.py:13
  50.2 0.2 fusion.141
  50.4 1.9 %collective-permute-start.11 = (f32[16,1,512]{2,1,0:T(1,128)S(1)}, f32[16,1,512]{2,1,0:T(1,128)S(1)}, u32[]{:S(2)}, u32[]{:S(2)}) collective-permute-start(f32[16,1,512]{2,1,0:T(1,128)S(1)} %get-tuple-element.65), channel_id=1, source_target_pairs={{0,1},{1,2},{2,3},{3,4},{4,5},{5,6},{6,7},{7,8},{8,9},{9,10},{10,1... | collective-permute-start | bytes 98312 | tf_op jit(solution)/shard_map/ppermute | solution.py:13
  52.3 5.5 %collective-permute-start.12 = (f32[16,1,512]{2,1,0:T(1,128)S(1)}, f32[16,1,512]{2,1,0:T(1,128)S(1)}, u32[]{:S(2)}, u32[]{:S(2)}) collective-permute-start(f32[16,1,512]{2,1,0:T(1,128)S(1)} %get-tuple-element.66), channel_id=1, source_target_pairs={{1,0},{2,1},{3,2},{4,3},{5,4},{6,5},{7,6},{8,7},{9,8},{10,9},{11,1... | collective-permute-start | bytes 98312 | tf_op jit(solution)/shard_map/ppermute | solution.py:13
  57.9 1.0 fusion.64
  58.9 1.9 %collective-permute-start.9 = (f32[16,16,512]{2,1,0:T(8,128)S(1)}, f32[16,16,512]{2,1,0:T(8,128)S(1)}, u32[]{:S(2)}, u32[]{:S(2)}) collective-permute-start(f32[16,16,512]{2,1,0:T(8,128)S(1)} %fusion.64), channel_id=1, source_target_pairs={{0,32},{32,0},{64,96},{96,64},{128,160},{160,128},{192,224},{224,1... | collective-permute-start | bytes 1572872 | tf_op jit(solution)/shard_map/ppermute | solution.py:19
  61.1 1.9 %collective-permute-start.20 = (f32[16,16,512]{2,1,0:T(8,128)S(1)}, f32[16,16,512]{2,1,0:T(8,128)S(1)}, u32[]{:S(2)}, u32[]{:S(2)}) collective-permute-start(f32[16,16,512]{2,1,0:T(8,128)S(1)} %add_multiply_fusion.9), channel_id=1, source_target_pairs={{0,64},{32,96},{64,0},{96,32},{128,192},{160,224},{192,128},{224,1... | collective-permute-start | bytes 1572872 | tf_op jit(solution)/shard_map/ppermute | solution.py:19
  63.0 0.7 fusion.106
  63.7 0.2 fusion.131
  63.9 7.6 %collective-permute-start.13 = (f32[16,16,512]{2,1,0:T(8,128)S(1)}, f32[16,16,512]{2,1,0:T(8,128)S(1)}, u32[]{:S(2)}, u32[]{:S(2)}) collective-permute-start(f32[16,16,512]{2,1,0:T(8,128)S(1)} %get-tuple-element.4), channel_id=1, source_target_pairs={{0,64},{32,96},{64,128},{96,160},{128,192},{160,224},{192,256},{22... | collective-permute-start | bytes 1572872 | tf_op jit(solution)/shard_map/ppermute | solution.py:13
  71.6 1.9 %collective-permute-start.14 = (f32[16,1,512]{2,1,0:T(1,128)S(1)}, f32[16,1,512]{2,1,0:T(1,128)S(1)}, u32[]{:S(2)}, u32[]{:S(2)}) collective-permute-start(f32[16,1,512]{2,1,0:T(1,128)S(1)} %get-tuple-element.56), channel_id=1, source_target_pairs={{0,1},{1,2},{2,3},{3,4},{4,5},{5,6},{6,7},{7,8},{8,9},{9,10},{10,1... | collective-permute-start | bytes 98312 | tf_op jit(solution)/shard_map/ppermute | solution.py:13
  73.6 5.5 %collective-permute-start.15 = (f32[16,1,512]{2,1,0:T(1,128)S(1)}, f32[16,1,512]{2,1,0:T(1,128)S(1)}, u32[]{:S(2)}, u32[]{:S(2)}) collective-permute-start(f32[16,1,512]{2,1,0:T(1,128)S(1)} %get-tuple-element.55), channel_id=1, source_target_pairs={{1,0},{2,1},{3,2},{4,3},{5,4},{6,5},{7,6},{8,7},{9,8},{10,9},{11,1... | collective-permute-start | bytes 98312 | tf_op jit(solution)/shard_map/ppermute | solution.py:13
  79.3 0.7 collective-permute-done.15
  80.1 7.1 %collective-permute-done.13 = f32[16,16,512]{2,1,0:T(8,128)S(1)} collective-permute-done((f32[16,16,512]{2,1,0:T(8,128)S(1)}, f32[16,16,512]{2,1,0:T(8,128)S(1)}, u32[]{:S(2)}, u32[]{:S(2)}) %collective-permute-start.13) | collective-permute-done | bytes 524320 | tf_op jit(solution)/shard_map/ppermute | solution.py:13
  87.2 1.2 fusion.78
  88.6 6.0 %collective-permute-start.16 = (f32[16,16,512]{2,1,0:T(8,128)S(1)}, f32[16,16,512]{2,1,0:T(8,128)S(1)}, u32[]{:S(2)}, u32[]{:S(2)}) collective-permute-start(f32[16,16,512]{2,1,0:T(8,128)S(1)} %fusion.78), channel_id=1, source_target_pairs={{0,64},{32,96},{64,128},{96,160},{128,192},{160,224},{192,256},{22... | collective-permute-start | bytes 1572872 | tf_op jit(solution)/shard_map/ppermute | solution.py:13
  94.7 1.9 %collective-permute-start.17 = (f32[16,1,512]{2,1,0:T(1,128)S(1)}, f32[16,1,512]{2,1,0:T(1,128)S(1)}, u32[]{:S(2)}, u32[]{:S(2)}) collective-permute-start(f32[16,1,512]{2,1,0:T(1,128)S(1)} %get-tuple-element.40), channel_id=1, source_target_pairs={{0,1},{1,2},{2,3},{3,4},{4,5},{5,6},{6,7},{7,8},{8,9},{9,10},{10,1... | collective-permute-start | bytes 98312 | tf_op jit(solution)/shard_map/ppermute | solution.py:13
  96.6 5.5 %collective-permute-start.18 = (f32[16,1,512]{2,1,0:T(1,128)S(1)}, f32[16,1,512]{2,1,0:T(1,128)S(1)}, u32[]{:S(2)}, u32[]{:S(2)}) collective-permute-start(f32[16,1,512]{2,1,0:T(1,128)S(1)} %get-tuple-element.39), channel_id=1, source_target_pairs={{1,0},{2,1},{3,2},{4,3},{5,4},{6,5},{7,6},{8,7},{9,8},{10,9},{11,1... | collective-permute-start | bytes 98312 | tf_op jit(solution)/shard_map/ppermute | solution.py:13
  102.4 0.8 collective-permute-done.18
  103.1 2.0 %collective-permute-done.16 = f32[16,16,512]{2,1,0:T(8,128)S(1)} collective-permute-done((f32[16,16,512]{2,1,0:T(8,128)S(1)}, f32[16,16,512]{2,1,0:T(8,128)S(1)}, u32[]{:S(2)}, u32[]{:S(2)}) %collective-permute-start.16) | collective-permute-done | bytes 524320 | tf_op jit(solution)/shard_map/ppermute | solution.py:13
  105.1 1.3 fusion.87
  106.5 1.9 %collective-permute-start.19 = (f32[16,16,512]{2,1,0:T(8,128)S(1)}, f32[16,16,512]{2,1,0:T(8,128)S(1)}, u32[]{:S(2)}, u32[]{:S(2)}) collective-permute-start(f32[16,16,512]{2,1,0:T(8,128)S(1)} %get-tuple-element.31), channel_id=1, source_target_pairs={{0,64},{32,96},{64,0},{96,32},{128,192},{160,224},{192,128},{224,1... | collective-permute-start | bytes 1572872 | tf_op jit(solution)/shard_map/ppermute | solution.py:19
  108.5 1.9 %collective-permute-start.21 = (f32[16,1,512]{2,1,0:T(1,128)S(1)}, f32[16,1,512]{2,1,0:T(1,128)S(1)}, u32[]{:S(2)}, u32[]{:S(2)}) collective-permute-start(f32[16,1,512]{2,1,0:T(1,128)S(1)} %get-tuple-element.41), channel_id=1, source_target_pairs={{0,1},{1,2},{2,3},{3,4},{4,5},{5,6},{6,7},{7,8},{8,9},{9,10},{10,1... | collective-permute-start | bytes 98312 | tf_op jit(solution)/shard_map/ppermute | solution.py:13
  110.4 5.7 %collective-permute-start.22 = (f32[16,1,512]{2,1,0:T(1,128)S(1)}, f32[16,1,512]{2,1,0:T(1,128)S(1)}, u32[]{:S(2)}, u32[]{:S(2)}) collective-permute-start(f32[16,1,512]{2,1,0:T(1,128)S(1)} %get-tuple-element.42), channel_id=1, source_target_pairs={{1,0},{2,1},{3,2},{4,3},{5,4},{6,5},{7,6},{8,7},{9,8},{10,9},{11,1... | collective-permute-start | bytes 98312 | tf_op jit(solution)/shard_map/ppermute | solution.py:13
  116.4 0.5 collective-permute-done.22
  116.9 3.3 %collective-permute-done.19 = f32[16,16,512]{2,1,0:T(8,128)S(1)} collective-permute-done((f32[16,16,512]{2,1,0:T(8,128)S(1)}, f32[16,16,512]{2,1,0:T(8,128)S(1)}, u32[]{:S(2)}, u32[]{:S(2)}) %collective-permute-start.19) | collective-permute-done | bytes 524320 | tf_op jit(solution)/shard_map/ppermute | solution.py:19
  120.2 0.7 fusion.105
  120.9 6.1 %collective-permute-start.23 = (f32[16,16,512]{2,1,0:T(8,128)S(1)}, f32[16,16,512]{2,1,0:T(8,128)S(1)}, u32[]{:S(2)}, u32[]{:S(2)}) collective-permute-start(f32[16,16,512]{2,1,0:T(8,128)S(1)} %get-tuple-element.2), channel_id=1, source_target_pairs={{0,128},{32,160},{64,192},{96,224},{128,256},{160,288},{192,320},{... | collective-permute-start | bytes 1572872 | tf_op jit(solution)/shard_map/ppermute | solution.py:13
  127.0 1.9 %collective-permute-start.24 = (f32[16,1,512]{2,1,0:T(1,128)S(1)}, f32[16,1,512]{2,1,0:T(1,128)S(1)}, u32[]{:S(2)}, u32[]{:S(2)}) collective-permute-start(f32[16,1,512]{2,1,0:T(1,128)S(1)} %get-tuple-element.23), channel_id=1, source_target_pairs={{0,1},{1,2},{2,3},{3,4},{4,5},{5,6},{6,7},{7,8},{8,9},{9,10},{10,1... | collective-permute-start | bytes 98312 | tf_op jit(solution)/shard_map/ppermute | solution.py:13
  129.0 5.5 %collective-permute-start.25 = (f32[16,1,512]{2,1,0:T(1,128)S(1)}, f32[16,1,512]{2,1,0:T(1,128)S(1)}, u32[]{:S(2)}, u32[]{:S(2)}) collective-permute-start(f32[16,1,512]{2,1,0:T(1,128)S(1)} %get-tuple-element.24), channel_id=1, source_target_pairs={{1,0},{2,1},{3,2},{4,3},{5,4},{6,5},{7,6},{8,7},{9,8},{10,9},{11,1... | collective-permute-start | bytes 98312 | tf_op jit(solution)/shard_map/ppermute | solution.py:13
  134.8 0.7 collective-permute-done.25
  135.4 14.4 %collective-permute-done.23 = f32[16,16,512]{2,1,0:T(8,128)S(1)} collective-permute-done((f32[16,16,512]{2,1,0:T(8,128)S(1)}, f32[16,16,512]{2,1,0:T(8,128)S(1)}, u32[]{:S(2)}, u32[]{:S(2)}) %collective-permute-start.23) | collective-permute-done | bytes 524320 | tf_op jit(solution)/shard_map/ppermute | solution.py:13
  149.8 2.2 %fusion.108 = f32[1,1,16,16,512]{4,3,2,1,0:T(8,128)} fusion(f32[16,16,512]{2,1,0:T(8,128)S(1)} %fusion.55, f32[16,16,512]{2,1,0:T(8,128)S(1)} %fusion.78, f32[16,16,512]{2,1,0:T(8,128)S(1)} %get-tuple-element.3, f32[15,16,512]{2,1,0:T(8,128)S(1)} %get-tuple-element.30, f32[15,16,512]{2,1,0:T(8,128)S(1)} %get-tuple-element.29, ...), kind=kLoop, calls=%fused_computation.168 | loop fusion | flops 6291456 | bytes 9826304 | tf_op jit(solution)/shard_map/broadcast_in_dim | solution.py:112
  (55 shorter events, 3.3 us)
Async XLA Ops:
  0.6 1.4 copy-start
  2.1 13.3 %collective-permute-start.1 = (f32[2,16,1,512]{3,2,1,0:T(1,128)S(1)}, f32[2,16,1,512]{3,2,1,0:T(1,128)S(1)}, u32[]{:S(2)}, u32[]{:S(2)}) collective-permute-start(f32[2,16,1,512]{3,2,1,0:T(1,128)S(1)} %get-tuple-element.17), channel_id=1, source_target_pairs={{0,1},{1,2},{2,3},{3,4},{4,5},{5,6},{6,7},{7,8},{8,9},{9,10},{10,1... | collective-permute-start | bytes 196616 | tf_op jit(solution)/shard_map/ppermute | solution.py:13
  5.3 10.1 %collective-permute-start.2 = (f32[2,16,1,512]{3,2,1,0:T(1,128)S(1)}, f32[2,16,1,512]{3,2,1,0:T(1,128)S(1)}, u32[]{:S(2)}, u32[]{:S(2)}) collective-permute-start(f32[2,16,1,512]{3,2,1,0:T(1,128)S(1)} %get-tuple-element.18), channel_id=1, source_target_pairs={{1,0},{2,1},{3,2},{4,3},{5,4},{6,5},{7,6},{8,7},{9,8},{10,9},{11,1... | collective-permute-start | bytes 196616 | tf_op jit(solution)/shard_map/ppermute | solution.py:13
  9.5 11.2 %collective-permute-start = (f32[16,16,512]{2,1,0:T(8,128)S(1)}, f32[16,16,512]{2,1,0:T(8,128)S(1)}, u32[]{:S(2)}, u32[]{:S(2)}) collective-permute-start(f32[16,16,512]{2,1,0:T(8,128)S(1)} %bitcast.118), channel_id=1, source_target_pairs={{0,32},{32,64},{64,96},{96,128},{128,160},{160,192},{192,224},{224... | collective-permute-start | bytes 1572872 | tf_op jit(solution)/shard_map/ppermute | solution.py:13
  15.4 5.4 %copy-start.2 = (f32[1,16,16,512]{3,2,1,0:T(8,128)S(1)}, f32[1,16,16,512]{3,2,1,0:T(8,128)}, u32[]{:S(2)}) copy-start(f32[1,16,16,512]{3,2,1,0:T(8,128)} %param.5) | copy-start | bytes 1572868
  15.4 5.4 %copy-start.3 = (f32[1,1,16,16,512]{4,3,2,1,0:T(8,128)S(1)}, f32[1,1,16,16,512]{4,3,2,1,0:T(8,128)}, u32[]{:S(2)}) copy-start(f32[1,1,16,16,512]{4,3,2,1,0:T(8,128)} %param.4) | copy-start | bytes 1572868
  22.5 35.4 %copy-start.1 = (f32[16,16,512]{2,1,0:T(8,128)}, f32[16,16,512]{2,1,0:T(8,128)S(1)}, u32[]{:S(2)}) copy-start(f32[16,16,512]{2,1,0:T(8,128)S(1)} %get-tuple-element.9) | copy-start | bytes 1572868
  22.8 14.0 %collective-permute-start.3 = (f32[16,16,512]{2,1,0:T(8,128)S(1)}, f32[16,16,512]{2,1,0:T(8,128)S(1)}, u32[]{:S(2)}, u32[]{:S(2)}) collective-permute-start(f32[16,16,512]{2,1,0:T(8,128)S(1)} %get-tuple-element.8), channel_id=1, source_target_pairs={{0,32},{32,64},{64,96},{96,128},{128,160},{160,192},{192,224},{224... | collective-permute-start | bytes 1572872 | tf_op jit(solution)/shard_map/ppermute | solution.py:13
  27.2 9.6 %collective-permute-start.4 = (f32[16,1,512]{2,1,0:T(1,128)S(1)}, f32[16,1,512]{2,1,0:T(1,128)S(1)}, u32[]{:S(2)}, u32[]{:S(2)}) collective-permute-start(f32[16,1,512]{2,1,0:T(1,128)S(1)} %get-tuple-element.80), channel_id=1, source_target_pairs={{0,1},{1,2},{2,3},{3,4},{4,5},{5,6},{6,7},{7,8},{8,9},{9,10},{10,1... | collective-permute-start | bytes 98312 | tf_op jit(solution)/shard_map/ppermute | solution.py:13
  29.1 7.7 %collective-permute-start.5 = (f32[16,1,512]{2,1,0:T(1,128)S(1)}, f32[16,1,512]{2,1,0:T(1,128)S(1)}, u32[]{:S(2)}, u32[]{:S(2)}) collective-permute-start(f32[16,1,512]{2,1,0:T(1,128)S(1)} %get-tuple-element.79), channel_id=1, source_target_pairs={{1,0},{2,1},{3,2},{4,3},{5,4},{6,5},{7,6},{8,7},{9,8},{10,9},{11,1... | collective-permute-start | bytes 98312 | tf_op jit(solution)/shard_map/ppermute | solution.py:13
  34.8 15.2 %collective-permute-start.10 = (f32[16,16,512]{2,1,0:T(8,128)S(1)}, f32[16,16,512]{2,1,0:T(8,128)S(1)}, u32[]{:S(2)}, u32[]{:S(2)}) collective-permute-start(f32[16,16,512]{2,1,0:T(8,128)S(1)} %get-tuple-element.16), channel_id=1, source_target_pairs={{0,32},{32,0},{64,96},{96,64},{128,160},{160,128},{192,224},{224,1... | collective-permute-start | bytes 1572872 | tf_op jit(solution)/shard_map/ppermute | solution.py:19
  38.0 19.9 %collective-permute-start.6 = (f32[16,16,512]{2,1,0:T(8,128)S(1)}, f32[16,16,512]{2,1,0:T(8,128)S(1)}, u32[]{:S(2)}, u32[]{:S(2)}) collective-permute-start(f32[16,16,512]{2,1,0:T(8,128)S(1)} %fusion.55), channel_id=1, source_target_pairs={{0,32},{32,64},{64,96},{96,128},{128,160},{160,192},{192,224},{224... | collective-permute-start | bytes 1572872 | tf_op jit(solution)/shard_map/ppermute | solution.py:13
  42.4 15.4 %collective-permute-start.7 = (f32[16,1,512]{2,1,0:T(1,128)S(1)}, f32[16,1,512]{2,1,0:T(1,128)S(1)}, u32[]{:S(2)}, u32[]{:S(2)}) collective-permute-start(f32[16,1,512]{2,1,0:T(1,128)S(1)} %get-tuple-element.64), channel_id=1, source_target_pairs={{0,1},{1,2},{2,3},{3,4},{4,5},{5,6},{6,7},{7,8},{8,9},{9,10},{10,1... | collective-permute-start | bytes 98312 | tf_op jit(solution)/shard_map/ppermute | solution.py:13
  44.4 13.5 %collective-permute-start.8 = (f32[16,1,512]{2,1,0:T(1,128)S(1)}, f32[16,1,512]{2,1,0:T(1,128)S(1)}, u32[]{:S(2)}, u32[]{:S(2)}) collective-permute-start(f32[16,1,512]{2,1,0:T(1,128)S(1)} %get-tuple-element.63), channel_id=1, source_target_pairs={{1,0},{2,1},{3,2},{4,3},{5,4},{6,5},{7,6},{8,7},{9,8},{10,9},{11,1... | collective-permute-start | bytes 98312 | tf_op jit(solution)/shard_map/ppermute | solution.py:13
  50.4 12.6 %collective-permute-start.11 = (f32[16,1,512]{2,1,0:T(1,128)S(1)}, f32[16,1,512]{2,1,0:T(1,128)S(1)}, u32[]{:S(2)}, u32[]{:S(2)}) collective-permute-start(f32[16,1,512]{2,1,0:T(1,128)S(1)} %get-tuple-element.65), channel_id=1, source_target_pairs={{0,1},{1,2},{2,3},{3,4},{4,5},{5,6},{6,7},{7,8},{8,9},{9,10},{10,1... | collective-permute-start | bytes 98312 | tf_op jit(solution)/shard_map/ppermute | solution.py:13
  52.3 10.6 %collective-permute-start.12 = (f32[16,1,512]{2,1,0:T(1,128)S(1)}, f32[16,1,512]{2,1,0:T(1,128)S(1)}, u32[]{:S(2)}, u32[]{:S(2)}) collective-permute-start(f32[16,1,512]{2,1,0:T(1,128)S(1)} %get-tuple-element.66), channel_id=1, source_target_pairs={{1,0},{2,1},{3,2},{4,3},{5,4},{6,5},{7,6},{8,7},{9,8},{10,9},{11,1... | collective-permute-start | bytes 98312 | tf_op jit(solution)/shard_map/ppermute | solution.py:13
  58.9 4.1 %collective-permute-start.9 = (f32[16,16,512]{2,1,0:T(8,128)S(1)}, f32[16,16,512]{2,1,0:T(8,128)S(1)}, u32[]{:S(2)}, u32[]{:S(2)}) collective-permute-start(f32[16,16,512]{2,1,0:T(8,128)S(1)} %fusion.64), channel_id=1, source_target_pairs={{0,32},{32,0},{64,96},{96,64},{128,160},{160,128},{192,224},{224,1... | collective-permute-start | bytes 1572872 | tf_op jit(solution)/shard_map/ppermute | solution.py:19
  61.1 41.3 %collective-permute-start.20 = (f32[16,16,512]{2,1,0:T(8,128)S(1)}, f32[16,16,512]{2,1,0:T(8,128)S(1)}, u32[]{:S(2)}, u32[]{:S(2)}) collective-permute-start(f32[16,16,512]{2,1,0:T(8,128)S(1)} %add_multiply_fusion.9), channel_id=1, source_target_pairs={{0,64},{32,96},{64,0},{96,32},{128,192},{160,224},{192,128},{224,1... | collective-permute-start | bytes 1572872 | tf_op jit(solution)/shard_map/ppermute | solution.py:19
  63.9 23.2 %collective-permute-start.13 = (f32[16,16,512]{2,1,0:T(8,128)S(1)}, f32[16,16,512]{2,1,0:T(8,128)S(1)}, u32[]{:S(2)}, u32[]{:S(2)}) collective-permute-start(f32[16,16,512]{2,1,0:T(8,128)S(1)} %get-tuple-element.4), channel_id=1, source_target_pairs={{0,64},{32,96},{64,128},{96,160},{128,192},{160,224},{192,256},{22... | collective-permute-start | bytes 1572872 | tf_op jit(solution)/shard_map/ppermute | solution.py:13
  71.6 7.7 %collective-permute-start.14 = (f32[16,1,512]{2,1,0:T(1,128)S(1)}, f32[16,1,512]{2,1,0:T(1,128)S(1)}, u32[]{:S(2)}, u32[]{:S(2)}) collective-permute-start(f32[16,1,512]{2,1,0:T(1,128)S(1)} %get-tuple-element.56), channel_id=1, source_target_pairs={{0,1},{1,2},{2,3},{3,4},{4,5},{5,6},{6,7},{7,8},{8,9},{9,10},{10,1... | collective-permute-start | bytes 98312 | tf_op jit(solution)/shard_map/ppermute | solution.py:13
  73.6 6.5 %collective-permute-start.15 = (f32[16,1,512]{2,1,0:T(1,128)S(1)}, f32[16,1,512]{2,1,0:T(1,128)S(1)}, u32[]{:S(2)}, u32[]{:S(2)}) collective-permute-start(f32[16,1,512]{2,1,0:T(1,128)S(1)} %get-tuple-element.55), channel_id=1, source_target_pairs={{1,0},{2,1},{3,2},{4,3},{5,4},{6,5},{7,6},{8,7},{9,8},{10,9},{11,1... | collective-permute-start | bytes 98312 | tf_op jit(solution)/shard_map/ppermute | solution.py:13
  88.6 16.4 %collective-permute-start.16 = (f32[16,16,512]{2,1,0:T(8,128)S(1)}, f32[16,16,512]{2,1,0:T(8,128)S(1)}, u32[]{:S(2)}, u32[]{:S(2)}) collective-permute-start(f32[16,16,512]{2,1,0:T(8,128)S(1)} %fusion.78), channel_id=1, source_target_pairs={{0,64},{32,96},{64,128},{96,160},{128,192},{160,224},{192,256},{22... | collective-permute-start | bytes 1572872 | tf_op jit(solution)/shard_map/ppermute | solution.py:13
  94.7 7.6 %collective-permute-start.17 = (f32[16,1,512]{2,1,0:T(1,128)S(1)}, f32[16,1,512]{2,1,0:T(1,128)S(1)}, u32[]{:S(2)}, u32[]{:S(2)}) collective-permute-start(f32[16,1,512]{2,1,0:T(1,128)S(1)} %get-tuple-element.40), channel_id=1, source_target_pairs={{0,1},{1,2},{2,3},{3,4},{4,5},{5,6},{6,7},{7,8},{8,9},{9,10},{10,1... | collective-permute-start | bytes 98312 | tf_op jit(solution)/shard_map/ppermute | solution.py:13
  96.6 6.5 %collective-permute-start.18 = (f32[16,1,512]{2,1,0:T(1,128)S(1)}, f32[16,1,512]{2,1,0:T(1,128)S(1)}, u32[]{:S(2)}, u32[]{:S(2)}) collective-permute-start(f32[16,1,512]{2,1,0:T(1,128)S(1)} %get-tuple-element.39), channel_id=1, source_target_pairs={{1,0},{2,1},{3,2},{4,3},{5,4},{6,5},{7,6},{8,7},{9,8},{10,9},{11,1... | collective-permute-start | bytes 98312 | tf_op jit(solution)/shard_map/ppermute | solution.py:13
  106.5 13.6 %collective-permute-start.19 = (f32[16,16,512]{2,1,0:T(8,128)S(1)}, f32[16,16,512]{2,1,0:T(8,128)S(1)}, u32[]{:S(2)}, u32[]{:S(2)}) collective-permute-start(f32[16,16,512]{2,1,0:T(8,128)S(1)} %get-tuple-element.31), channel_id=1, source_target_pairs={{0,64},{32,96},{64,0},{96,32},{128,192},{160,224},{192,128},{224,1... | collective-permute-start | bytes 1572872 | tf_op jit(solution)/shard_map/ppermute | solution.py:19
  108.5 7.9 %collective-permute-start.21 = (f32[16,1,512]{2,1,0:T(1,128)S(1)}, f32[16,1,512]{2,1,0:T(1,128)S(1)}, u32[]{:S(2)}, u32[]{:S(2)}) collective-permute-start(f32[16,1,512]{2,1,0:T(1,128)S(1)} %get-tuple-element.41), channel_id=1, source_target_pairs={{0,1},{1,2},{2,3},{3,4},{4,5},{5,6},{6,7},{7,8},{8,9},{9,10},{10,1... | collective-permute-start | bytes 98312 | tf_op jit(solution)/shard_map/ppermute | solution.py:13
  110.4 6.5 %collective-permute-start.22 = (f32[16,1,512]{2,1,0:T(1,128)S(1)}, f32[16,1,512]{2,1,0:T(1,128)S(1)}, u32[]{:S(2)}, u32[]{:S(2)}) collective-permute-start(f32[16,1,512]{2,1,0:T(1,128)S(1)} %get-tuple-element.42), channel_id=1, source_target_pairs={{1,0},{2,1},{3,2},{4,3},{5,4},{6,5},{7,6},{8,7},{9,8},{10,9},{11,1... | collective-permute-start | bytes 98312 | tf_op jit(solution)/shard_map/ppermute | solution.py:13
  120.9 28.9 %collective-permute-start.23 = (f32[16,16,512]{2,1,0:T(8,128)S(1)}, f32[16,16,512]{2,1,0:T(8,128)S(1)}, u32[]{:S(2)}, u32[]{:S(2)}) collective-permute-start(f32[16,16,512]{2,1,0:T(8,128)S(1)} %get-tuple-element.2), channel_id=1, source_target_pairs={{0,128},{32,160},{64,192},{96,224},{128,256},{160,288},{192,320},{... | collective-permute-start | bytes 1572872 | tf_op jit(solution)/shard_map/ppermute | solution.py:13
  127.0 7.7 %collective-permute-start.24 = (f32[16,1,512]{2,1,0:T(1,128)S(1)}, f32[16,1,512]{2,1,0:T(1,128)S(1)}, u32[]{:S(2)}, u32[]{:S(2)}) collective-permute-start(f32[16,1,512]{2,1,0:T(1,128)S(1)} %get-tuple-element.23), channel_id=1, source_target_pairs={{0,1},{1,2},{2,3},{3,4},{4,5},{5,6},{6,7},{7,8},{8,9},{9,10},{10,1... | collective-permute-start | bytes 98312 | tf_op jit(solution)/shard_map/ppermute | solution.py:13
  129.0 6.5 %collective-permute-start.25 = (f32[16,1,512]{2,1,0:T(1,128)S(1)}, f32[16,1,512]{2,1,0:T(1,128)S(1)}, u32[]{:S(2)}, u32[]{:S(2)}) collective-permute-start(f32[16,1,512]{2,1,0:T(1,128)S(1)} %get-tuple-element.24), channel_id=1, source_target_pairs={{1,0},{2,1},{3,2},{4,3},{5,4},{6,5},{7,6},{8,7},{9,8},{10,9},{11,1... | collective-permute-start | bytes 98312 | tf_op jit(solution)/shard_map/ppermute | solution.py:13
where the time goes:
time: 153 us; the launch traced here: 152 us
  starting transfers between devices  101 us (66%)
  waiting for transfers between devices  34.7 us (23%)
  other arithmetic  12.2 us (8%)
  local copies, waits for them, and re-layouts  3.3 us (2%)
    ppermute x22, starting transfers between devices, shifted(): return lax.ppermute(block, axis, route)  92.9 us
    ppermute x22, waiting for transfers between devices, shifted(): return lax.ppermute(block, axis, route)  31.4 us
    ppermute x4, starting transfers between devices, from_partner(): return lax.ppermute(value, axis, pairs)  7.68 us
    ppermute x4, waiting for transfers between devices, from_partner(): return lax.ppermute(value, axis, pairs)  3.3 us
    div x3, other arithmetic, smooth(): update = damping * rhs_field / diag_term  3.08 us
  transfers between devices with their start and end apart: 26, of which 9 were waited for; matrix products, arithmetic and copies ran while one was open for 5% of the time, Pallas kernels for 0%

commit v1 on v0

v1 whole, which is shorter than its diff:
```python
import jax
import jax.numpy as jnp
from jax import lax
from jax.sharding import PartitionSpec as P

tau = 0.08
omega = 0.7


def routes(chips, slabs):
    def device(z, core, slab):
        return (2 * z + core) * slabs + slab

    every = [(z, c, s) for z in range(chips) for c in range(2) for s in range(slabs)]
    pair = [(device(z, c, s), device(z, 1 - c, s)) for z, c, s in every]
    outer = []
    for z, c, s in every:
        near = s - 1 if c == 0 else s + 1
        if 0 <= near < slabs:
            outer.append((device(z, c, s), device(z, 1 - c, near)))
    later = [(device(z, c, s), device(z + 1, c, s)) for z, c, s in every if z + 1 < chips]
    later2 = [(device(z, c, s), device(z + 2, c, s)) for z, c, s in every if z + 2 < chips]
    twin = [(device(z, c, s), device(z ^ 1, c, s)) for z, c, s in every]
    return pair, outer, later, later2, twin


def weights_of(c):
    mid = c[:, 1:-1]
    near = [c[:, :-2], c[:, 2:]] + flat_near(mid)
    weights = [0.5 * (mid + other) for other in near]
    total = weights[0]
    for w in weights[1:]:
        total = total + w
    return weights, total


def flat_near(v):
    zero_y = jnp.zeros_like(v[..., :1])
    zero_z = jnp.zeros_like(v[..., :1, :])
    return [
        jnp.concatenate([zero_y, v[..., :-1]], -1),
        jnp.concatenate([v[..., 1:], zero_y], -1),
        jnp.concatenate([zero_z, v[..., :-1, :]], -2),
        jnp.concatenate([v[..., 1:, :], zero_z], -2),
    ]


def operator(v, before, after, prev, weights, total, step):
    low = jnp.concatenate([before, v[:, :-1]], 1)
    high = jnp.concatenate([v[:, 1:], after], 1)
    near = [low, high] + flat_near(v)
    flux = weights[0] * near[0]
    for w, n in zip(weights[1:], near[1:]):
        flux = flux + w * n
    return v - prev + step * (total * v - flux)


def solution(mesh):
    slabs = mesh.shape["space"]
    chips = mesh.shape["tm"] // 2
    pair, outer, later, later2, twin = routes(chips, slabs)
    axes = ("tm", "space")

    def send(x, route):
        return lax.ppermute(x, axes, route)

    def shards(iterate, source_term, conductivity):
        core = lax.axis_index("tm") % 2
        first = core == 0

        def rows(a):
            a = jnp.swapaxes(a, 0, 1)
            return jnp.where(first, a, a[::-1])

        u_own = rows(iterate[0, 0])
        f_own = rows(source_term[0, 0])
        kappa = rows(conductivity[0])
        got = send(jnp.concatenate([u_own[7:][::-1], f_own[8:][::-1]], 0), pair)

        def both(own, other):
            return jnp.where(first, jnp.stack([own, other]), jnp.stack([other, own]))

        u = both(u_own[:9], got[:9])
        f = both(f_own[:8], got[9:])
        u_prev = send(u[1, :8], later)
        edge = send(jnp.concatenate([u[:, 0], kappa[:1]], 0), outer)
        u_all = jnp.concatenate([edge[:2, None], u], 1)
        kappa_all = jnp.concatenate([edge[2:], kappa[:9]], 0)
        c = kappa_all[None] * (1.0 + u_all * u_all)
        w, total = weights_of(c)
        u_mid = u_all[:, 1:-1]
        prev = jnp.stack([u_prev, u_mid[0]])
        b = f - operator(u_mid, u_all[:, :1], u_all[:, -1:], prev, w, total, tau)
        diag = 1.0 + tau * total
        e0 = omega * b / diag

        def exchange(v):
            return send(v[:, 0], outer)[:, None], send(v[:, -1], pair)[:, None]

        z0 = send(e0[1], later)
        o0, i0 = exchange(e0)
        e1 = e0 + omega * (b - operator(e0, o0, i0, jnp.stack([z0, e0[0]]), w, total, tau)) / diag
        z1 = send(e1[1], later)
        o1, i1 = exchange(e1)
        r = b - operator(e1, o1, i1, jnp.stack([z1, e1[0]]), w, total, tau)

        bm = (r[0] + r[1])[None]
        cm = (0.5 * (c[0] + c[1]))[None]
        wm, totalm = weights_of(cm)
        cm_twin = send(cm, twin)
        diagm = 1.0 + 2 * tau * totalm
        m0 = omega * bm / diagm
        zm0 = send(m0, later)
        o, i = exchange(m0)
        m1 = m0 + omega * (bm - operator(m0, o, i, zm0, wm, totalm, 2 * tau)) / diagm
        zm1 = send(m1, later)
        o, i = exchange(m1)
        rm = bm - operator(m1, o, i, zm1, wm, totalm, 2 * tau)

        bt = rm + send(rm, twin)
        ct = 0.5 * (cm + cm_twin)
        wt, totalt = weights_of(ct)
        diagt = 1.0 + 4 * tau * totalt
        t0 = omega * bt / diagt
        zt0 = send(t0, later2)
        o, i = exchange(t0)
        t1 = t0 + omega * (bt - operator(t0, o, i, zt0, wt, totalt, 4 * tau)) / diagt
        update = e1 + (m1 + t1)

        def mine(x):
            return jnp.where(first, x[0], x[1]), jnp.where(first, x[1], x[0])

        own_up, other_up = mine(update)
        own_b, other_b = mine(b)
        got_b = send(other_b, pair)
        got_up = send(other_up, pair)

        def natural(own, got):
            a = jnp.concatenate([own, got[::-1]], 0)
            return jnp.swapaxes(jnp.where(first, a, a[::-1]), 0, 1)

        new = iterate[0, 0] + natural(own_up, got_up)
        return new[None, None], natural(own_b, got_b)[None, None]

    spec = P("tm", "space", None, None, None)
    return jax.shard_map(
        shards,
        mesh=mesh,
        in_specs=(spec, spec, P("space", None, None, None)),
        out_specs=(spec, spec),
        check_vma=False,
    )
```

time: 153 us -> 120 us (0.78)
  the two profiles are of different devices: /device:TPU:71 before, /device:TPU:85 now
where the time goes in v1:
time: 120 us; the launch traced here: 119 us
  starting transfers between devices  72.9 us (61%)
  waiting for transfers between devices  23.8 us (20%)
  other arithmetic  11.1 us (9%)
  local copies, waits for them, and re-layouts  9.53 us (8%)
  between operations  1.53 us (1%)
    ppermute x22, starting transfers between devices, send(): return lax.ppermute(x, axes, route)  72.9 us
    ppermute x22, waiting for transfers between devices, send(): return lax.ppermute(x, axes, route)  23.8 us
    unnamed x16, local copies, waits for them, and re-layouts  2.95 us
  transfers between devices with their start and end apart: 22, of which 10 were waited for; matrix products, arithmetic and copies ran while one was open for 10% of the time, Pallas kernels for 0%

profile of v1, /device:TPU:85, one launch (start us, length us, event | category | flops | bytes accessed | tf_op | source)
XLA Modules:
  0.0 118.8 jit_solution(886646263331004699)
XLA Ops:
  0.7 1.4 %copy.49 = f32[1,16,16,512]{3,1,2,0:T(8,128)S(1)} copy(f32[1,16,16,512]{3,2,1,0:T(8,128)} %param.5) | data formatting | bytes 1048576 | tf_op args[2]
  2.1 0.3 copy.50
  2.6 1.0 copy-done.2
  4.3 2.6 %collective-permute-start = (f32[17,16,512]{2,1,0:T(8,128)S(1)}, f32[17,16,512]{2,1,0:T(8,128)S(1)}, u32[]{:S(2)}, u32[]{:S(2)}) collective-permute-start(f32[17,16,512]{2,1,0:T(8,128)S(1)} %pad_maximum_fusion.1), channel_id=1, source_target_pairs={{0,32},{1,33},{2,34},{3,35},{4,36},{5,37},{6,38},{7,39},{8,40},{9,... | collective-permute-start | bytes 1671176 | tf_op jit(solution)/shard_map/ppermute | solution.py:65
  7.1 1.3 %collective-permute-done = f32[17,16,512]{2,1,0:T(8,128)S(1)} collective-permute-done((f32[17,16,512]{2,1,0:T(8,128)S(1)}, f32[17,16,512]{2,1,0:T(8,128)S(1)}, u32[]{:S(2)}, u32[]{:S(2)}) %collective-permute-start) | collective-permute-done | bytes 557088 | tf_op jit(solution)/shard_map/ppermute | solution.py:65
  8.7 0.5 maximum_select_fusion
  9.6 3.5 %collective-permute-start.2 = (f32[3,16,512]{2,1,0:T(8,128)S(1)}, f32[3,16,512]{2,1,0:T(8,128)S(1)}, u32[]{:S(2)}, u32[]{:S(2)}) collective-permute-start(f32[3,16,512]{2,1,0:T(8,128)S(1)} %pad_maximum_fusion.5), channel_id=1, source_target_pairs={{1,32},{2,33},{3,34},{4,35},{5,36},{6,37},{7,38},{8,39},{9,40},{10... | collective-permute-start | bytes 294920 | tf_op jit(solution)/shard_map/ppermute | solution.py:65
  13.1 4.0 %collective-permute-start.1 = (f32[8,16,512]{2,0,1:T(8,128)S(1)}, f32[8,16,512]{2,0,1:T(8,128)S(1)}, u32[]{:S(2)}, u32[]{:S(2)}) collective-permute-start(f32[8,16,512]{2,0,1:T(8,128)S(1)} %get-tuple-element.16), channel_id=1, source_target_pairs={{0,64},{1,65},{2,66},{3,67},{4,68},{5,69},{6,70},{7,71},{8,72},{9,... | collective-permute-start | bytes 786440 | tf_op jit(solution)/shard_map/ppermute | solution.py:65
  17.5 0.3 fusion.1
  18.4 2.1 %collective-permute-start.16 = (f32[1,10,16,512]{3,1,2,0:T(8,128)S(1)}, f32[1,10,16,512]{3,1,2,0:T(8,128)S(1)}, u32[]{:S(2)}, u32[]{:S(2)}) collective-permute-start(f32[1,10,16,512]{3,1,2,0:T(8,128)S(1)} %fusion.2), channel_id=1, source_target_pairs={{0,64},{1,65},{2,66},{3,67},{4,68},{5,69},{6,70},{7,71},{8,72},{9,... | collective-permute-start | bytes 983048 | tf_op jit(solution)/shard_map/ppermute | solution.py:65
  20.6 2.1 %collective-permute-done.1 = f32[8,16,512]{2,0,1:T(8,128)S(1)} collective-permute-done((f32[8,16,512]{2,0,1:T(8,128)S(1)}, f32[8,16,512]{2,0,1:T(8,128)S(1)}, u32[]{:S(2)}, u32[]{:S(2)}) %collective-permute-start.1) | collective-permute-done | bytes 262176 | tf_op jit(solution)/shard_map/ppermute | solution.py:65
  22.7 1.5 %fusion.36 = (f32[2,8,16,512]{3,1,2,0:T(8,128)S(1)}, f32[2,8,16,512]{3,1,2,0:T(8,128)S(1)}, f32[2,8,16,512]{3,1,2,0:T(8,128)S(1)}, f32[2,8,16,512]{3,1,2,0:T(8,1...) fusion(f32[2,8,15,512]{3,1,2,0:T(8,128)S(1)} %get-tuple-element, ...), kind=kLoop, calls=%fused_computation.64 | loop fusion | flops 5242880 | bytes 12447744 | tf_op jit(solution)/shard_map/div | solution.py:95
  24.9 1.9 %collective-permute-start.4 = (f32[2,16,512]{2,1,0:T(8,128)S(1)}, f32[2,16,512]{2,1,0:T(8,128)S(1)}, u32[]{:S(2)}, u32[]{:S(2)}) collective-permute-start(f32[2,16,512]{2,1,0:T(8,128)S(1)} %bitcast.104), channel_id=1, source_target_pairs={{1,32},{2,33},{3,34},{4,35},{5,36},{6,37},{7,38},{8,39},{9,40},{10... | collective-permute-start | bytes 196616 | tf_op jit(solution)/shard_map/ppermute | solution.py:65
  26.8 2.5 %collective-permute-start.5 = (f32[2,16,512]{2,1,0:T(8,128)S(1)}, f32[2,16,512]{2,1,0:T(8,128)S(1)}, u32[]{:S(2)}, u32[]{:S(2)}) collective-permute-start(f32[2,16,512]{2,1,0:T(8,128)S(1)} %bitcast.105), channel_id=1, source_target_pairs={{0,32},{1,33},{2,34},{3,35},{4,36},{5,37},{6,38},{7,39},{8,40},{9,... | collective-permute-start | bytes 196616 | tf_op jit(solution)/shard_map/ppermute | solution.py:65
  29.3 1.9 %collective-permute-start.21 = (f32[8,16,512]{2,0,1:T(8,128)S(1)}, f32[8,16,512]{2,0,1:T(8,128)}, u32[]{:S(2)}, u32[]{:S(2)}) collective-permute-start(f32[8,16,512]{2,0,1:T(8,128)S(1)} %get-tuple-element.23), channel_id=1, source_target_pairs={{0,32},{1,33},{2,34},{3,35},{4,36},{5,37},{6,38},{7,39},{8,40},{9,... | collective-permute-start | bytes 786440 | tf_op jit(solution)/shard_map/ppermute | solution.py:65
  31.2 5.9 %collective-permute-start.3 = (f32[8,16,512]{2,0,1:T(8,128)S(1)}, f32[8,16,512]{2,0,1:T(8,128)S(1)}, u32[]{:S(2)}, u32[]{:S(2)}) collective-permute-start(f32[8,16,512]{2,0,1:T(8,128)S(1)} %get-tuple-element.52), channel_id=1, source_target_pairs={{0,64},{1,65},{2,66},{3,67},{4,68},{5,69},{6,70},{7,71},{8,72},{9,... | collective-permute-start | bytes 786440 | tf_op jit(solution)/shard_map/ppermute | solution.py:65
  37.4 5.4 %collective-permute-done.3 = f32[8,16,512]{2,0,1:T(8,128)S(1)} collective-permute-done((f32[8,16,512]{2,0,1:T(8,128)S(1)}, f32[8,16,512]{2,0,1:T(8,128)S(1)}, u32[]{:S(2)}, u32[]{:S(2)}) %collective-permute-start.3) | collective-permute-done | bytes 262176 | tf_op jit(solution)/shard_map/ppermute | solution.py:65
  42.8 0.9 fusion.18
  44.2 4.1 %collective-permute-start.6 = (f32[8,16,512]{2,0,1:T(8,128)S(1)}, f32[8,16,512]{2,0,1:T(8,128)S(1)}, u32[]{:S(2)}, u32[]{:S(2)}) collective-permute-start(f32[8,16,512]{2,0,1:T(8,128)S(1)} %get-tuple-element.42), channel_id=1, source_target_pairs={{0,64},{1,65},{2,66},{3,67},{4,68},{5,69},{6,70},{7,71},{8,72},{9,... | collective-permute-start | bytes 786440 | tf_op jit(solution)/shard_map/ppermute | solution.py:65
  48.4 5.7 %collective-permute-start.7 = (f32[2,16,512]{2,1,0:T(8,128)S(1)}, f32[2,16,512]{2,1,0:T(8,128)S(1)}, u32[]{:S(2)}, u32[]{:S(2)}) collective-permute-start(f32[2,16,512]{2,1,0:T(8,128)S(1)} %bitcast.106), channel_id=1, source_target_pairs={{1,32},{2,33},{3,34},{4,35},{5,36},{6,37},{7,38},{8,39},{9,40},{10... | collective-permute-start | bytes 196616 | tf_op jit(solution)/shard_map/ppermute | solution.py:65
  54.2 1.9 %collective-permute-start.8 = (f32[2,16,512]{2,1,0:T(8,128)S(1)}, f32[2,16,512]{2,1,0:T(8,128)S(1)}, u32[]{:S(2)}, u32[]{:S(2)}) collective-permute-start(f32[2,16,512]{2,1,0:T(8,128)S(1)} %bitcast.107), channel_id=1, source_target_pairs={{0,32},{1,33},{2,34},{3,35},{4,36},{5,37},{6,38},{7,39},{8,40},{9,... | collective-permute-start | bytes 196616 | tf_op jit(solution)/shard_map/ppermute | solution.py:65
  56.3 1.0 collective-permute-done.8
  57.4 1.0 fusion.27
  58.4 0.3 fusion.76
  58.9 5.3 %collective-permute-start.9 = (f32[1,8,16,512]{3,1,2,0:T(8,128)S(1)}, f32[1,8,16,512]{3,1,2,0:T(8,128)S(1)}, u32[]{:S(2)}, u32[]{:S(2)}) collective-permute-start(f32[1,8,16,512]{3,1,2,0:T(8,128)S(1)} %fusion.76), channel_id=1, source_target_pairs={{0,64},{1,65},{2,66},{3,67},{4,68},{5,69},{6,70},{7,71},{8,72},{9,... | collective-permute-start | bytes 786440 | tf_op jit(solution)/shard_map/ppermute | solution.py:65
  64.2 2.8 %collective-permute-start.10 = (f32[1,16,512]{2,0,1:T(1,128)S(1)}, f32[1,16,512]{2,0,1:T(1,128)S(1)}, u32[]{:S(2)}, u32[]{:S(2)}) collective-permute-start(f32[1,16,512]{2,0,1:T(1,128)S(1)} %get-tuple-element.81), channel_id=1, source_target_pairs={{1,32},{2,33},{3,34},{4,35},{5,36},{6,37},{7,38},{8,39},{9,40},{10... | collective-permute-start | bytes 98312 | tf_op jit(solution)/shard_map/ppermute | solution.py:65
  67.0 1.9 %collective-permute-start.11 = (f32[1,16,512]{2,0,1:T(1,128)S(1)}, f32[1,16,512]{2,0,1:T(1,128)S(1)}, u32[]{:S(2)}, u32[]{:S(2)}) collective-permute-start(f32[1,16,512]{2,0,1:T(1,128)S(1)} %get-tuple-element.80), channel_id=1, source_target_pairs={{0,32},{1,33},{2,34},{3,35},{4,36},{5,37},{6,38},{7,39},{8,40},{9,... | collective-permute-start | bytes 98312 | tf_op jit(solution)/shard_map/ppermute | solution.py:65
  69.0 0.5 collective-permute-done.10
  69.5 0.6 collective-permute-done.11
  70.1 0.6 fusion.52
  70.9 5.3 %collective-permute-start.12 = (f32[1,8,16,512]{3,1,2,0:T(8,128)S(1)}, f32[1,8,16,512]{3,1,2,0:T(8,128)S(1)}, u32[]{:S(2)}, u32[]{:S(2)}) collective-permute-start(f32[1,8,16,512]{3,1,2,0:T(8,128)S(1)} %fusion.52), channel_id=1, source_target_pairs={{0,64},{1,65},{2,66},{3,67},{4,68},{5,69},{6,70},{7,71},{8,72},{9,... | collective-permute-start | bytes 786440 | tf_op jit(solution)/shard_map/ppermute | solution.py:65
  76.3 3.8 %collective-permute-start.13 = (f32[1,16,512]{2,0,1:T(1,128)S(1)}, f32[1,16,512]{2,0,1:T(1,128)S(1)}, u32[]{:S(2)}, u32[]{:S(2)}) collective-permute-start(f32[1,16,512]{2,0,1:T(1,128)S(1)} %get-tuple-element.73), channel_id=1, source_target_pairs={{1,32},{2,33},{3,34},{4,35},{5,36},{6,37},{7,38},{8,39},{9,40},{10... | collective-permute-start | bytes 98312 | tf_op jit(solution)/shard_map/ppermute | solution.py:65
  80.2 2.1 %collective-permute-start.14 = (f32[1,16,512]{2,0,1:T(1,128)S(1)}, f32[1,16,512]{2,0,1:T(1,128)S(1)}, u32[]{:S(2)}, u32[]{:S(2)}) collective-permute-start(f32[1,16,512]{2,0,1:T(1,128)S(1)} %get-tuple-element.72), channel_id=1, source_target_pairs={{0,32},{1,33},{2,34},{3,35},{4,36},{5,37},{6,38},{7,39},{8,40},{9,... | collective-permute-start | bytes 98312 | tf_op jit(solution)/shard_map/ppermute | solution.py:65
  82.3 0.9 collective-permute-done.14
  83.3 1.3 %fusion.61 = f32[1,8,16,512]{3,1,2,0:T(8,128)} fusion(f32[1,7,16,512]{3,1,2,0:T(8,128)S(1)} %get-tuple-element.71, f32[1,1,16,512]{3,1,2,0:T(1,128)S(1)} %bitcast.109, f32[1,1,16,512]{3,1,2,0:T(1,128)S(1)} %bitcast.111, f32[1,7,16,512]{3,1,2,0:T(8,128)S(1)} %get-tuple-element.70, f32[1,8,15,512]{3,1,2,0:T(8,128)S(1)} %get-tuple-element.69, ...), kind=kLoop, calls=%fused_computation.109 | loop fusion | flops 2424832 | bytes 4651008 | tf_op jit(solution)/shard_map/sub | solution.py:118
  84.5 1.9 %collective-permute-start.15 = (f32[1,8,16,512]{3,1,2,0:T(8,128)}, f32[1,8,16,512]{3,1,2,0:T(8,128)}, u32[]{:S(2)}, u32[]{:S(2)}) collective-permute-start(f32[1,8,16,512]{3,1,2,0:T(8,128)} %fusion.61), channel_id=1, source_target_pairs={{0,64},{1,65},{2,66},{3,67},{4,68},{5,69},{6,70},{7,71},{8,72},{9,... | collective-permute-start | bytes 786440 | tf_op jit(solution)/shard_map/ppermute | solution.py:65
  86.7 1.7 %rev.34 = f32[8,16,512]{2,0,1:T(8,128)S(1)} reverse(f32[8,16,512]{2,0,1:T(8,128)} %collective-permute-done.21), dimensions={0} | reverse | bytes 524288 | tf_op jit(solution)/shard_map/rev | solution.py:139
  88.4 6.1 %collective-permute-done.15 = f32[1,8,16,512]{3,1,2,0:T(8,128)} collective-permute-done((f32[1,8,16,512]{3,1,2,0:T(8,128)}, f32[1,8,16,512]{3,1,2,0:T(8,128)}, u32[]{:S(2)}, u32[]{:S(2)}) %collective-permute-start.15) | collective-permute-done | bytes 262176 | tf_op jit(solution)/shard_map/ppermute | solution.py:65
  94.5 1.3 %fusion.75 = (f32[1,8,16,512]{3,1,2,0:T(8,128)S(1)}, f32[1,8,16,512]{3,1,2,0:T(8,128)S(1)}) fusion(f32[1,8,15,512]{3,1,2,0:T(8,128)S(1)} %get-tuple-element.29, f32[1,10,16,512]{3,1,2,0:T(8,128)S(1)} %add_multiply_fusion, f32[1,8,15,512]{3,1,2,0:T(8,128)S(1)} %get-tuple-element.28, f32[1,8,16,511]{3,1,2,0:T(8,128)S(1)} %get-tuple-element.27, ...), kind=kLoop, calls=%fused_computation.132 | loop fusion | flops 1441792 | bytes 2849792 | tf_op jit(solution)/shard_map/div | solution.py:124
  96.0 5.5 %collective-permute-start.17 = (f32[1,8,16,512]{3,1,2,0:T(8,128)S(1)}, f32[1,8,16,512]{3,1,2,0:T(8,128)S(1)}, u32[]{:S(2)}, u32[]{:S(2)}) collective-permute-start(f32[1,8,16,512]{3,1,2,0:T(8,128)S(1)} %get-tuple-element.2), channel_id=1, source_target_pairs={{0,128},{1,129},{2,130},{3,131},{4,132},{5,133},{6,134},{7,135},{8... | collective-permute-start | bytes 786440 | tf_op jit(solution)/shard_map/ppermute | solution.py:65
  101.6 3.8 %collective-permute-start.18 = (f32[1,16,512]{2,0,1:T(1,128)S(1)}, f32[1,16,512]{2,0,1:T(1,128)S(1)}, u32[]{:S(2)}, u32[]{:S(2)}) collective-permute-start(f32[1,16,512]{2,0,1:T(1,128)S(1)} %get-tuple-element.58), channel_id=1, source_target_pairs={{1,32},{2,33},{3,34},{4,35},{5,36},{6,37},{7,38},{8,39},{9,40},{10... | collective-permute-start | bytes 98312 | tf_op jit(solution)/shard_map/ppermute | solution.py:65
  105.4 1.9 %collective-permute-start.19 = (f32[1,16,512]{2,0,1:T(1,128)S(1)}, f32[1,16,512]{2,0,1:T(1,128)S(1)}, u32[]{:S(2)}, u32[]{:S(2)}) collective-permute-start(f32[1,16,512]{2,0,1:T(1,128)S(1)} %get-tuple-element.59), channel_id=1, source_target_pairs={{0,32},{1,33},{2,34},{3,35},{4,36},{5,37},{6,38},{7,39},{8,40},{9,... | collective-permute-start | bytes 98312 | tf_op jit(solution)/shard_map/ppermute | solution.py:65
  107.4 1.1 collective-permute-done.19
  108.5 4.6 %collective-permute-done.17 = f32[1,8,16,512]{3,1,2,0:T(8,128)S(1)} collective-permute-done((f32[1,8,16,512]{3,1,2,0:T(8,128)S(1)}, f32[1,8,16,512]{3,1,2,0:T(8,128)S(1)}, u32[]{:S(2)}, u32[]{:S(2)}) %collective-permute-start.17) | collective-permute-done | bytes 262176 | tf_op jit(solution)/shard_map/ppermute | solution.py:65
  113.1 0.7 fusion.77
  113.9 2.5 %collective-permute-start.20 = (f32[8,16,512]{2,0,1:T(8,128)S(1)}, f32[8,16,512]{2,0,1:T(8,128)S(1)}, u32[]{:S(2)}, u32[]{:S(2)}) collective-permute-start(f32[8,16,512]{2,0,1:T(8,128)S(1)} %get-tuple-element.25), channel_id=1, source_target_pairs={{0,32},{1,33},{2,34},{3,35},{4,36},{5,37},{6,38},{7,39},{8,40},{9,... | collective-permute-start | bytes 786440 | tf_op jit(solution)/shard_map/ppermute | solution.py:65
  116.6 0.9 select_bitcast_fusion
  117.8 0.9 fusion.35
  (95 shorter events, 6.0 us)
Async XLA Ops:
  0.6 1.4 %copy-start.3 = (f32[1,1,16,16,512]{4,3,2,1,0:T(8,128)S(1)}, f32[1,1,16,16,512]{4,3,2,1,0:T(8,128)}, u32[]{:S(2)}) copy-start(f32[1,1,16,16,512]{4,3,2,1,0:T(8,128)} %param.4) | copy-start | bytes 1572868
  2.6 1.0 copy-start.2
  4.3 4.2 %collective-permute-start = (f32[17,16,512]{2,1,0:T(8,128)S(1)}, f32[17,16,512]{2,1,0:T(8,128)S(1)}, u32[]{:S(2)}, u32[]{:S(2)}) collective-permute-start(f32[17,16,512]{2,1,0:T(8,128)S(1)} %pad_maximum_fusion.1), channel_id=1, source_target_pairs={{0,32},{1,33},{2,34},{3,35},{4,36},{5,37},{6,38},{7,39},{8,40},{9,... | collective-permute-start | bytes 1671176 | tf_op jit(solution)/shard_map/ppermute | solution.py:65
  9.2 8.4 %copy-start = (f32[2,9,16,512]{3,1,2,0:T(8,128)}, f32[2,9,16,512]{3,1,2,0:T(8,128)S(1)}, u32[]{:S(2)}) copy-start(f32[2,9,16,512]{3,1,2,0:T(8,128)S(1)} %maximum_select_fusion) | copy-start | bytes 1769476
  9.6 7.6 %collective-permute-start.2 = (f32[3,16,512]{2,1,0:T(8,128)S(1)}, f32[3,16,512]{2,1,0:T(8,128)S(1)}, u32[]{:S(2)}, u32[]{:S(2)}) collective-permute-start(f32[3,16,512]{2,1,0:T(8,128)S(1)} %pad_maximum_fusion.5), channel_id=1, source_target_pairs={{1,32},{2,33},{3,34},{4,35},{5,36},{6,37},{7,38},{8,39},{9,40},{10... | collective-permute-start | bytes 294920 | tf_op jit(solution)/shard_map/ppermute | solution.py:65
  13.1 9.6 %collective-permute-start.1 = (f32[8,16,512]{2,0,1:T(8,128)S(1)}, f32[8,16,512]{2,0,1:T(8,128)S(1)}, u32[]{:S(2)}, u32[]{:S(2)}) collective-permute-start(f32[8,16,512]{2,0,1:T(8,128)S(1)} %get-tuple-element.16), channel_id=1, source_target_pairs={{0,64},{1,65},{2,66},{3,67},{4,68},{5,69},{6,70},{7,71},{8,72},{9,... | collective-permute-start | bytes 786440 | tf_op jit(solution)/shard_map/ppermute | solution.py:65
  18.4 4.3 %copy-start.1 = (f32[2,9,16,512]{3,1,2,0:T(8,128)S(1)}, f32[2,9,16,512]{3,1,2,0:T(8,128)}, u32[]{:S(2)}) copy-start(f32[2,9,16,512]{3,1,2,0:T(8,128)} %copy-done) | copy-start | bytes 1769476
  18.4 4.3 %slice-start = ((f32[2,9,16,512]{3,1,2,0:T(8,128)}), f32[2,7,16,512]{3,1,2,0:T(8,128)S(1)}, s32[]{:S(2)}) async-start(f32[2,9,16,512]{3,1,2,0:T(8,128)} %copy-done), calls=%async_computation | async-start | bytes 1048576 | tf_op jit(solution)/shard_map/slice | solution.py:49
  18.4 18.9 %collective-permute-start.16 = (f32[1,10,16,512]{3,1,2,0:T(8,128)S(1)}, f32[1,10,16,512]{3,1,2,0:T(8,128)S(1)}, u32[]{:S(2)}, u32[]{:S(2)}) collective-permute-start(f32[1,10,16,512]{3,1,2,0:T(8,128)S(1)} %fusion.2), channel_id=1, source_target_pairs={{0,64},{1,65},{2,66},{3,67},{4,68},{5,69},{6,70},{7,71},{8,72},{9,... | collective-permute-start | bytes 983048 | tf_op jit(solution)/shard_map/ppermute | solution.py:65
  24.9 12.3 %collective-permute-start.4 = (f32[2,16,512]{2,1,0:T(8,128)S(1)}, f32[2,16,512]{2,1,0:T(8,128)S(1)}, u32[]{:S(2)}, u32[]{:S(2)}) collective-permute-start(f32[2,16,512]{2,1,0:T(8,128)S(1)} %bitcast.104), channel_id=1, source_target_pairs={{1,32},{2,33},{3,34},{4,35},{5,36},{6,37},{7,38},{8,39},{9,40},{10... | collective-permute-start | bytes 196616 | tf_op jit(solution)/shard_map/ppermute | solution.py:65
  26.8 10.4 %collective-permute-start.5 = (f32[2,16,512]{2,1,0:T(8,128)S(1)}, f32[2,16,512]{2,1,0:T(8,128)S(1)}, u32[]{:S(2)}, u32[]{:S(2)}) collective-permute-start(f32[2,16,512]{2,1,0:T(8,128)S(1)} %bitcast.105), channel_id=1, source_target_pairs={{0,32},{1,33},{2,34},{3,35},{4,36},{5,37},{6,38},{7,39},{8,40},{9,... | collective-permute-start | bytes 196616 | tf_op jit(solution)/shard_map/ppermute | solution.py:65
  29.3 57.3 %collective-permute-start.21 = (f32[8,16,512]{2,0,1:T(8,128)S(1)}, f32[8,16,512]{2,0,1:T(8,128)}, u32[]{:S(2)}, u32[]{:S(2)}) collective-permute-start(f32[8,16,512]{2,0,1:T(8,128)S(1)} %get-tuple-element.23), channel_id=1, source_target_pairs={{0,32},{1,33},{2,34},{3,35},{4,36},{5,37},{6,38},{7,39},{8,40},{9,... | collective-permute-start | bytes 786440 | tf_op jit(solution)/shard_map/ppermute | solution.py:65
  31.2 11.6 %collective-permute-start.3 = (f32[8,16,512]{2,0,1:T(8,128)S(1)}, f32[8,16,512]{2,0,1:T(8,128)S(1)}, u32[]{:S(2)}, u32[]{:S(2)}) collective-permute-start(f32[8,16,512]{2,0,1:T(8,128)S(1)} %get-tuple-element.52), channel_id=1, source_target_pairs={{0,64},{1,65},{2,66},{3,67},{4,68},{5,69},{6,70},{7,71},{8,72},{9,... | collective-permute-start | bytes 786440 | tf_op jit(solution)/shard_map/ppermute | solution.py:65
  44.2 13.2 %collective-permute-start.6 = (f32[8,16,512]{2,0,1:T(8,128)S(1)}, f32[8,16,512]{2,0,1:T(8,128)S(1)}, u32[]{:S(2)}, u32[]{:S(2)}) collective-permute-start(f32[8,16,512]{2,0,1:T(8,128)S(1)} %get-tuple-element.42), channel_id=1, source_target_pairs={{0,64},{1,65},{2,66},{3,67},{4,68},{5,69},{6,70},{7,71},{8,72},{9,... | collective-permute-start | bytes 786440 | tf_op jit(solution)/shard_map/ppermute | solution.py:65
  48.4 7.8 %collective-permute-start.7 = (f32[2,16,512]{2,1,0:T(8,128)S(1)}, f32[2,16,512]{2,1,0:T(8,128)S(1)}, u32[]{:S(2)}, u32[]{:S(2)}) collective-permute-start(f32[2,16,512]{2,1,0:T(8,128)S(1)} %bitcast.106), channel_id=1, source_target_pairs={{1,32},{2,33},{3,34},{4,35},{5,36},{6,37},{7,38},{8,39},{9,40},{10... | collective-permute-start | bytes 196616 | tf_op jit(solution)/shard_map/ppermute | solution.py:65
  54.2 3.1 %collective-permute-start.8 = (f32[2,16,512]{2,1,0:T(8,128)S(1)}, f32[2,16,512]{2,1,0:T(8,128)S(1)}, u32[]{:S(2)}, u32[]{:S(2)}) collective-permute-start(f32[2,16,512]{2,1,0:T(8,128)S(1)} %bitcast.107), channel_id=1, source_target_pairs={{0,32},{1,33},{2,34},{3,35},{4,36},{5,37},{6,38},{7,39},{8,40},{9,... | collective-permute-start | bytes 196616 | tf_op jit(solution)/shard_map/ppermute | solution.py:65
  58.9 11.2 %collective-permute-start.9 = (f32[1,8,16,512]{3,1,2,0:T(8,128)S(1)}, f32[1,8,16,512]{3,1,2,0:T(8,128)S(1)}, u32[]{:S(2)}, u32[]{:S(2)}) collective-permute-start(f32[1,8,16,512]{3,1,2,0:T(8,128)S(1)} %fusion.76), channel_id=1, source_target_pairs={{0,64},{1,65},{2,66},{3,67},{4,68},{5,69},{6,70},{7,71},{8,72},{9,... | collective-permute-start | bytes 786440 | tf_op jit(solution)/shard_map/ppermute | solution.py:65
  64.2 5.3 %collective-permute-start.10 = (f32[1,16,512]{2,0,1:T(1,128)S(1)}, f32[1,16,512]{2,0,1:T(1,128)S(1)}, u32[]{:S(2)}, u32[]{:S(2)}) collective-permute-start(f32[1,16,512]{2,0,1:T(1,128)S(1)} %get-tuple-element.81), channel_id=1, source_target_pairs={{1,32},{2,33},{3,34},{4,35},{5,36},{6,37},{7,38},{8,39},{9,40},{10... | collective-permute-start | bytes 98312 | tf_op jit(solution)/shard_map/ppermute | solution.py:65
  67.0 3.1 %collective-permute-start.11 = (f32[1,16,512]{2,0,1:T(1,128)S(1)}, f32[1,16,512]{2,0,1:T(1,128)S(1)}, u32[]{:S(2)}, u32[]{:S(2)}) collective-permute-start(f32[1,16,512]{2,0,1:T(1,128)S(1)} %get-tuple-element.80), channel_id=1, source_target_pairs={{0,32},{1,33},{2,34},{3,35},{4,36},{5,37},{6,38},{7,39},{8,40},{9,... | collective-permute-start | bytes 98312 | tf_op jit(solution)/shard_map/ppermute | solution.py:65
  70.9 12.3 %collective-permute-start.12 = (f32[1,8,16,512]{3,1,2,0:T(8,128)S(1)}, f32[1,8,16,512]{3,1,2,0:T(8,128)S(1)}, u32[]{:S(2)}, u32[]{:S(2)}) collective-permute-start(f32[1,8,16,512]{3,1,2,0:T(8,128)S(1)} %fusion.52), channel_id=1, source_target_pairs={{0,64},{1,65},{2,66},{3,67},{4,68},{5,69},{6,70},{7,71},{8,72},{9,... | collective-permute-start | bytes 786440 | tf_op jit(solution)/shard_map/ppermute | solution.py:65
  76.3 6.0 %collective-permute-start.13 = (f32[1,16,512]{2,0,1:T(1,128)S(1)}, f32[1,16,512]{2,0,1:T(1,128)S(1)}, u32[]{:S(2)}, u32[]{:S(2)}) collective-permute-start(f32[1,16,512]{2,0,1:T(1,128)S(1)} %get-tuple-element.73), channel_id=1, source_target_pairs={{1,32},{2,33},{3,34},{4,35},{5,36},{6,37},{7,38},{8,39},{9,40},{10... | collective-permute-start | bytes 98312 | tf_op jit(solution)/shard_map/ppermute | solution.py:65
  80.2 3.1 %collective-permute-start.14 = (f32[1,16,512]{2,0,1:T(1,128)S(1)}, f32[1,16,512]{2,0,1:T(1,128)S(1)}, u32[]{:S(2)}, u32[]{:S(2)}) collective-permute-start(f32[1,16,512]{2,0,1:T(1,128)S(1)} %get-tuple-element.72), channel_id=1, source_target_pairs={{0,32},{1,33},{2,34},{3,35},{4,36},{5,37},{6,38},{7,39},{8,40},{9,... | collective-permute-start | bytes 98312 | tf_op jit(solution)/shard_map/ppermute | solution.py:65
  84.5 10.0 %collective-permute-start.15 = (f32[1,8,16,512]{3,1,2,0:T(8,128)}, f32[1,8,16,512]{3,1,2,0:T(8,128)}, u32[]{:S(2)}, u32[]{:S(2)}) collective-permute-start(f32[1,8,16,512]{3,1,2,0:T(8,128)} %fusion.61), channel_id=1, source_target_pairs={{0,64},{1,65},{2,66},{3,67},{4,68},{5,69},{6,70},{7,71},{8,72},{9,... | collective-permute-start | bytes 786440 | tf_op jit(solution)/shard_map/ppermute | solution.py:65
  96.0 17.1 %collective-permute-start.17 = (f32[1,8,16,512]{3,1,2,0:T(8,128)S(1)}, f32[1,8,16,512]{3,1,2,0:T(8,128)S(1)}, u32[]{:S(2)}, u32[]{:S(2)}) collective-permute-start(f32[1,8,16,512]{3,1,2,0:T(8,128)S(1)} %get-tuple-element.2), channel_id=1, source_target_pairs={{0,128},{1,129},{2,130},{3,131},{4,132},{5,133},{6,134},{7,135},{8... | collective-permute-start | bytes 786440 | tf_op jit(solution)/shard_map/ppermute | solution.py:65
  101.6 5.8 %collective-permute-start.18 = (f32[1,16,512]{2,0,1:T(1,128)S(1)}, f32[1,16,512]{2,0,1:T(1,128)S(1)}, u32[]{:S(2)}, u32[]{:S(2)}) collective-permute-start(f32[1,16,512]{2,0,1:T(1,128)S(1)} %get-tuple-element.58), channel_id=1, source_target_pairs={{1,32},{2,33},{3,34},{4,35},{5,36},{6,37},{7,38},{8,39},{9,40},{10... | collective-permute-start | bytes 98312 | tf_op jit(solution)/shard_map/ppermute | solution.py:65
  105.4 3.1 %collective-permute-start.19 = (f32[1,16,512]{2,0,1:T(1,128)S(1)}, f32[1,16,512]{2,0,1:T(1,128)S(1)}, u32[]{:S(2)}, u32[]{:S(2)}) collective-permute-start(f32[1,16,512]{2,0,1:T(1,128)S(1)} %get-tuple-element.59), channel_id=1, source_target_pairs={{0,32},{1,33},{2,34},{3,35},{4,36},{5,37},{6,38},{7,39},{8,40},{9,... | collective-permute-start | bytes 98312 | tf_op jit(solution)/shard_map/ppermute | solution.py:65
  113.9 3.6 %collective-permute-start.20 = (f32[8,16,512]{2,0,1:T(8,128)S(1)}, f32[8,16,512]{2,0,1:T(8,128)S(1)}, u32[]{:S(2)}, u32[]{:S(2)}) collective-permute-start(f32[8,16,512]{2,0,1:T(8,128)S(1)} %get-tuple-element.25), channel_id=1, source_target_pairs={{0,32},{1,33},{2,34},{3,35},{4,36},{5,37},{6,38},{7,39},{8,40},{9,... | collective-permute-start | bytes 786440 | tf_op jit(solution)/shard_map/ppermute | solution.py:65

commit v2 on v1

v2 whole, which is shorter than its diff:
```python
import functools
import jax
import jax.numpy as jnp
from jax import lax
from jax.experimental import pallas as pl
from jax.experimental.pallas import tpu as pltpu
from jax.sharding import PartitionSpec as P

tau = 0.08
omega = 0.7
keep = 1.0 - omega


def routes(chips, slabs):
    def device(z, core, slab):
        return (2 * z + core) * slabs + slab

    every = [(z, c, s) for z in range(chips) for c in range(2) for s in range(slabs)]
    pair = [(device(z, c, s), device(z, 1 - c, s)) for z, c, s in every]
    outer = []
    for z, c, s in every:
        near = s - 1 if c == 0 else s + 1
        if 0 <= near < slabs:
            outer.append((device(z, c, s), device(z, 1 - c, near)))
    later = [(device(z, c, s), device(z + 1, c, s)) for z, c, s in every if z + 1 < chips]
    later2 = [(device(z, c, s), device(z + 2, c, s)) for z, c, s in every if z + 2 < chips]
    twin = [(device(z, c, s), device(z ^ 1, c, s)) for z, c, s in every]
    in_chip = [[device(z, 0, s), device(z, 1, s)] for z in range(chips) for s in range(slabs)]
    twins = [
        [device(2 * k, c, s), device(2 * k + 1, c, s)]
        for k in range(chips // 2)
        for c in range(2)
        for s in range(slabs)
    ]
    return pair, outer, later, later2, twin, in_chip, twins


def iota(v, axis):
    return lax.broadcasted_iota(jnp.int32, v.shape, axis)


def around(v):
    ny = v.shape[1]
    nz = v.shape[0]
    return (
        pltpu.roll(v, 1, 1),
        pltpu.roll(v, ny - 1, 1),
        pltpu.roll(v, 1, 0),
        pltpu.roll(v, nz - 1, 0),
    )


def faces(c, low, high, step):
    ny = c.shape[1]
    nz = c.shape[0]
    y = iota(c, 1)
    z = iota(c, 0)
    inside = (y > 0, y < ny - 1, z > 0, z < nz - 1)
    near = [jnp.where(ok, n, 0.0) for ok, n in zip(inside, around(c))]
    total = low + high
    for n in near:
        total = total + n
    diag = 1.0 + step * (3.0 * c + 0.5 * total)
    weights = [jnp.where(ok, (0.5 * step) * (c + n), 0.0) for ok, n in zip(inside, near)]
    return weights, (0.5 * step) * (c + high), diag


def spread(v, low, high, weights, w_low, w_high):
    flux = w_low * low + w_high * high
    for w, n in zip(weights, around(v)):
        flux = flux + w * n
    return flux


def k_split(info, u, f, kap, uo, fo, ko, send):
    def rows(mirror):
        for x in range(16):
            row = 15 - x if mirror else x
            if row <= 8:
                value = u[:, x, :]
                uo[row] = value
                ko[row] = kap[:, x, :]
                if row <= 7:
                    fo[row] = f[:, x, :]
            back = 15 - row
            if back <= 8:
                send[back] = u[:, x, :]
                if back <= 7:
                    send[9 + back] = f[:, x, :]

    pl.when(info[0] == 0)(lambda: rows(False))
    pl.when(info[0] == 1)(lambda: rows(True))


def k_pack(info, uo, fo, ko, got, u, f, edge, zu, cm):
    h = info[0]
    for x in range(9):
        u[h, x] = uo[x]
        u[1 - h, x] = got[x]
        cm[x] = (0.5 * ko[x]) * (2.0 + uo[x] * uo[x] + got[x] * got[x])
    for x in range(8):
        f[h, x] = fo[x]
        f[1 - h, x] = got[9 + x]
        zu[x] = u[1, x]
    for x in range(3):
        edge[x] = u[0, x]
        edge[3 + x] = u[1, x]
        edge[6 + x] = ko[x]
    for x in range(2):
        edge[9 + x] = f[0, x]
        edge[11 + x] = f[1, x]


def k_residual(info, u, f, ko, edge, zu, w, wx, diag, gain, b, e0, cm, zpay, ipay, c):
    h = info[0]
    real = info[1] == 1

    def uu(t, x):
        return u[t, x] if x >= 0 else edge[3 * t - x - 1]

    for x in range(-3, 9):
        k = ko[x] if x >= 0 else edge[5 - x]
        for t in range(2):
            v = uu(t, x)
            c[t, x + 3] = k * (1.0 + v * v)
        cm[x + 3] = 0.5 * (c[0, x + 3] + c[1, x + 3])
    for t in range(2):
        wx[t, 0] = (0.5 * tau) * (c[t, 0] + c[t, 1])
        for x in range(-2, 8):
            i = x + 2
            weights, w_high, d = faces(c[t, i + 1], c[t, i], c[t, i + 2], tau)
            wx[t, i + 1] = w_high
            for k in range(4):
                w[k, t, i] = weights[k]
            g = omega / d
            diag[t, i] = d
            gain[t, i] = g
            v = uu(t, x)
            f_row = f[t, x] if x >= 0 else edge[8 + 2 * t - x]
            value = f_row - d * v + spread(v, uu(t, x - 1), uu(t, x + 1), weights, wx[t, i], w_high)
            if t == 1:
                value = value + uu(0, x)
            elif x >= 0:
                value = value + zu[x]
            if x < 0:
                value = jnp.where(real, value, 0.0)
            b[t, i] = value
            e0[t, i] = g * value
    for i in range(9):
        zpay[i] = e0[1, i + 1]
    zpay[9] = edge[3]
    zpay[10] = edge[4]
    ipay[0] = e0[0, 9]
    ipay[1] = e0[1, 9]
    for x in range(8):
        ipay[2 + x] = b[1 - h, x + 2]


def k_fine(info, w, wx, gain, b, e0, z, near, e1, zpay, ipay, v):
    h = info[0]
    real = info[1] == 1
    for t in range(2):
        for i in range(10):
            value = e0[t, i]
            if t == 0 and i < 2:
                value = value + jnp.where(real, gain[t, i] * z[10 - i], 0.0)
            v[t, i] = value
        v[t, 10] = near[1 - h, t]
    for t in range(2):
        for i in range(1, 10):
            here = v[t, i]
            weights = [w[k, t, i] for k in range(4)]
            flux = spread(here, v[t, i - 1], v[t, i + 1], weights, wx[t, i], wx[t, i + 1])
            prev = z[i - 1] if t == 0 else v[0, i]
            right = b[t, i] + prev
            if t == 0 and i == 1:
                right = right + z[9]
            value = keep * here + gain[t, i] * (right + flux)
            if i == 1:
                value = jnp.where(real, value, 0.0)
            e1[t, i - 1] = value
    for x in range(8):
        zpay[x] = e1[1, x + 1]
    ipay[0] = e1[0, 8]
    ipay[1] = e1[1, 8]


def k_mid_faces(cm, cm_twin, w, wx, diag, gain, ct):
    wx[0] = tau * (cm[0] + cm[1])
    for i in range(10):
        weights, w_high, d = faces(cm[i + 1], cm[i], cm[i + 2], 2 * tau)
        wx[i + 1] = w_high
        for k in range(4):
            w[k, i] = weights[k]
        diag[i] = d
        gain[i] = omega / d
    for x in range(9):
        ct[x] = 0.5 * (cm[x + 3] + cm_twin[x])


def k_restrict(info, w, wx, diag, b, e1, z, near, gain_mid, ct, bm, m0, edge, ipay):
    h = info[0]
    for x in range(8):
        i = x + 2
        parts = []
        for t in range(2):
            here = e1[t, x + 1]
            high = e1[t, x + 2] if x < 7 else near[1 - h, t]
            weights = [w[k, t, i] for k in range(4)]
            flux = spread(here, e1[t, x], high, weights, wx[t, i], wx[t, i + 1])
            prev = z[x] if t == 0 else e1[0, x + 1]
            parts.append(b[t, i] - diag[t, i] * here + prev + flux)
        value = parts[0] + parts[1]
        bm[x] = value
        m0[x] = gain_mid[i] * value
    edge[0] = bm[0]
    edge[1] = bm[1]
    edge[2] = ct[0]
    ipay[0] = m0[7]


def k_mid(info, w, wx, gain, bm, m0, edge, z, near, m1, zpay, ipay):
    h = info[0]
    real = info[1] == 1

    def v(x):
        if x < 0:
            return gain[x + 2] * edge[-x - 1]
        return m0[x] if x < 8 else near[1 - h, 0]

    for x in range(-1, 8):
        i = x + 2
        here = v(x)
        weights = [w[k, i] for k in range(4)]
        flux = spread(here, v(x - 1), v(x + 1), weights, wx[i], wx[i + 1])
        right = edge[0] if x < 0 else bm[x] + z[x]
        value = keep * here + gain[i] * (right + flux)
        if x < 0:
            value = jnp.where(real, value, 0.0)
        else:
            zpay[x] = value
        m1[x + 1] = value
    zpay[8] = v(-1)
    ipay[0] = m1[8]


def k_mid_left(info, w, wx, diag, gain, bm, m1, z, near, rm):
    h = info[0]
    real = info[1] == 1

    def v(x):
        if x < 0:
            return m1[0] + jnp.where(real, gain[1] * z[8], 0.0)
        return m1[x + 1] if x < 8 else near[1 - h, 0]

    for x in range(8):
        i = x + 2
        here = v(x)
        weights = [w[k, i] for k in range(4)]
        flux = spread(here, v(x - 1), v(x + 1), weights, wx[i], wx[i + 1])
        rm[x] = bm[x] - diag[i] * here + z[x] + flux


def k_top_faces(ct, edge, w, wx, gain):
    wx[0] = (2 * tau) * (edge[2] + ct[0])
    for x in range(8):
        low = ct[x - 1] if x else edge[2]
        weights, w_high, d = faces(ct[x], low, ct[x + 1], 4 * tau)
        wx[x + 1] = w_high
        for k in range(4):
            w[k, x] = weights[k]
        gain[x] = omega / d


def k_top_start(gain, rm, bt, t0, edge, ipay):
    for x in range(8):
        value = rm[0, x] + rm[1, x]
        bt[x] = value
        t0[x] = gain[x] * value
    edge[0] = t0[0]
    ipay[0] = t0[7]


def k_top(info, w, wx, gain, bt, t0, edge, z, near, m1, e1, mine, other):
    h = info[0]
    for x in range(8):
        here = t0[x]
        low = t0[x - 1] if x else edge[0]
        high = t0[x + 1] if x < 7 else near[1 - h, 0]
        weights = [w[k, x] for k in range(4)]
        flux = spread(here, low, high, weights, wx[x], wx[x + 1])
        value = keep * here + gain[x] * (bt[x] + z[x] + flux)
        value = value + m1[x + 1]
        mine[x] = e1[h, x + 1] + value
        other[x] = e1[1 - h, x + 1] + value


def k_residual_out(info, b, near, out):
    h = info[0]

    def rows(mirror):
        for x in range(16):
            row = 15 - x if mirror else x
            out[:, x, :] = b[h, row + 2] if row < 8 else near[1 - h, 2 + 15 - row]

    pl.when(h == 0)(lambda: rows(False))
    pl.when(h == 1)(lambda: rows(True))


def k_state_out(info, u, mine, got, out):
    h = info[0]

    def rows(mirror):
        for x in range(16):
            row = 15 - x if mirror else x
            out[:, x, :] = u[:, x, :] + (mine[row] if row < 8 else got[15 - row])

    pl.when(h == 0)(lambda: rows(False))
    pl.when(h == 1)(lambda: rows(True))


VMEM = pl.BlockSpec(memory_space=pltpu.VMEM)
SMEM = pl.BlockSpec(memory_space=pltpu.SMEM)


def solution(mesh):
    slabs = mesh.shape["space"]
    chips = mesh.shape["tm"] // 2
    pair, outer, later, later2, twin, in_chip, twins = routes(chips, slabs)
    axes = ("tm", "space")

    def send(x, route):
        return lax.ppermute(x, axes, route)

    def gather(x, groups):
        return lax.all_gather(x, axes, axis_index_groups=groups)

    def call(kernel, shapes, *args, info=None, scratch=(), work=20):
        lead = () if info is None else (info,)
        size = sum(a.size for a in args) * 4
        return pl.pallas_call(
            kernel,
            out_shape=[jax.ShapeDtypeStruct(s + (16, 512), jnp.float32) for s in shapes],
            in_specs=[SMEM] * len(lead) + [VMEM] * len(args),
            out_specs=[VMEM] * len(shapes),
            scratch_shapes=[pltpu.VMEM(s + (16, 512), jnp.float32) for s in scratch],
            cost_estimate=pl.CostEstimate(flops=work * 131072, bytes_accessed=size, transcendentals=0),
            compiler_params=pltpu.CompilerParams(vmem_limit_bytes=24 * 2**20),
            name=kernel.__name__,
        )(*lead, *args)

    def shards(iterate, source_term, conductivity):
        core = lax.axis_index("tm") % 2
        slab = lax.axis_index("space")
        edge_slab = jnp.where(core == 0, 0, slabs - 1)
        info = jnp.stack([core, (slab != edge_slab).astype(jnp.int32)]).astype(jnp.int32)
        u_in = iterate[0, 0]

        uo, fo, ko, pay = call(
            k_split, [(9,), (8,), (9,), (17,)], u_in, source_term[0, 0], conductivity[0], info=info
        )
        got = send(pay, pair)
        u, f, edge, zu, cm_part = call(
            k_pack, [(2, 9), (2, 8), (13,), (8,), (9,)], uo, fo, ko, got, info=info
        )
        edge = send(edge, outer)
        zu = send(zu, later)
        cm_twin = send(cm_part, twin)
        w, wx, diag, gain, b, e0, cm, zpay, ipay = call(
            k_residual,
            [(4, 2, 10), (2, 11), (2, 10), (2, 10), (2, 10), (2, 10), (12,), (11,), (10,)],
            u, f, ko, edge, zu,
            info=info,
            scratch=[(2, 12)],
        )
        z = send(zpay, later)
        near_b = gather(ipay, in_chip)
        e1, zpay, ipay = call(
            k_fine, [(2, 9), (8,), (2,)], w, wx, gain, b, e0, z, near_b, info=info, scratch=[(2, 11)]
        )
        z = send(zpay, later)
        near = gather(ipay, in_chip)
        (residual,) = call(k_residual_out, [(16,)], b, near_b, info=info)
        wm, wxm, diagm, gainm, ct = call(
            k_mid_faces, [(4, 10), (11,), (10,), (10,), (9,)], cm, cm_twin
        )
        bm, m0, pay, ipay = call(
            k_restrict, [(8,), (8,), (3,), (1,)], w, wx, diag, b, e1, z, near, gainm, ct, info=info
        )
        z = send(m0, later)
        edge = send(pay, outer)
        near = gather(ipay, in_chip)
        m1, zpay, ipay = call(
            k_mid, [(9,), (9,), (1,)], wm, wxm, gainm, bm, m0, edge, z, near, info=info
        )
        z = send(zpay, later)
        near = gather(ipay, in_chip)
        wt, wxt, gaint = call(k_top_faces, [(4, 8), (9,), (8,)], ct, edge)
        (rm,) = call(k_mid_left, [(8,)], wm, wxm, diagm, gainm, bm, m1, z, near, info=info)
        rms = gather(rm, twins)
        bt, t0, pay, ipay = call(k_top_start, [(8,), (8,), (1,), (1,)], gaint, rms)
        z = send(t0, later2)
        edge = send(pay, outer)
        near = gather(ipay, in_chip)
        mine, other = call(
            k_top, [(8,), (8,)], wt, wxt, gaint, bt, t0, edge, z, near, m1, e1, info=info
        )
        got = send(other, pair)
        (new,) = call(k_state_out, [(16,)], u_in, mine, got, info=info)
        return new[None, None], residual[None, None]

    spec = P("tm", "space", None, None, None)
    return jax.shard_map(
        shards,
        mesh=mesh,
        in_specs=(spec, spec, P("space", None, None, None)),
        out_specs=(spec, spec),
        check_vma=False,
    )
```

time: 120 us -> 109 us (0.908)
  the two profiles are of different devices: /device:TPU:85 before, /device:TPU:95 now
where the time goes in v2:
time: 109 us; the launch traced here: 108 us
  starting transfers between devices  48.3 us (44%)
  waiting for transfers between devices  24.7 us (23%)
  blocking collectives  18.7 us (17%)
  Pallas kernels  12.2 us (11%)
  local copies, waits for them, and re-layouts  3.13 us (3%)
    ppermute x12, starting transfers between devices, send(): return lax.ppermute(x, axes, route)  48.3 us
    ppermute x12, waiting for transfers between devices, send(): return lax.ppermute(x, axes, route)  24.7 us
    all_gather x6, blocking collectives, gather(): return lax.all_gather(x, axes, axis_index_groups=groups)  18.7 us
    pallas_call x13, Pallas kernels, call(): pl.pallas_call(kernel, out_shape=[jax.ShapeDtypeStruct(s + (16, 512), jnp...  12.2 us
    unnamed x8, local copies, waits for them, and re-layouts  3.13 us
  transfers between devices with their start and end apart: 12, of which 8 were waited for; matrix products, arithmetic and copies ran while one was open for 0% of the time, Pallas kernels for 3%

profile of v2, /device:TPU:95, one launch (start us, length us, event | category | flops | bytes accessed | tf_op | source)
XLA Modules:
  0.0 108.0 jit_solution(4851581369215041843)
XLA Ops:
  0.6 0.1 pad_add_fusion.info
  0.7 1.0 copy-done
  1.8 1.0 copy-done.2
  2.8 1.0 copy-done.3
  3.8 0.8 k_split.1
  4.7 2.6 %collective-permute-start = (f32[17,16,512]{2,1,0:T(8,128)S(1)}, f32[17,16,512]{2,1,0:T(8,128)S(1)}, u32[]{:S(2)}, u32[]{:S(2)}) collective-permute-start(f32[17,16,512]{2,1,0:T(8,128)S(1)} %get-tuple-element.47), channel_id=1, source_target_pairs={{0,32},{1,33},{2,34},{3,35},{4,36},{5,37},{6,38},{7,39},{8,40},{9,... | collective-permute-start | bytes 1671176 | tf_op jit(solution)/shard_map/ppermute | solution.py:333
  7.3 1.6 %collective-permute-done.got = f32[17,16,512]{2,1,0:T(8,128)S(1)} collective-permute-done((f32[17,16,512]{2,1,0:T(8,128)S(1)}, f32[17,16,512]{2,1,0:T(8,128)S(1)}, u32[]{:S(2)}, u32[]{:S(2)}) %collective-permute-start) | collective-permute-done | bytes 557088 | tf_op jit(solution)/shard_map/ppermute | solution.py:333
  8.8 0.7 k_pack.1
  9.5 4.7 %collective-permute-start.1 = (f32[13,16,512]{2,1,0:T(8,128)S(1)}, f32[13,16,512]{2,1,0:T(8,128)S(1)}, u32[]{:S(2)}, u32[]{:S(2)}) collective-permute-start(f32[13,16,512]{2,1,0:T(8,128)S(1)} %get-tuple-element.50), channel_id=1, source_target_pairs={{1,32},{2,33},{3,34},{4,35},{5,36},{6,37},{7,38},{8,39},{9,40},{10... | collective-permute-start | bytes 1277960 | tf_op jit(solution)/shard_map/ppermute | solution.py:333
  14.2 4.0 %collective-permute-start.2 = (f32[8,16,512]{2,1,0:T(8,128)S(1)}, f32[8,16,512]{2,1,0:T(8,128)S(1)}, u32[]{:S(2)}, u32[]{:S(2)}) collective-permute-start(f32[8,16,512]{2,1,0:T(8,128)S(1)} %get-tuple-element.51), channel_id=1, source_target_pairs={{0,64},{1,65},{2,66},{3,67},{4,68},{5,69},{6,70},{7,71},{8,72},{9,... | collective-permute-start | bytes 786440 | tf_op jit(solution)/shard_map/ppermute | solution.py:333
  18.2 4.4 %collective-permute-done.2.zu = f32[8,16,512]{2,1,0:T(8,128)S(1)} collective-permute-done((f32[8,16,512]{2,1,0:T(8,128)S(1)}, f32[8,16,512]{2,1,0:T(8,128)S(1)}, u32[]{:S(2)}, u32[]{:S(2)}) %collective-permute-start.2) | collective-permute-done | bytes 262176 | tf_op jit(solution)/shard_map/ppermute | solution.py:333
  22.6 0.0 collective-permute-done.1.edge
  22.6 2.0 %k_residual.1 = (f32[4,2,10,16,512]{4,3,2,1,0:T(8,128)S(1)}, f32[2,11,16,512]{3,2,1,0:T(8,128)S(1)}, f32[2,10,16,512]{3,2,1,0:T(8,128)S(1)}, f32[2,10,16,512]{3,...) custom-call(s32[2]{0:T(128)S(1)} %pad_add_fusion.info, ...), custom_call_target="tpu_custom_call" | custom-call | flops 2621440 | bytes 2097152 | tf_op jit(solution)/shard_map/k_residual/pallas_call | solution.py:341
  24.6 4.0 %collective-permute-start.4 = (f32[11,16,512]{2,1,0:T(8,128)S(1)}, f32[11,16,512]{2,1,0:T(8,128)S(1)}, u32[]{:S(2)}, u32[]{:S(2)}) collective-permute-start(f32[11,16,512]{2,1,0:T(8,128)S(1)} %get-tuple-element.61), channel_id=1, source_target_pairs={{0,64},{1,65},{2,66},{3,67},{4,68},{5,69},{6,70},{7,71},{8,72},{9,... | collective-permute-start | bytes 1081352 | tf_op jit(solution)/shard_map/ppermute | solution.py:333
  28.6 1.9 %collective-permute-start.3 = (f32[9,16,512]{2,1,0:T(8,128)S(1)}, f32[9,16,512]{2,1,0:T(8,128)S(1)}, u32[]{:S(2)}, u32[]{:S(2)}) collective-permute-start(f32[9,16,512]{2,1,0:T(8,128)S(1)} %get-tuple-element.53), channel_id=1, source_target_pairs={{0,64},{1,65},{2,66},{3,67},{4,68},{5,69},{6,70},{7,71},{8,72},{9,... | collective-permute-start | bytes 884744 | tf_op jit(solution)/shard_map/ppermute | solution.py:333
  30.5 2.3 %all-gather = f32[20,16,512]{2,1,0:T(8,128)S(1)} all-gather(f32[10,16,512]{2,1,0:T(8,128)S(1)} %get-tuple-element.62), channel_id=2, replica_groups={{0,32},{1,33},{2,34},{3,35},{4,36},{5,37},{6,38},{7,39},{8,40},{9,41},{..., dimensions={0}, use_global_device_ids=true | all-gather | bytes 983040 | tf_op jit(solution)/shard_map/all_gather | solution.py:336
  32.8 4.1 %collective-permute-done.4.z = f32[11,16,512]{2,1,0:T(8,128)S(1)} collective-permute-done((f32[11,16,512]{2,1,0:T(8,128)S(1)}, f32[11,16,512]{2,1,0:T(8,128)S(1)}, u32[]{:S(2)}, u32[]{:S(2)}) %collective-permute-start.4) | collective-permute-done | bytes 360480 | tf_op jit(solution)/shard_map/ppermute | solution.py:333
  36.9 1.1 %k_fine.1 = (f32[2,9,16,512]{3,2,1,0:T(8,128)S(1)}, f32[8,16,512]{2,1,0:T(8,128)S(1)}, f32[2,16,512]{2,1,0:T(8,128)S(1)}) custom-call(s32[2]{0:T(128)S(1)} %pad_add_fusion.info, f32[4,2,10,16,512]{4,3,2,1,0:T(8,128)S(1)} %get-tuple-element.55.w, f32[2,11,16,512]{3,2,1,0:T(8,128)S(1)} %get-tuple-element.56.wx, f32[2,10,16,512]{3,2,1,0:T(8,128)S(1)} %get-tuple-element.59.gain, ...), custom_call_target="tpu_custom_call" | custom-call | flops 2621440 | bytes 6324224 | tf_op jit(solution)/shard_map/k_fine/pallas_call | solution.py:341
  38.0 5.1 %collective-permute-start.5 = (f32[8,16,512]{2,1,0:T(8,128)S(1)}, f32[8,16,512]{2,1,0:T(8,128)S(1)}, u32[]{:S(2)}, u32[]{:S(2)}) collective-permute-start(f32[8,16,512]{2,1,0:T(8,128)S(1)} %get-tuple-element.64), channel_id=1, source_target_pairs={{0,64},{1,65},{2,66},{3,67},{4,68},{5,69},{6,70},{7,71},{8,72},{9,... | collective-permute-start | bytes 786440 | tf_op jit(solution)/shard_map/ppermute | solution.py:333
  43.2 0.0 collective-permute-done.3.cm_twin
  43.2 0.4 k_mid_faces.1
  43.6 1.9 %all-gather.1 = f32[4,16,512]{2,1,0:T(8,128)S(1)} all-gather(f32[2,16,512]{2,1,0:T(8,128)S(1)} %get-tuple-element.65), channel_id=3, replica_groups={{0,32},{1,33},{2,34},{3,35},{4,36},{5,37},{6,38},{7,39},{8,40},{9,41},{..., dimensions={0}, use_global_device_ids=true | all-gather | bytes 196608 | tf_op jit(solution)/shard_map/all_gather | solution.py:336
  45.5 3.5 %collective-permute-done.5.z = f32[8,16,512]{2,1,0:T(8,128)S(1)} collective-permute-done((f32[8,16,512]{2,1,0:T(8,128)S(1)}, f32[8,16,512]{2,1,0:T(8,128)S(1)}, u32[]{:S(2)}, u32[]{:S(2)}) %collective-permute-start.5) | collective-permute-done | bytes 262176 | tf_op jit(solution)/shard_map/ppermute | solution.py:333
  49.0 1.1 %k_restrict.1 = (f32[8,16,512]{2,1,0:T(8,128)S(1)}, f32[8,16,512]{2,1,0:T(8,128)S(1)}, f32[3,16,512]{2,1,0:T(8,128)S(1)}, f32[1,16,512]{2,1,0:T(8,128)S(1)}) custom-call(s32[2]{0:T(128)S(1)} %pad_add_fusion.info, f32[4,2,10,16,512]{4,3,2,1,0:T(8,128)S(1)} %get-tuple-element.55.w, f32[2,11,16,512]{3,2,1,0:T(8,128)S(1)} %get-tuple-element.56.wx, ...), custom_call_target="tpu_custom_call" | custom-call | flops 2621440 | bytes 6258688 | tf_op jit(solution)/shard_map/k_restrict/pallas_call | solution.py:341
  50.1 4.4 %collective-permute-start.7 = (f32[8,16,512]{2,1,0:T(8,128)S(1)}, f32[8,16,512]{2,1,0:T(8,128)S(1)}, u32[]{:S(2)}, u32[]{:S(2)}) collective-permute-start(f32[8,16,512]{2,1,0:T(8,128)S(1)} %get-tuple-element.75.m0), channel_id=1, source_target_pairs={{0,64},{1,65},{2,66},{3,67},{4,68},{5,69},{6,70},{7,71},{8,72},{9,... | collective-permute-start | bytes 786440 | tf_op jit(solution)/shard_map/ppermute | solution.py:333
  54.5 4.9 %collective-permute-start.6 = (f32[3,16,512]{2,1,0:T(8,128)S(1)}, f32[3,16,512]{2,1,0:T(8,128)S(1)}, u32[]{:S(2)}, u32[]{:S(2)}) collective-permute-start(f32[3,16,512]{2,1,0:T(8,128)S(1)} %get-tuple-element.67), channel_id=1, source_target_pairs={{1,32},{2,33},{3,34},{4,35},{5,36},{6,37},{7,38},{8,39},{9,40},{10... | collective-permute-start | bytes 294920 | tf_op jit(solution)/shard_map/ppermute | solution.py:333
  59.4 1.9 %all-gather.2 = f32[2,16,512]{2,1,0:T(8,128)S(1)} all-gather(f32[1,16,512]{2,1,0:T(8,128)S(1)} %get-tuple-element.76), channel_id=4, replica_groups={{0,32},{1,33},{2,34},{3,35},{4,36},{5,37},{6,38},{7,39},{8,40},{9,41},{..., dimensions={0}, use_global_device_ids=true | all-gather | bytes 98304 | tf_op jit(solution)/shard_map/all_gather | solution.py:336
  61.3 0.4 collective-permute-done.6.edge
  61.7 0.0 collective-permute-done.7.z
  61.7 0.9 k_mid.1
  62.6 4.8 %collective-permute-start.8 = (f32[9,16,512]{2,1,0:T(8,128)S(1)}, f32[9,16,512]{2,1,0:T(8,128)S(1)}, u32[]{:S(2)}, u32[]{:S(2)}) collective-permute-start(f32[9,16,512]{2,1,0:T(8,128)S(1)} %get-tuple-element.78), channel_id=1, source_target_pairs={{0,64},{1,65},{2,66},{3,67},{4,68},{5,69},{6,70},{7,71},{8,72},{9,... | collective-permute-start | bytes 884744 | tf_op jit(solution)/shard_map/ppermute | solution.py:333
  67.4 0.3 k_top_faces.1
  67.7 1.9 %all-gather.3 = f32[2,16,512]{2,1,0:T(8,128)S(1)} all-gather(f32[1,16,512]{2,1,0:T(8,128)S(1)} %get-tuple-element.79), channel_id=5, replica_groups={{0,32},{1,33},{2,34},{3,35},{4,36},{5,37},{6,38},{7,39},{8,40},{9,41},{..., dimensions={0}, use_global_device_ids=true | all-gather | bytes 98304 | tf_op jit(solution)/shard_map/all_gather | solution.py:336
  69.6 4.4 %collective-permute-done.8.z = f32[9,16,512]{2,1,0:T(8,128)S(1)} collective-permute-done((f32[9,16,512]{2,1,0:T(8,128)S(1)}, f32[9,16,512]{2,1,0:T(8,128)S(1)}, u32[]{:S(2)}, u32[]{:S(2)}) %collective-permute-start.8) | collective-permute-done | bytes 294944 | tf_op jit(solution)/shard_map/ppermute | solution.py:333
  74.0 0.9 k_mid_left.1
  74.8 7.9 %all-gather.4 = f32[16,16,512]{2,1,0:T(8,128)S(1)} all-gather(f32[8,16,512]{2,1,0:T(8,128)S(1)} %k_mid_left.1), channel_id=6, replica_groups={{0,64},{1,65},{2,66},{3,67},{4,68},{5,69},{6,70},{7,71},{8,72},{9,73},{..., dimensions={0}, use_global_device_ids=true | all-gather | bytes 786432 | tf_op jit(solution)/shard_map/all_gather | solution.py:336
  82.7 0.1 k_top_start.1
  82.8 7.2 %collective-permute-start.10 = (f32[8,16,512]{2,1,0:T(8,128)S(1)}, f32[8,16,512]{2,1,0:T(8,128)S(1)}, u32[]{:S(2)}, u32[]{:S(2)}) collective-permute-start(f32[8,16,512]{2,1,0:T(8,128)S(1)} %get-tuple-element.81.t0), channel_id=1, source_target_pairs={{0,128},{1,129},{2,130},{3,131},{4,132},{5,133},{6,134},{7,135},{8... | collective-permute-start | bytes 786440 | tf_op jit(solution)/shard_map/ppermute | solution.py:333
  90.0 2.3 %collective-permute-start.9 = (f32[1,16,512]{2,1,0:T(8,128)S(1)}, f32[1,16,512]{2,1,0:T(8,128)S(1)}, u32[]{:S(2)}, u32[]{:S(2)}) collective-permute-start(f32[1,16,512]{2,1,0:T(8,128)S(1)} %get-tuple-element.82), channel_id=1, source_target_pairs={{1,32},{2,33},{3,34},{4,35},{5,36},{6,37},{7,38},{8,39},{9,40},{10... | collective-permute-start | bytes 98312 | tf_op jit(solution)/shard_map/ppermute | solution.py:333
  92.3 3.0 %all-gather.5 = f32[2,16,512]{2,1,0:T(8,128)S(1)} all-gather(f32[1,16,512]{2,1,0:T(8,128)S(1)} %get-tuple-element.83), channel_id=7, replica_groups={{0,32},{1,33},{2,34},{3,35},{4,36},{5,37},{6,38},{7,39},{8,40},{9,41},{..., dimensions={0}, use_global_device_ids=true | all-gather | bytes 98304 | tf_op jit(solution)/shard_map/all_gather | solution.py:336
  95.3 1.2 %collective-permute-done.9.edge = f32[1,16,512]{2,1,0:T(8,128)S(1)} collective-permute-done((f32[1,16,512]{2,1,0:T(8,128)S(1)}, f32[1,16,512]{2,1,0:T(8,128)S(1)}, u32[]{:S(2)}, u32[]{:S(2)}) %collective-permute-start.9) | collective-permute-done | bytes 32800 | tf_op jit(solution)/shard_map/ppermute | solution.py:333
  96.5 5.1 %collective-permute-done.10.z = f32[8,16,512]{2,1,0:T(8,128)S(1)} collective-permute-done((f32[8,16,512]{2,1,0:T(8,128)S(1)}, f32[8,16,512]{2,1,0:T(8,128)S(1)}, u32[]{:S(2)}, u32[]{:S(2)}) %collective-permute-start.10) | collective-permute-done | bytes 262176 | tf_op jit(solution)/shard_map/ppermute | solution.py:333
  101.6 0.9 k_top.1
  102.5 2.4 %collective-permute-start.11 = (f32[8,16,512]{2,1,0:T(8,128)S(1)}, f32[8,16,512]{2,1,0:T(8,128)S(1)}, u32[]{:S(2)}, u32[]{:S(2)}) collective-permute-start(f32[8,16,512]{2,1,0:T(8,128)S(1)} %get-tuple-element.85), channel_id=1, source_target_pairs={{0,32},{1,33},{2,34},{3,35},{4,36},{5,37},{6,38},{7,39},{8,40},{9,... | collective-permute-start | bytes 786440 | tf_op jit(solution)/shard_map/ppermute | solution.py:333
  104.9 1.5 %k_residual_out.1 = f32[16,16,512]{2,1,0:T(8,128)} custom-call(s32[2]{0:T(128)S(1)} %pad_add_fusion.info, f32[2,10,16,512]{3,2,1,0:T(8,128)S(1)} %get-tuple-element.58.b, f32[2,10,16,512]{3,2,1,0:T(8,128)S(1)} %bitcast.14), custom_call_target="tpu_custom_call" | custom-call | flops 2621440 | bytes 1310720 | tf_op jit(solution)/shard_map/k_residual_out/pallas_call | solution.py:341
  106.4 0.0 collective-permute-done.11.got
  106.4 0.0 copy-done.1
  106.4 1.6 %k_state_out.1 = f32[16,16,512]{2,1,0:T(8,128)} custom-call(s32[2]{0:T(128)S(1)} %pad_add_fusion.info, f32[16,16,512]{2,1,0:T(8,128)S(1)} %bitcast.17, f32[8,16,512]{2,1,0:T(8,128)S(1)} %get-tuple-element.84.mine, f32[8,16,512]{2,1,0:T(8,128)S(1)} %collective-permute-done.11.got), custom_call_target="tpu_custom_call" | custom-call | flops 2621440 | bytes 1048576 | tf_op jit(solution)/shard_map/k_state_out/pallas_call | solution.py:341
  (4 shorter events, 0.0 us)
Async XLA Ops:
  0.7 1.0 copy-start
  1.8 1.0 copy-start.2
  2.8 1.0 copy-start.3
  4.7 4.2 %collective-permute-start = (f32[17,16,512]{2,1,0:T(8,128)S(1)}, f32[17,16,512]{2,1,0:T(8,128)S(1)}, u32[]{:S(2)}, u32[]{:S(2)}) collective-permute-start(f32[17,16,512]{2,1,0:T(8,128)S(1)} %get-tuple-element.47), channel_id=1, source_target_pairs={{0,32},{1,33},{2,34},{3,35},{4,36},{5,37},{6,38},{7,39},{8,40},{9,... | collective-permute-start | bytes 1671176 | tf_op jit(solution)/shard_map/ppermute | solution.py:333
  9.5 13.1 %collective-permute-start.1 = (f32[13,16,512]{2,1,0:T(8,128)S(1)}, f32[13,16,512]{2,1,0:T(8,128)S(1)}, u32[]{:S(2)}, u32[]{:S(2)}) collective-permute-start(f32[13,16,512]{2,1,0:T(8,128)S(1)} %get-tuple-element.50), channel_id=1, source_target_pairs={{1,32},{2,33},{3,34},{4,35},{5,36},{6,37},{7,38},{8,39},{9,40},{10... | collective-permute-start | bytes 1277960 | tf_op jit(solution)/shard_map/ppermute | solution.py:333
  14.2 8.4 %collective-permute-start.2 = (f32[8,16,512]{2,1,0:T(8,128)S(1)}, f32[8,16,512]{2,1,0:T(8,128)S(1)}, u32[]{:S(2)}, u32[]{:S(2)}) collective-permute-start(f32[8,16,512]{2,1,0:T(8,128)S(1)} %get-tuple-element.51), channel_id=1, source_target_pairs={{0,64},{1,65},{2,66},{3,67},{4,68},{5,69},{6,70},{7,71},{8,72},{9,... | collective-permute-start | bytes 786440 | tf_op jit(solution)/shard_map/ppermute | solution.py:333
  24.6 12.3 %collective-permute-start.4 = (f32[11,16,512]{2,1,0:T(8,128)S(1)}, f32[11,16,512]{2,1,0:T(8,128)S(1)}, u32[]{:S(2)}, u32[]{:S(2)}) collective-permute-start(f32[11,16,512]{2,1,0:T(8,128)S(1)} %get-tuple-element.61), channel_id=1, source_target_pairs={{0,64},{1,65},{2,66},{3,67},{4,68},{5,69},{6,70},{7,71},{8,72},{9,... | collective-permute-start | bytes 1081352 | tf_op jit(solution)/shard_map/ppermute | solution.py:333
  28.6 14.5 %collective-permute-start.3 = (f32[9,16,512]{2,1,0:T(8,128)S(1)}, f32[9,16,512]{2,1,0:T(8,128)S(1)}, u32[]{:S(2)}, u32[]{:S(2)}) collective-permute-start(f32[9,16,512]{2,1,0:T(8,128)S(1)} %get-tuple-element.53), channel_id=1, source_target_pairs={{0,64},{1,65},{2,66},{3,67},{4,68},{5,69},{6,70},{7,71},{8,72},{9,... | collective-permute-start | bytes 884744 | tf_op jit(solution)/shard_map/ppermute | solution.py:333
  38.0 10.9 %collective-permute-start.5 = (f32[8,16,512]{2,1,0:T(8,128)S(1)}, f32[8,16,512]{2,1,0:T(8,128)S(1)}, u32[]{:S(2)}, u32[]{:S(2)}) collective-permute-start(f32[8,16,512]{2,1,0:T(8,128)S(1)} %get-tuple-element.64), channel_id=1, source_target_pairs={{0,64},{1,65},{2,66},{3,67},{4,68},{5,69},{6,70},{7,71},{8,72},{9,... | collective-permute-start | bytes 786440 | tf_op jit(solution)/shard_map/ppermute | solution.py:333
  50.1 11.6 %collective-permute-start.7 = (f32[8,16,512]{2,1,0:T(8,128)S(1)}, f32[8,16,512]{2,1,0:T(8,128)S(1)}, u32[]{:S(2)}, u32[]{:S(2)}) collective-permute-start(f32[8,16,512]{2,1,0:T(8,128)S(1)} %get-tuple-element.75.m0), channel_id=1, source_target_pairs={{0,64},{1,65},{2,66},{3,67},{4,68},{5,69},{6,70},{7,71},{8,72},{9,... | collective-permute-start | bytes 786440 | tf_op jit(solution)/shard_map/ppermute | solution.py:333
  54.5 7.2 %collective-permute-start.6 = (f32[3,16,512]{2,1,0:T(8,128)S(1)}, f32[3,16,512]{2,1,0:T(8,128)S(1)}, u32[]{:S(2)}, u32[]{:S(2)}) collective-permute-start(f32[3,16,512]{2,1,0:T(8,128)S(1)} %get-tuple-element.67), channel_id=1, source_target_pairs={{1,32},{2,33},{3,34},{4,35},{5,36},{6,37},{7,38},{8,39},{9,40},{10... | collective-permute-start | bytes 294920 | tf_op jit(solution)/shard_map/ppermute | solution.py:333
  62.6 11.3 %collective-permute-start.8 = (f32[9,16,512]{2,1,0:T(8,128)S(1)}, f32[9,16,512]{2,1,0:T(8,128)S(1)}, u32[]{:S(2)}, u32[]{:S(2)}) collective-permute-start(f32[9,16,512]{2,1,0:T(8,128)S(1)} %get-tuple-element.78), channel_id=1, source_target_pairs={{0,64},{1,65},{2,66},{3,67},{4,68},{5,69},{6,70},{7,71},{8,72},{9,... | collective-permute-start | bytes 884744 | tf_op jit(solution)/shard_map/ppermute | solution.py:333
  82.8 18.8 %collective-permute-start.10 = (f32[8,16,512]{2,1,0:T(8,128)S(1)}, f32[8,16,512]{2,1,0:T(8,128)S(1)}, u32[]{:S(2)}, u32[]{:S(2)}) collective-permute-start(f32[8,16,512]{2,1,0:T(8,128)S(1)} %get-tuple-element.81.t0), channel_id=1, source_target_pairs={{0,128},{1,129},{2,130},{3,131},{4,132},{5,133},{6,134},{7,135},{8... | collective-permute-start | bytes 786440 | tf_op jit(solution)/shard_map/ppermute | solution.py:333
  90.0 6.4 %collective-permute-start.9 = (f32[1,16,512]{2,1,0:T(8,128)S(1)}, f32[1,16,512]{2,1,0:T(8,128)S(1)}, u32[]{:S(2)}, u32[]{:S(2)}) collective-permute-start(f32[1,16,512]{2,1,0:T(8,128)S(1)} %get-tuple-element.82), channel_id=1, source_target_pairs={{1,32},{2,33},{3,34},{4,35},{5,36},{6,37},{7,38},{8,39},{9,40},{10... | collective-permute-start | bytes 98312 | tf_op jit(solution)/shard_map/ppermute | solution.py:333
  95.3 11.1 %copy-start.1 = (f32[1,1,16,16,512]{4,3,2,1,0:T(8,128)S(1)}, f32[1,1,16,16,512]{4,3,2,1,0:T(8,128)}, u32[]{:S(2)}) copy-start(f32[1,1,16,16,512]{4,3,2,1,0:T(8,128)} %param.3) | copy-start | bytes 1572868
  102.5 3.9 %collective-permute-start.11 = (f32[8,16,512]{2,1,0:T(8,128)S(1)}, f32[8,16,512]{2,1,0:T(8,128)S(1)}, u32[]{:S(2)}, u32[]{:S(2)}) collective-permute-start(f32[8,16,512]{2,1,0:T(8,128)S(1)} %get-tuple-element.85), channel_id=1, source_target_pairs={{0,32},{1,33},{2,34},{3,35},{4,36},{5,37},{6,38},{7,39},{8,40},{9,... | collective-permute-start | bytes 786440 | tf_op jit(solution)/shard_map/ppermute | solution.py:333

commit v3 on v2

v3 whole, which is shorter than its diff:
```python
import functools
import jax
import jax.numpy as jnp
from jax import lax
from jax.experimental import pallas as pl
from jax.experimental.pallas import tpu as pltpu
from jax.sharding import PartitionSpec as P

tau = 0.08
omega = 0.7
keep = 1.0 - omega


def routes(chips, slabs):
    def device(z, core, slab):
        return (2 * z + core) * slabs + slab

    every = [(z, c, s) for z in range(chips) for c in range(2) for s in range(slabs)]
    pair = [(device(z, c, s), device(z, 1 - c, s)) for z, c, s in every]
    outer = []
    for z, c, s in every:
        near = s - 1 if c == 0 else s + 1
        if 0 <= near < slabs:
            outer.append((device(z, c, s), device(z, 1 - c, near)))
    later = [(device(z, c, s), device(z + 1, c, s)) for z, c, s in every if z + 1 < chips]
    later2 = [(device(z, c, s), device(z + 2, c, s)) for z, c, s in every if z + 2 < chips]
    twin = [(device(z, c, s), device(z ^ 1, c, s)) for z, c, s in every]
    in_chip = [[device(z, 0, s), device(z, 1, s)] for z in range(chips) for s in range(slabs)]
    twins = [
        [device(2 * k, c, s), device(2 * k + 1, c, s)]
        for k in range(chips // 2)
        for c in range(2)
        for s in range(slabs)
    ]
    return pair, outer, later, later2, twin, in_chip, twins


def own_core():
    return lax.rem(lax.axis_index("tm"), 2)


def has_outer():
    slab = lax.axis_index("space")
    last = lax.axis_size("space") - 1
    return slab != jnp.where(own_core() == 0, 0, last)


def iota(v, axis):
    return lax.broadcasted_iota(jnp.int32, v.shape, axis)


def around(v):
    ny = v.shape[1]
    nz = v.shape[0]
    return (
        pltpu.roll(v, 1, 1),
        pltpu.roll(v, ny - 1, 1),
        pltpu.roll(v, 1, 0),
        pltpu.roll(v, nz - 1, 0),
    )


def faces(c, low, high, step):
    ny = c.shape[1]
    nz = c.shape[0]
    y = iota(c, 1)
    z = iota(c, 0)
    inside = (y > 0, y < ny - 1, z > 0, z < nz - 1)
    near = [jnp.where(ok, n, 0.0) for ok, n in zip(inside, around(c))]
    total = low + high
    for n in near:
        total = total + n
    diag = 1.0 + step * (3.0 * c + 0.5 * total)
    weights = [jnp.where(ok, (0.5 * step) * (c + n), 0.0) for ok, n in zip(inside, near)]
    return weights, (0.5 * step) * (c + high), diag


def spread(v, low, high, weights, w_low, w_high):
    flux = w_low * low + w_high * high
    for w, n in zip(weights, around(v)):
        flux = flux + w * n
    return flux


def each_row(fill):
    def rows(mirror):
        for x in range(16):
            fill(x, 15 - x if mirror else x)

    pl.when(own_core() == 0)(lambda: rows(False))
    pl.when(own_core() == 1)(lambda: rows(True))


def k_load_u(u, uo, send):
    def fill(x, row):
        if row <= 8:
            uo[row] = u[:, x, :]
        if row >= 7:
            send[15 - row] = u[:, x, :]

    each_row(fill)


def k_load_f(f, send0, fo, send):
    def fill(x, row):
        if row <= 7:
            fo[row] = f[:, x, :]
        else:
            send[24 - row] = f[:, x, :]

    each_row(fill)


def k_load_k(kap, ko):
    def fill(x, row):
        if row <= 8:
            ko[row] = kap[:, x, :]

    each_row(fill)


def k_pack(uo, fo, ko, got, u, f, edge, zu):
    h = own_core()
    for x in range(9):
        u[h, x] = uo[x]
        u[1 - h, x] = got[x]
    for x in range(8):
        f[h, x] = fo[x]
        f[1 - h, x] = got[9 + x]
        zu[x] = u[1, x]
    for x in range(3):
        edge[x] = u[0, x]
        edge[3 + x] = u[1, x]
        edge[6 + x] = ko[x]
    for x in range(2):
        edge[9 + x] = f[0, x]
        edge[11 + x] = f[1, x]


def k_inner(u, f, ko, w, wx, diag, gain, b, e0, cm, c):
    for x in range(9):
        for t in range(2):
            v = u[t, x]
            c[t, x] = ko[x] * (1.0 + v * v)
        cm[x + 3] = 0.5 * (c[0, x] + c[1, x])
    for t in range(2):
        wx[t, 3] = (0.5 * tau) * (c[t, 0] + c[t, 1])
        for x in range(1, 8):
            i = x + 2
            weights, w_high, d = faces(c[t, x], c[t, x - 1], c[t, x + 1], tau)
            wx[t, i + 1] = w_high
            for k in range(4):
                w[k, t, i] = weights[k]
            g = omega / d
            diag[t, i] = d
            gain[t, i] = g
            v = u[t, x]
            flux = spread(v, u[t, x - 1], u[t, x + 1], weights, wx[t, i], w_high)
            value = f[t, x] - d * v + flux
            if t == 1:
                value = value + u[0, x]
                e0[t, i] = g * value
            b[t, i] = value


def k_edge(
    u, f, ko, edge, w0, wx0, diag0, gain0, b0, e00, cm0, w, wx, diag, gain, b, e0, cm, zpay, c
):
    real = has_outer()

    def uu(t, x):
        return u[t, x] if x >= 0 else edge[3 * t - x - 1]

    for x in range(-3, 2):
        k = ko[x] if x >= 0 else edge[5 - x]
        for t in range(2):
            v = uu(t, x)
            c[t, x + 3] = k * (1.0 + v * v)
        if x < 0:
            cm[x + 3] = 0.5 * (c[0, x + 3] + c[1, x + 3])
    for t in range(2):
        wx[t, 0] = (0.5 * tau) * (c[t, 0] + c[t, 1])
        for x in range(-2, 1):
            i = x + 2
            weights, w_high, d = faces(c[t, i + 1], c[t, i], c[t, i + 2], tau)
            wx[t, i + 1] = w_high
            for k in range(4):
                w[k, t, i] = weights[k]
            g = omega / d
            diag[t, i] = d
            gain[t, i] = g
            v = uu(t, x)
            f_row = f[t, x] if x >= 0 else edge[8 + 2 * t - x]
            value = f_row - d * v + spread(v, uu(t, x - 1), uu(t, x + 1), weights, wx[t, i], w_high)
            if t == 1:
                value = value + uu(0, x)
            if x < 0:
                value = jnp.where(real, value, 0.0)
            b[t, i] = value
            e0[t, i] = g * value
    for i in range(9):
        zpay[i] = e0[1, i + 1]
    zpay[9] = edge[3]
    zpay[10] = edge[4]


def k_prev(zu, gain, b0, e00, b, e0, ipay):
    h = own_core()
    for x in range(8):
        value = b0[0, x + 2] + zu[x]
        b[0, x + 2] = value
        e0[0, x + 2] = gain[0, x + 2] * value
    ipay[0] = e0[0, 9]
    ipay[1] = e0[1, 9]
    for x in range(8):
        ipay[2 + x] = b[1 - h, x + 2]


def smoothed(here, low, high, w, wx, gain, t, i, right):
    weights = [w[k, t, i] for k in range(4)]
    flux = spread(here, low, high, weights, wx[t, i], wx[t, i + 1])
    return keep * here + gain[t, i] * (right + flux)


def k_fine(w, wx, gain, b, e0, near, e1, zpay):
    h = own_core()
    for t in (1, 0):
        for x in range(1 - t, 8):
            i = x + 2
            high = e0[t, i + 1] if x < 7 else near[1 - h, t]
            right = b[t, i] + e0[0, i] if t == 1 else b[t, i]
            value = smoothed(e0[t, i], e0[t, i - 1], high, w, wx, gain, t, i, right)
            e1[t, i - 1] = value
            if t == 1:
                zpay[x] = value


def k_fine_prev(w, wx, gain, b, e0, z, e10, e1, ipay):
    real = has_outer()
    for x in range(1, 8):
        i = x + 2
        e1[0, i - 1] = e10[0, i - 1] + gain[0, i] * z[i - 1]
    far, edge = [
        e0[0, i] + jnp.where(real, gain[0, i] * z[10 - i], 0.0) for i in range(2)
    ]
    e1[0, 1] = smoothed(e0[0, 2], edge, e0[0, 3], w, wx, gain, 0, 2, b[0, 2] + z[1])
    value = smoothed(edge, far, e0[0, 2], w, wx, gain, 0, 1, b[0, 1] + z[0] + z[9])
    e1[0, 0] = jnp.where(real, value, 0.0)
    value = smoothed(e0[1, 1], e0[1, 0], e0[1, 2], w, wx, gain, 1, 1, b[1, 1] + edge)
    e1[1, 0] = jnp.where(real, value, 0.0)
    ipay[0] = e1[0, 8]
    ipay[1] = e10[1, 8]


def k_mid_faces(cm, w, wx, diag, gain):
    wx[0] = tau * (cm[0] + cm[1])
    for i in range(10):
        weights, w_high, d = faces(cm[i + 1], cm[i], cm[i + 2], 2 * tau)
        wx[i + 1] = w_high
        for k in range(4):
            w[k, i] = weights[k]
        diag[i] = d
        gain[i] = omega / d


def k_restrict(w, wx, diag, b, e1, near, part):
    h = own_core()
    for x in range(8):
        i = x + 2
        value = e1[0, x + 1]
        for t in range(2):
            here = e1[t, x + 1]
            high = e1[t, x + 2] if x < 7 else near[1 - h, t]
            weights = [w[k, t, i] for k in range(4)]
            flux = spread(here, e1[t, x], high, weights, wx[t, i], wx[t, i + 1])
            value = value + (b[t, i] - diag[t, i] * here + flux)
        part[x] = value


def k_restrict_prev(part, z, gain, bm, m0, edge, ipay):
    for x in range(8):
        value = part[x] + z[x]
        bm[x] = value
        m0[x] = gain[x + 2] * value
    edge[0] = bm[0]
    edge[1] = bm[1]
    ipay[0] = m0[7]


def smoothed_mid(here, low, high, w, wx, gain, i, right):
    weights = [w[k, i] for k in range(4)]
    flux = spread(here, low, high, weights, wx[i], wx[i + 1])
    return keep * here + gain[i] * (right + flux)


def k_mid(w, wx, gain, bm, m0, near, cm, m1, cpay):
    h = own_core()
    for x in range(10):
        cpay[x] = cm[x + 2]
    for x in range(1, 8):
        high = m0[x + 1] if x < 7 else near[1 - h, 0]
        m1[x + 1] = smoothed_mid(m0[x], m0[x - 1], high, w, wx, gain, x + 2, bm[x])


def k_mid_prev(w, wx, gain, bm, m0, edge, z, m10, m1, zpay, ipay):
    real = has_outer()
    far, near = gain[0] * edge[1], gain[1] * edge[0]
    for x in range(1, 8):
        value = m10[x + 1] + gain[x + 2] * z[x]
        m1[x + 1] = value
        zpay[x] = value
    value = smoothed_mid(m0[0], near, m0[1], w, wx, gain, 2, bm[0] + z[0])
    m1[1] = value
    zpay[0] = value
    value = smoothed_mid(near, far, m0[0], w, wx, gain, 1, edge[0])
    m1[0] = jnp.where(real, value, 0.0)
    zpay[8] = near
    ipay[0] = m1[8]


def left_mid(here, low, high, w, wx, diag, i, right):
    weights = [w[k, i] for k in range(4)]
    flux = spread(here, low, high, weights, wx[i], wx[i + 1])
    return right - diag[i] * here + flux


def k_mid_left(w, wx, diag, bm, m1, near, rm):
    h = own_core()
    for x in range(1, 8):
        high = m1[x + 2] if x < 7 else near[1 - h, 0]
        rm[x] = left_mid(m1[x + 1], m1[x], high, w, wx, diag, x + 2, bm[x])


def k_mid_left_prev(w, wx, diag, gain, bm, m1, z, rm0, rm):
    real = has_outer()
    low = m1[0] + jnp.where(real, gain[1] * z[8], 0.0)
    rm[0] = left_mid(m1[1], low, m1[2], w, wx, diag, 2, bm[0] + z[0])
    for x in range(1, 8):
        rm[x] = rm0[x] + z[x]


def k_top_faces(cm, twin, _, w, wx, gain, ct):
    for i in range(10):
        ct[i] = 0.5 * (cm[i + 2] + twin[i])
    wx[0] = (2 * tau) * (ct[0] + ct[1])
    for x in range(8):
        weights, w_high, d = faces(ct[x + 1], ct[x], ct[x + 2], 4 * tau)
        wx[x + 1] = w_high
        for k in range(4):
            w[k, x] = weights[k]
        gain[x] = omega / d


def k_top_start(gain, rm, bt, t0, edge, ipay):
    for x in range(8):
        value = rm[0, x] + rm[1, x]
        bt[x] = value
        t0[x] = gain[x] * value
    edge[0] = t0[0]
    ipay[0] = t0[7]


def k_top(w, wx, gain, bt, t0, near, m1, e1, mine, other):
    h = own_core()
    for x in range(1, 8):
        high = t0[x + 1] if x < 7 else near[1 - h, 0]
        value = smoothed_mid(t0[x], t0[x - 1], high, w, wx, gain, x, bt[x]) + m1[x + 1]
        mine[x] = e1[h, x + 1] + value
        other[x] = e1[1 - h, x + 1] + value


def k_top_prev(w, wx, gain, bt, t0, edge, z, m1, e1, mine0, other0, mine, other):
    h = own_core()
    for x in range(1, 8):
        value = gain[x] * z[x]
        mine[x] = mine0[x] + value
        other[x] = other0[x] + value
    value = smoothed_mid(t0[0], edge[0], t0[1], w, wx, gain, 0, bt[0] + z[0]) + m1[1]
    mine[0] = e1[h, 1] + value
    other[0] = e1[1 - h, 1] + value


def k_residual_out(b, near, out):
    h = own_core()

    def rows(mirror):
        for x in range(16):
            row = 15 - x if mirror else x
            out[:, x, :] = b[h, row + 2] if row < 8 else near[1 - h, 2 + 15 - row]

    pl.when(h == 0)(lambda: rows(False))
    pl.when(h == 1)(lambda: rows(True))


def store_half(u, add, out, buf, sems, start, row_of):
    copies = []
    for j in range(2):
        part = pl.ds(8 * j, 8)
        for x in range(8):
            buf[part, x, :] = u[part, start + x, :] + add[row_of(x), part, :]
        copies.append(
            pltpu.make_async_copy(buf.at[part], out.at[part, pl.ds(start, 8)], sems.at[j])
        )
        copies[-1].start()
    for copy in copies:
        copy.wait()


def k_state_own(u, mine, out, buf, sems):
    pl.when(own_core() == 0)(lambda: store_half(u, mine, out, buf, sems, 0, lambda x: x))
    pl.when(own_core() == 1)(lambda: store_half(u, mine, out, buf, sems, 8, lambda x: 7 - x))


def k_state_far(u, got, out0, out, buf, sems):
    pl.when(own_core() == 0)(lambda: store_half(u, got, out, buf, sems, 8, lambda x: 7 - x))
    pl.when(own_core() == 1)(lambda: store_half(u, got, out, buf, sems, 0, lambda x: x))


VMEM = pl.BlockSpec(memory_space=pltpu.VMEM)
HBM = pl.BlockSpec(memory_space=pltpu.HBM)


def solution(mesh):
    slabs = mesh.shape["space"]
    chips = mesh.shape["tm"] // 2
    pair, outer, later, later2, twin, in_chip, twins = routes(chips, slabs)
    axes = ("tm", "space")

    def send(x, route):
        return lax.ppermute(x, axes, route)

    def gather(x, groups):
        return lax.all_gather(x, axes, axis_index_groups=groups)

    def call(kernel, shapes, *args, scratch=(), alias=(), work=20, sems=0, far=(), far_out=()):
        size = sum(a.size for a in args) * 4
        scratches = [pltpu.VMEM(s + (16, 512), jnp.float32) for s in scratch]
        if sems:
            scratches.append(pltpu.SemaphoreType.DMA((sems,)))
        return pl.pallas_call(
            kernel,
            out_shape=[jax.ShapeDtypeStruct(s + (16, 512), jnp.float32) for s in shapes],
            in_specs=[HBM if i in far else VMEM for i in range(len(args))],
            out_specs=[HBM if i in far_out else VMEM for i in range(len(shapes))],
            scratch_shapes=scratches,
            input_output_aliases=dict(alias),
            cost_estimate=pl.CostEstimate(flops=work * 131072, bytes_accessed=size, transcendentals=0),
            compiler_params=pltpu.CompilerParams(vmem_limit_bytes=24 * 2**20),
            name=kernel.__name__,
        )(*args)

    def shards(iterate, source_term, conductivity):
        u_in = iterate[0, 0]

        uo, pay = call(k_load_u, [(9,), (17,)], u_in)
        fo, pay = call(k_load_f, [(8,), (17,)], source_term[0, 0], pay, alias=[(1, 1)])
        (ko,) = call(k_load_k, [(9,)], conductivity[0])
        got = send(pay, pair)
        u, f, edge, zu = call(k_pack, [(2, 9), (2, 8), (13,), (8,)], uo, fo, ko, got)
        edge = send(edge, outer)
        zu = send(zu, later)
        fields = [(4, 2, 10), (2, 11), (2, 10), (2, 10), (2, 10), (2, 10), (12,)]
        held = call(k_inner, fields, u, f, ko, scratch=[(2, 9)])
        w, wx, diag, gain, b, e0, cm, zpay = call(
            k_edge, fields + [(11,)], u, f, ko, edge, *held,
            scratch=[(2, 5)], alias=[(4 + i, i) for i in range(7)],
        )
        z = send(zpay, later)
        b, e0, ipay = call(
            k_prev, [(2, 10), (2, 10), (10,)], zu, gain, b, e0, alias=[(2, 0), (3, 1)]
        )
        near_b = gather(ipay, in_chip)
        e1, zpay = call(k_fine, [(2, 9), (8,)], w, wx, gain, b, e0, near_b)
        z1 = send(zpay, later)
        e1, ipay = call(
            k_fine_prev, [(2, 9), (2,)], w, wx, gain, b, e0, z, e1, alias=[(6, 0)]
        )
        near = gather(ipay, in_chip)
        (residual,) = call(k_residual_out, [(16,)], b, near_b)
        (part,) = call(k_restrict, [(8,)], w, wx, diag, b, e1, near)
        wm, wxm, diagm, gainm = call(k_mid_faces, [(4, 10), (11,), (10,), (10,)], cm)
        bm, m0, pay, ipay = call(
            k_restrict_prev, [(8,), (8,), (2,), (1,)], part, z1, gainm
        )
        z = send(m0, later)
        edge = send(pay, outer)
        near = gather(ipay, in_chip)
        m1, pay = call(k_mid, [(9,), (10,)], wm, wxm, gainm, bm, m0, near, cm)
        cm_twin = send(pay, twin)
        m1, zpay, ipay = call(
            k_mid_prev, [(9,), (9,), (1,)], wm, wxm, gainm, bm, m0, edge, z, m1,
            alias=[(7, 0)],
        )
        z = send(zpay, later)
        near = gather(ipay, in_chip)
        wt, wxt, gaint = call(k_top_faces, [(4, 8), (9,), (8,)], cm, cm_twin, residual, scratch=[(10,)], far=(2,))
        (rm,) = call(k_mid_left, [(8,)], wm, wxm, diagm, bm, m1, near)
        (rm,) = call(
            k_mid_left_prev, [(8,)], wm, wxm, diagm, gainm, bm, m1, z, rm, alias=[(7, 0)]
        )
        rms = gather(rm, twins)
        bt, t0, pay, ipay = call(k_top_start, [(8,), (8,), (1,), (1,)], gaint, rms)
        z = send(t0, later2)
        edge = send(pay, outer)
        near = gather(ipay, in_chip)
        mine, other = call(
            k_top, [(8,), (8,)], wt, wxt, gaint, bt, t0, near, m1, e1
        )
        mine, other = call(
            k_top_prev, [(8,), (8,)], wt, wxt, gaint, bt, t0, edge, z, m1, e1, mine, other,
            alias=[(9, 0), (10, 1)],
        )
        got = send(other, pair)
        half = pltpu.VMEM((16, 8, 512), jnp.float32)
        own_spec = dict(
            out_shape=jax.ShapeDtypeStruct((16, 16, 512), jnp.float32),
            out_specs=HBM,
            scratch_shapes=[half, pltpu.SemaphoreType.DMA((2,))],
            compiler_params=pltpu.CompilerParams(vmem_limit_bytes=24 * 2**20),
        )
        new = pl.pallas_call(
            k_state_own, in_specs=[VMEM, VMEM], name="k_state_own", **own_spec
        )(u_in, mine)
        new = pl.pallas_call(
            k_state_far,
            in_specs=[VMEM, VMEM, HBM],
            input_output_aliases={2: 0},
            name="k_state_far",
            **own_spec,
        )(u_in, got, new)
        return new[None, None], residual[None, None]

    spec = P("tm", "space", None, None, None)
    return jax.shard_map(
        shards,
        mesh=mesh,
        in_specs=(spec, spec, P("space", None, None, None)),
        out_specs=(spec, spec),
        check_vma=False,
    )
```

time: 109 us -> 96.9 us (0.89)
  the two profiles are of different devices: /device:TPU:95 before, /device:TPU:71 now
where the time goes in v3:
time: 96.9 us; the launch traced here: 96.2 us
  starting transfers between devices  48.3 us (50%)
  blocking collectives  23.3 us (24%)
  waiting for transfers between devices  13.2 us (14%)
  Pallas kernels  7.39 us (8%)
  local copies, waits for them, and re-layouts  3.12 us (3%)
    ppermute x12, starting transfers between devices, send(): return lax.ppermute(x, axes, route)  48.3 us
    all_gather x6, blocking collectives, gather(): return lax.all_gather(x, axes, axis_index_groups=groups)  23.3 us
    ppermute x12, waiting for transfers between devices, send(): return lax.ppermute(x, axes, route)  13.2 us
    pallas_call x21, Pallas kernels, call(): pl.pallas_call(kernel, out_shape=[jax.ShapeDtypeStruct(s + (16, 512), jnp...  5.81 us
    unnamed x10, local copies, waits for them, and re-layouts  3.12 us
  transfers between devices with their start and end apart: 12, of which 6 were waited for; matrix products, arithmetic and copies ran while one was open for 0% of the time, Pallas kernels for 6%

profile of v3, /device:TPU:71, one launch (start us, length us, event | category | flops | bytes accessed | tf_op | source)
XLA Modules:
  0.0 96.2 jit_solution(6346866913965785374)
XLA Ops:
  0.6 1.0 %copy-done = f32[1,1,16,16,512]{4,3,2,1,0:T(8,128)S(1)} copy-done((f32[1,1,16,16,512]{4,3,2,1,0:T(8,128)S(1)}, f32[1,1,16,16,512]{4,3,2,1,0:T(8,128)}, u32[]{:S(2)}) %copy-start) | copy-done | bytes 524312
  1.7 0.1 k_load_u.1
  1.8 1.0 %copy-done.3 = f32[1,1,16,16,512]{4,3,2,1,0:T(8,128)S(1)} copy-done((f32[1,1,16,16,512]{4,3,2,1,0:T(8,128)S(1)}, f32[1,1,16,16,512]{4,3,2,1,0:T(8,128)}, u32[]{:S(2)}) %copy-start.3) | copy-done | bytes 524312
  2.8 0.1 k_load_f.1
  2.9 2.6 %collective-permute-start = (f32[17,16,512]{2,1,0:T(8,128)S(1)}, f32[17,16,512]{2,1,0:T(8,128)S(1)}, u32[]{:S(2)}, u32[]{:S(2)}) collective-permute-start(f32[17,16,512]{2,1,0:T(8,128)S(1)} %get-tuple-element.59), channel_id=1, source_target_pairs={{0,32},{1,33},{2,34},{3,35},{4,36},{5,37},{6,38},{7,39},{8,40},{9,... | collective-permute-start | bytes 1671176 | tf_op jit(solution)/shard_map/ppermute | solution.py:430
  5.5 1.0 %copy-done.4 = f32[1,16,16,512]{3,2,1,0:T(8,128)S(1)} copy-done((f32[1,16,16,512]{3,2,1,0:T(8,128)S(1)}, f32[1,16,16,512]{3,2,1,0:T(8,128)}, u32[]{:S(2)}) %copy-start.4) | copy-done | bytes 524312
  6.6 0.1 k_load_k.1.ko
  6.6 0.5 collective-permute-done.got
  7.1 0.1 k_pack.1
  7.2 3.5 %collective-permute-start.1 = (f32[13,16,512]{2,1,0:T(8,128)S(1)}, f32[13,16,512]{2,1,0:T(8,128)S(1)}, u32[]{:S(2)}, u32[]{:S(2)}) collective-permute-start(f32[13,16,512]{2,1,0:T(8,128)S(1)} %get-tuple-element.62), channel_id=1, source_target_pairs={{1,32},{2,33},{3,34},{4,35},{5,36},{6,37},{7,38},{8,39},{9,40},{10... | collective-permute-start | bytes 1277960 | tf_op jit(solution)/shard_map/ppermute | solution.py:430
  10.7 4.0 %collective-permute-start.2 = (f32[8,16,512]{2,1,0:T(8,128)S(1)}, f32[8,16,512]{2,1,0:T(8,128)S(1)}, u32[]{:S(2)}, u32[]{:S(2)}) collective-permute-start(f32[8,16,512]{2,1,0:T(8,128)S(1)} %get-tuple-element.77), channel_id=1, source_target_pairs={{0,64},{1,65},{2,66},{3,67},{4,68},{5,69},{6,70},{7,71},{8,72},{9,... | collective-permute-start | bytes 786440 | tf_op jit(solution)/shard_map/ppermute | solution.py:430
  14.7 1.0 %k_inner.1 = (f32[4,2,10,16,512]{4,3,2,1,0:T(8,128)S(1)}, f32[2,11,16,512]{3,2,1,0:T(8,128)S(1)}, f32[2,10,16,512]{3,2,1,0:T(8,128)S(1)}, f32[2,10,16,512]{3,2,1...) custom-call(f32[2,9,16,512]{3,2,1,0:T(8,128)S(1)} %get-tuple-element.60., ...), custom_call_target="tpu_custom_call" | custom-call | flops 2621440 | bytes 1409024 | tf_op jit(solution)/shard_map/k_inner/pallas_call | solution.py:440
  15.7 1.3 %collective-permute-done.1.edge = f32[13,16,512]{2,1,0:T(8,128)S(1)} collective-permute-done((f32[13,16,512]{2,1,0:T(8,128)S(1)}, f32[13,16,512]{2,1,0:T(8,128)S(1)}, u32[]{:S(2)}, u32[]{:S(2)}) %collective-permute-start.1) | collective-permute-done | bytes 426016 | tf_op jit(solution)/shard_map/ppermute | solution.py:430
  17.0 0.5 k_edge.1
  17.4 4.0 %collective-permute-start.3 = (f32[11,16,512]{2,1,0:T(8,128)S(1)}, f32[11,16,512]{2,1,0:T(8,128)S(1)}, u32[]{:S(2)}, u32[]{:S(2)}) collective-permute-start(f32[11,16,512]{2,1,0:T(8,128)S(1)} %get-tuple-element.83), channel_id=1, source_target_pairs={{0,64},{1,65},{2,66},{3,67},{4,68},{5,69},{6,70},{7,71},{8,72},{9,... | collective-permute-start | bytes 1081352 | tf_op jit(solution)/shard_map/ppermute | solution.py:430
  21.4 0.1 k_prev.1
  21.5 4.4 %all-gather = f32[20,16,512]{2,1,0:T(8,128)S(1)} all-gather(f32[10,16,512]{2,1,0:T(8,128)S(1)} %get-tuple-element.84), channel_id=2, replica_groups={{0,32},{1,33},{2,34},{3,35},{4,36},{5,37},{6,38},{7,39},{8,40},{9,41},{..., dimensions={0}, use_global_device_ids=true | all-gather | bytes 983040 | tf_op jit(solution)/shard_map/all_gather | solution.py:433
  25.9 0.4 k_fine.1
  26.3 4.3 %collective-permute-start.4 = (f32[8,16,512]{2,1,0:T(8,128)S(1)}, f32[8,16,512]{2,1,0:T(8,128)S(1)}, u32[]{:S(2)}, u32[]{:S(2)}) collective-permute-start(f32[8,16,512]{2,1,0:T(8,128)S(1)} %get-tuple-element.88), channel_id=1, source_target_pairs={{0,64},{1,65},{2,66},{3,67},{4,68},{5,69},{6,70},{7,71},{8,72},{9,... | collective-permute-start | bytes 786440 | tf_op jit(solution)/shard_map/ppermute | solution.py:430
  30.7 0.4 k_mid_faces.1
  31.1 0.2 k_fine_prev.1
  31.3 2.2 %all-gather.1 = f32[4,16,512]{2,1,0:T(8,128)S(1)} all-gather(f32[2,16,512]{2,1,0:T(8,128)S(1)} %get-tuple-element.87), channel_id=3, replica_groups={{0,32},{1,33},{2,34},{3,35},{4,36},{5,37},{6,38},{7,39},{8,40},{9,41},{..., dimensions={0}, use_global_device_ids=true | all-gather | bytes 196608 | tf_op jit(solution)/shard_map/all_gather | solution.py:433
  33.5 0.5 k_restrict.1.part
  33.9 2.1 %collective-permute-done.4.z = f32[8,16,512]{2,1,0:T(8,128)S(1)} collective-permute-done((f32[8,16,512]{2,1,0:T(8,128)S(1)}, f32[8,16,512]{2,1,0:T(8,128)S(1)}, u32[]{:S(2)}, u32[]{:S(2)}) %collective-permute-start.4) | collective-permute-done | bytes 262176 | tf_op jit(solution)/shard_map/ppermute | solution.py:430
  36.0 4.9 %collective-permute-start.7 = (f32[8,16,512]{2,1,0:T(8,128)S(1)}, f32[8,16,512]{2,1,0:T(8,128)S(1)}, u32[]{:S(2)}, u32[]{:S(2)}) collective-permute-start(f32[8,16,512]{2,1,0:T(8,128)S(1)} %get-tuple-element.90.m0), channel_id=1, source_target_pairs={{0,64},{1,65},{2,66},{3,67},{4,68},{5,69},{6,70},{7,71},{8,72},{9,... | collective-permute-start | bytes 786440 | tf_op jit(solution)/shard_map/ppermute | solution.py:430
  40.9 2.5 %collective-permute-start.6 = (f32[2,16,512]{2,1,0:T(8,128)S(1)}, f32[2,16,512]{2,1,0:T(8,128)S(1)}, u32[]{:S(2)}, u32[]{:S(2)}) collective-permute-start(f32[2,16,512]{2,1,0:T(8,128)S(1)} %get-tuple-element.97), channel_id=1, source_target_pairs={{1,32},{2,33},{3,34},{4,35},{5,36},{6,37},{7,38},{8,39},{9,40},{10... | collective-permute-start | bytes 196616 | tf_op jit(solution)/shard_map/ppermute | solution.py:430
  43.4 4.7 %all-gather.2 = f32[2,16,512]{2,1,0:T(8,128)S(1)} all-gather(f32[1,16,512]{2,1,0:T(8,128)S(1)} %get-tuple-element.91), channel_id=4, replica_groups={{0,32},{1,33},{2,34},{3,35},{4,36},{5,37},{6,38},{7,39},{8,40},{9,41},{..., dimensions={0}, use_global_device_ids=true | all-gather | bytes 98304 | tf_op jit(solution)/shard_map/all_gather | solution.py:433
  48.2 0.3 k_mid.1
  48.4 1.9 %collective-permute-start.5 = (f32[10,16,512]{2,1,0:T(8,128)S(1)}, f32[10,16,512]{2,1,0:T(8,128)S(1)}, u32[]{:S(2)}, u32[]{:S(2)}) collective-permute-start(f32[10,16,512]{2,1,0:T(8,128)S(1)} %get-tuple-element.92), channel_id=1, source_target_pairs={{0,64},{1,65},{2,66},{3,67},{4,68},{5,69},{6,70},{7,71},{8,72},{9,... | collective-permute-start | bytes 983048 | tf_op jit(solution)/shard_map/ppermute | solution.py:430
  50.4 0.1 k_mid_prev.1
  50.5 7.4 %collective-permute-start.8 = (f32[9,16,512]{2,1,0:T(8,128)S(1)}, f32[9,16,512]{2,1,0:T(8,128)S(1)}, u32[]{:S(2)}, u32[]{:S(2)}) collective-permute-start(f32[9,16,512]{2,1,0:T(8,128)S(1)} %get-tuple-element.100), channel_id=1, source_target_pairs={{0,64},{1,65},{2,66},{3,67},{4,68},{5,69},{6,70},{7,71},{8,72},{9,... | collective-permute-start | bytes 884744 | tf_op jit(solution)/shard_map/ppermute | solution.py:430
  57.9 0.9 k_residual_out.1._
  58.9 2.5 %all-gather.3 = f32[2,16,512]{2,1,0:T(8,128)S(1)} all-gather(f32[1,16,512]{2,1,0:T(8,128)S(1)} %get-tuple-element.101), channel_id=5, replica_groups={{0,32},{1,33},{2,34},{3,35},{4,36},{5,37},{6,38},{7,39},{8,40},{9,41},{..., dimensions={0}, use_global_device_ids=true | all-gather | bytes 98304 | tf_op jit(solution)/shard_map/all_gather | solution.py:433
  61.4 0.2 k_mid_left.1.rm0
  61.7 0.4 k_top_faces.1
  62.1 3.5 %collective-permute-done.8.z = f32[9,16,512]{2,1,0:T(8,128)S(1)} collective-permute-done((f32[9,16,512]{2,1,0:T(8,128)S(1)}, f32[9,16,512]{2,1,0:T(8,128)S(1)}, u32[]{:S(2)}, u32[]{:S(2)}) %collective-permute-start.8) | collective-permute-done | bytes 294944 | tf_op jit(solution)/shard_map/ppermute | solution.py:430
  65.6 0.1 k_mid_left_prev.1
  65.7 7.3 %all-gather.4 = f32[16,16,512]{2,1,0:T(8,128)S(1)} all-gather(f32[8,16,512]{2,1,0:T(8,128)S(1)} %k_mid_left_prev.1), channel_id=6, replica_groups={{0,64},{1,65},{2,66},{3,67},{4,68},{5,69},{6,70},{7,71},{8,72},{9,73},{..., dimensions={0}, use_global_device_ids=true | all-gather | bytes 786432 | tf_op jit(solution)/shard_map/all_gather | solution.py:433
  73.0 7.2 %collective-permute-start.10 = (f32[8,16,512]{2,1,0:T(8,128)S(1)}, f32[8,16,512]{2,1,0:T(8,128)S(1)}, u32[]{:S(2)}, u32[]{:S(2)}) collective-permute-start(f32[8,16,512]{2,1,0:T(8,128)S(1)} %get-tuple-element.103.t0), channel_id=1, source_target_pairs={{0,128},{1,129},{2,130},{3,131},{4,132},{5,133},{6,134},{7,135},{8... | collective-permute-start | bytes 786440 | tf_op jit(solution)/shard_map/ppermute | solution.py:430
  80.2 3.7 %collective-permute-start.9 = (f32[1,16,512]{2,1,0:T(8,128)S(1)}, f32[1,16,512]{2,1,0:T(8,128)S(1)}, u32[]{:S(2)}, u32[]{:S(2)}) collective-permute-start(f32[1,16,512]{2,1,0:T(8,128)S(1)} %get-tuple-element.104), channel_id=1, source_target_pairs={{1,32},{2,33},{3,34},{4,35},{5,36},{6,37},{7,38},{8,39},{9,40},{10... | collective-permute-start | bytes 98312 | tf_op jit(solution)/shard_map/ppermute | solution.py:430
  83.9 2.1 %all-gather.5 = f32[2,16,512]{2,1,0:T(8,128)S(1)} all-gather(f32[1,16,512]{2,1,0:T(8,128)S(1)} %get-tuple-element.105), channel_id=7, replica_groups={{0,32},{1,33},{2,34},{3,35},{4,36},{5,37},{6,38},{7,39},{8,40},{9,41},{..., dimensions={0}, use_global_device_ids=true | all-gather | bytes 98304 | tf_op jit(solution)/shard_map/all_gather | solution.py:433
  86.0 0.3 k_top.1
  86.3 5.5 %collective-permute-done.10.z = f32[8,16,512]{2,1,0:T(8,128)S(1)} collective-permute-done((f32[8,16,512]{2,1,0:T(8,128)S(1)}, f32[8,16,512]{2,1,0:T(8,128)S(1)}, u32[]{:S(2)}, u32[]{:S(2)}) %collective-permute-start.10) | collective-permute-done | bytes 262176 | tf_op jit(solution)/shard_map/ppermute | solution.py:430
  91.8 0.1 k_top_prev.1
  91.9 2.4 %collective-permute-start.11 = (f32[8,16,512]{2,1,0:T(8,128)S(1)}, f32[8,16,512]{2,1,0:T(8,128)S(1)}, u32[]{:S(2)}, u32[]{:S(2)}) collective-permute-start(f32[8,16,512]{2,1,0:T(8,128)S(1)} %get-tuple-element.108), channel_id=1, source_target_pairs={{0,32},{1,33},{2,34},{3,35},{4,36},{5,37},{6,38},{7,39},{8,40},{9,... | collective-permute-start | bytes 786440 | tf_op jit(solution)/shard_map/ppermute | solution.py:430
  94.3 0.8 k_state_own.1.out0
  95.1 0.3 collective-permute-done.11.got
  95.5 0.8 k_state_far.1
  (15 shorter events, 0.1 us)
Async XLA Ops:
  0.6 1.0 %copy-start = (f32[1,1,16,16,512]{4,3,2,1,0:T(8,128)S(1)}, f32[1,1,16,16,512]{4,3,2,1,0:T(8,128)}, u32[]{:S(2)}) copy-start(f32[1,1,16,16,512]{4,3,2,1,0:T(8,128)} %param.3) | copy-start | bytes 1572868
  1.8 1.0 %copy-start.3 = (f32[1,1,16,16,512]{4,3,2,1,0:T(8,128)S(1)}, f32[1,1,16,16,512]{4,3,2,1,0:T(8,128)}, u32[]{:S(2)}) copy-start(f32[1,1,16,16,512]{4,3,2,1,0:T(8,128)} %param.4) | copy-start | bytes 1572868
  2.9 4.2 %collective-permute-start = (f32[17,16,512]{2,1,0:T(8,128)S(1)}, f32[17,16,512]{2,1,0:T(8,128)S(1)}, u32[]{:S(2)}, u32[]{:S(2)}) collective-permute-start(f32[17,16,512]{2,1,0:T(8,128)S(1)} %get-tuple-element.59), channel_id=1, source_target_pairs={{0,32},{1,33},{2,34},{3,35},{4,36},{5,37},{6,38},{7,39},{8,40},{9,... | collective-permute-start | bytes 1671176 | tf_op jit(solution)/shard_map/ppermute | solution.py:430
  5.5 1.0 %copy-start.4 = (f32[1,16,16,512]{3,2,1,0:T(8,128)S(1)}, f32[1,16,16,512]{3,2,1,0:T(8,128)}, u32[]{:S(2)}) copy-start(f32[1,16,16,512]{3,2,1,0:T(8,128)} %param.5) | copy-start | bytes 1572868
  7.2 9.7 %collective-permute-start.1 = (f32[13,16,512]{2,1,0:T(8,128)S(1)}, f32[13,16,512]{2,1,0:T(8,128)S(1)}, u32[]{:S(2)}, u32[]{:S(2)}) collective-permute-start(f32[13,16,512]{2,1,0:T(8,128)S(1)} %get-tuple-element.62), channel_id=1, source_target_pairs={{1,32},{2,33},{3,34},{4,35},{5,36},{6,37},{7,38},{8,39},{9,40},{10... | collective-permute-start | bytes 1277960 | tf_op jit(solution)/shard_map/ppermute | solution.py:430
  10.7 10.7 %collective-permute-start.2 = (f32[8,16,512]{2,1,0:T(8,128)S(1)}, f32[8,16,512]{2,1,0:T(8,128)S(1)}, u32[]{:S(2)}, u32[]{:S(2)}) collective-permute-start(f32[8,16,512]{2,1,0:T(8,128)S(1)} %get-tuple-element.77), channel_id=1, source_target_pairs={{0,64},{1,65},{2,66},{3,67},{4,68},{5,69},{6,70},{7,71},{8,72},{9,... | collective-permute-start | bytes 786440 | tf_op jit(solution)/shard_map/ppermute | solution.py:430
  17.4 13.6 %collective-permute-start.3 = (f32[11,16,512]{2,1,0:T(8,128)S(1)}, f32[11,16,512]{2,1,0:T(8,128)S(1)}, u32[]{:S(2)}, u32[]{:S(2)}) collective-permute-start(f32[11,16,512]{2,1,0:T(8,128)S(1)} %get-tuple-element.83), channel_id=1, source_target_pairs={{0,64},{1,65},{2,66},{3,67},{4,68},{5,69},{6,70},{7,71},{8,72},{9,... | collective-permute-start | bytes 1081352 | tf_op jit(solution)/shard_map/ppermute | solution.py:430
  26.3 9.6 %collective-permute-start.4 = (f32[8,16,512]{2,1,0:T(8,128)S(1)}, f32[8,16,512]{2,1,0:T(8,128)S(1)}, u32[]{:S(2)}, u32[]{:S(2)}) collective-permute-start(f32[8,16,512]{2,1,0:T(8,128)S(1)} %get-tuple-element.88), channel_id=1, source_target_pairs={{0,64},{1,65},{2,66},{3,67},{4,68},{5,69},{6,70},{7,71},{8,72},{9,... | collective-permute-start | bytes 786440 | tf_op jit(solution)/shard_map/ppermute | solution.py:430
  36.0 14.3 %collective-permute-start.7 = (f32[8,16,512]{2,1,0:T(8,128)S(1)}, f32[8,16,512]{2,1,0:T(8,128)S(1)}, u32[]{:S(2)}, u32[]{:S(2)}) collective-permute-start(f32[8,16,512]{2,1,0:T(8,128)S(1)} %get-tuple-element.90.m0), channel_id=1, source_target_pairs={{0,64},{1,65},{2,66},{3,67},{4,68},{5,69},{6,70},{7,71},{8,72},{9,... | collective-permute-start | bytes 786440 | tf_op jit(solution)/shard_map/ppermute | solution.py:430
  40.9 9.4 %collective-permute-start.6 = (f32[2,16,512]{2,1,0:T(8,128)S(1)}, f32[2,16,512]{2,1,0:T(8,128)S(1)}, u32[]{:S(2)}, u32[]{:S(2)}) collective-permute-start(f32[2,16,512]{2,1,0:T(8,128)S(1)} %get-tuple-element.97), channel_id=1, source_target_pairs={{1,32},{2,33},{3,34},{4,35},{5,36},{6,37},{7,38},{8,39},{9,40},{10... | collective-permute-start | bytes 196616 | tf_op jit(solution)/shard_map/ppermute | solution.py:430
  48.4 13.2 %collective-permute-start.5 = (f32[10,16,512]{2,1,0:T(8,128)S(1)}, f32[10,16,512]{2,1,0:T(8,128)S(1)}, u32[]{:S(2)}, u32[]{:S(2)}) collective-permute-start(f32[10,16,512]{2,1,0:T(8,128)S(1)} %get-tuple-element.92), channel_id=1, source_target_pairs={{0,64},{1,65},{2,66},{3,67},{4,68},{5,69},{6,70},{7,71},{8,72},{9,... | collective-permute-start | bytes 983048 | tf_op jit(solution)/shard_map/ppermute | solution.py:430
  50.5 15.1 %collective-permute-start.8 = (f32[9,16,512]{2,1,0:T(8,128)S(1)}, f32[9,16,512]{2,1,0:T(8,128)S(1)}, u32[]{:S(2)}, u32[]{:S(2)}) collective-permute-start(f32[9,16,512]{2,1,0:T(8,128)S(1)} %get-tuple-element.100), channel_id=1, source_target_pairs={{0,64},{1,65},{2,66},{3,67},{4,68},{5,69},{6,70},{7,71},{8,72},{9,... | collective-permute-start | bytes 884744 | tf_op jit(solution)/shard_map/ppermute | solution.py:430
  58.9 2.8 %copy-start.2 = (f32[16,16,512]{2,1,0:T(8,128)S(1)}, f32[16,16,512]{2,1,0:T(8,128)}, u32[]{:S(2)}) copy-start(f32[16,16,512]{2,1,0:T(8,128)} %k_residual_out.1._) | copy-start | bytes 1572868
  73.0 18.8 %collective-permute-start.10 = (f32[8,16,512]{2,1,0:T(8,128)S(1)}, f32[8,16,512]{2,1,0:T(8,128)S(1)}, u32[]{:S(2)}, u32[]{:S(2)}) collective-permute-start(f32[8,16,512]{2,1,0:T(8,128)S(1)} %get-tuple-element.103.t0), channel_id=1, source_target_pairs={{0,128},{1,129},{2,130},{3,131},{4,132},{5,133},{6,134},{7,135},{8... | collective-permute-start | bytes 786440 | tf_op jit(solution)/shard_map/ppermute | solution.py:430
  80.2 6.1 %collective-permute-start.9 = (f32[1,16,512]{2,1,0:T(8,128)S(1)}, f32[1,16,512]{2,1,0:T(8,128)S(1)}, u32[]{:S(2)}, u32[]{:S(2)}) collective-permute-start(f32[1,16,512]{2,1,0:T(8,128)S(1)} %get-tuple-element.104), channel_id=1, source_target_pairs={{1,32},{2,33},{3,34},{4,35},{5,36},{6,37},{7,38},{8,39},{9,40},{10... | collective-permute-start | bytes 98312 | tf_op jit(solution)/shard_map/ppermute | solution.py:430
  86.3 8.1 %copy-start.1 = (f32[1,1,16,16,512]{4,3,2,1,0:T(8,128)S(1)}, f32[1,1,16,16,512]{4,3,2,1,0:T(8,128)}, u32[]{:S(2)}) copy-start(f32[1,1,16,16,512]{4,3,2,1,0:T(8,128)} %param.3) | copy-start | bytes 1572868
  91.9 3.6 %collective-permute-start.11 = (f32[8,16,512]{2,1,0:T(8,128)S(1)}, f32[8,16,512]{2,1,0:T(8,128)S(1)}, u32[]{:S(2)}, u32[]{:S(2)}) collective-permute-start(f32[8,16,512]{2,1,0:T(8,128)S(1)} %get-tuple-element.108), channel_id=1, source_target_pairs={{0,32},{1,33},{2,34},{3,35},{4,36},{5,37},{6,38},{7,39},{8,40},{9,... | collective-permute-start | bytes 786440 | tf_op jit(solution)/shard_map/ppermute | solution.py:430

commit v4 on v3

--- a/solution.py
+++ b/solution.py
@@ -93,9 +93,9 @@
 
 def k_load_u(u, uo, send):
     def fill(x, row):
-        if row <= 8:
+        if row <= 10:
             uo[row] = u[:, x, :]
-        if row >= 7:
+        if row >= 5:
             send[15 - row] = u[:, x, :]
 
     each_row(fill)
@@ -103,17 +103,17 @@
 
 def k_load_f(f, send0, fo, send):
     def fill(x, row):
-        if row <= 7:
+        if row <= 9:
             fo[row] = f[:, x, :]
-        else:
-            send[24 - row] = f[:, x, :]
+        if row >= 6:
+            send[26 - row] = f[:, x, :]
 
     each_row(fill)
 
 
 def k_load_k(kap, ko):
     def fill(x, row):
-        if row <= 8:
+        if row <= 10:
             ko[row] = kap[:, x, :]
 
     each_row(fill)
@@ -121,12 +121,12 @@
 
 def k_pack(uo, fo, ko, got, u, f, edge, zu):
     h = own_core()
-    for x in range(9):
+    for x in range(11):
         u[h, x] = uo[x]
         u[1 - h, x] = got[x]
-    for x in range(8):
+    for x in range(10):
         f[h, x] = fo[x]
-        f[1 - h, x] = got[9 + x]
+        f[1 - h, x] = got[11 + x]
         zu[x] = u[1, x]
     for x in range(3):
         edge[x] = u[0, x]
@@ -138,14 +138,15 @@
 
 
 def k_inner(u, f, ko, w, wx, diag, gain, b, e0, cm, c):
-    for x in range(9):
+    for x in range(11):
         for t in range(2):
             v = u[t, x]
             c[t, x] = ko[x] * (1.0 + v * v)
-        cm[x + 3] = 0.5 * (c[0, x] + c[1, x])
+        if x < 9:
+            cm[x + 3] = 0.5 * (c[0, x] + c[1, x])
     for t in range(2):
         wx[t, 3] = (0.5 * tau) * (c[t, 0] + c[t, 1])
-        for x in range(1, 8):
+        for x in range(1, 10):
             i = x + 2
             weights, w_high, d = faces(c[t, x], c[t, x - 1], c[t, x + 1], tau)
             wx[t, i + 1] = w_high
@@ -198,22 +199,17 @@
                 value = jnp.where(real, value, 0.0)
             b[t, i] = value
             e0[t, i] = g * value
-    for i in range(9):
+    for i in range(10):
         zpay[i] = e0[1, i + 1]
-    zpay[9] = edge[3]
-    zpay[10] = edge[4]
-
-
-def k_prev(zu, gain, b0, e00, b, e0, ipay):
-    h = own_core()
-    for x in range(8):
+    zpay[10] = edge[3]
+    zpay[11] = edge[4]
+
+
+def k_prev(zu, gain, b0, e00, b, e0):
+    for x in range(10):
         value = b0[0, x + 2] + zu[x]
         b[0, x + 2] = value
         e0[0, x + 2] = gain[0, x + 2] * value
-    ipay[0] = e0[0, 9]
-    ipay[1] = e0[1, 9]
-    for x in range(8):
-        ipay[2 + x] = b[1 - h, x + 2]
 
 
 def smoothed(here, low, high, w, wx, gain, t, i, right):
@@ -222,34 +218,30 @@
     return keep * here + gain[t, i] * (right + flux)
 
 
-def k_fine(w, wx, gain, b, e0, near, e1, zpay):
-    h = own_core()
+def k_fine(w, wx, gain, b, e0, e1, zpay):
     for t in (1, 0):
-        for x in range(1 - t, 8):
+        for x in range(1 - t, 9):
             i = x + 2
-            high = e0[t, i + 1] if x < 7 else near[1 - h, t]
             right = b[t, i] + e0[0, i] if t == 1 else b[t, i]
-            value = smoothed(e0[t, i], e0[t, i - 1], high, w, wx, gain, t, i, right)
+            value = smoothed(e0[t, i], e0[t, i - 1], e0[t, i + 1], w, wx, gain, t, i, right)
             e1[t, i - 1] = value
-            if t == 1:
+            if t == 1 and x < 8:
                 zpay[x] = value
 
 
-def k_fine_prev(w, wx, gain, b, e0, z, e10, e1, ipay):
+def k_fine_prev(w, wx, gain, b, e0, z, e10, e1):
     real = has_outer()
-    for x in range(1, 8):
+    for x in range(1, 9):
         i = x + 2
         e1[0, i - 1] = e10[0, i - 1] + gain[0, i] * z[i - 1]
     far, edge = [
-        e0[0, i] + jnp.where(real, gain[0, i] * z[10 - i], 0.0) for i in range(2)
+        e0[0, i] + jnp.where(real, gain[0, i] * z[11 - i], 0.0) for i in range(2)
     ]
     e1[0, 1] = smoothed(e0[0, 2], edge, e0[0, 3], w, wx, gain, 0, 2, b[0, 2] + z[1])
-    value = smoothed(edge, far, e0[0, 2], w, wx, gain, 0, 1, b[0, 1] + z[0] + z[9])
+    value = smoothed(edge, far, e0[0, 2], w, wx, gain, 0, 1, b[0, 1] + z[0] + z[10])
     e1[0, 0] = jnp.where(real, value, 0.0)
     value = smoothed(e0[1, 1], e0[1, 0], e0[1, 2], w, wx, gain, 1, 1, b[1, 1] + edge)
     e1[1, 0] = jnp.where(real, value, 0.0)
-    ipay[0] = e1[0, 8]
-    ipay[1] = e10[1, 8]
 
 
 def k_mid_faces(cm, w, wx, diag, gain):
@@ -263,25 +255,27 @@
         gain[i] = omega / d
 
 
-def k_restrict(w, wx, diag, b, e1, near, part):
-    h = own_core()
+def k_restrict(w, wx, diag, b, e1, cm, part, cpay):
     for x in range(8):
         i = x + 2
         value = e1[0, x + 1]
         for t in range(2):
             here = e1[t, x + 1]
-            high = e1[t, x + 2] if x < 7 else near[1 - h, t]
             weights = [w[k, t, i] for k in range(4)]
-            flux = spread(here, e1[t, x], high, weights, wx[t, i], wx[t, i + 1])
+            flux = spread(here, e1[t, x], e1[t, x + 2], weights, wx[t, i], wx[t, i + 1])
             value = value + (b[t, i] - diag[t, i] * here + flux)
         part[x] = value
-
-
-def k_restrict_prev(part, z, gain, bm, m0, edge, ipay):
+    for x in range(10):
+        cpay[x] = cm[x + 2]
+
+
+def k_restrict_prev(part, z, gain, b, bm, m0, edge, ipay):
+    h = own_core()
     for x in range(8):
         value = part[x] + z[x]
         bm[x] = value
         m0[x] = gain[x + 2] * value
+        ipay[1 + x] = b[1 - h, x + 2]
     edge[0] = bm[0]
     edge[1] = bm[1]
     ipay[0] = m0[7]
@@ -293,10 +287,8 @@
     return keep * here + gain[i] * (right + flux)
 
 
-def k_mid(w, wx, gain, bm, m0, near, cm, m1, cpay):
-    h = own_core()
-    for x in range(10):
-        cpay[x] = cm[x + 2]
+def k_mid(w, wx, gain, bm, m0, near, _, m1):
+    h = own_core()
     for x in range(1, 8):
         high = m0[x + 1] if x < 7 else near[1 - h, 0]
         m1[x + 1] = smoothed_mid(m0[x], m0[x - 1], high, w, wx, gain, x + 2, bm[x])
@@ -339,9 +331,7 @@
         rm[x] = rm0[x] + z[x]
 
 
-def k_top_faces(cm, twin, _, w, wx, gain, ct):
-    for i in range(10):
-        ct[i] = 0.5 * (cm[i + 2] + twin[i])
+def k_top_faces(ct, w, wx, gain):
     wx[0] = (2 * tau) * (ct[0] + ct[1])
     for x in range(8):
         weights, w_high, d = faces(ct[x + 1], ct[x], ct[x + 2], 4 * tau)
@@ -380,40 +370,44 @@
     other[0] = e1[1 - h, 1] + value
 
 
-def k_residual_out(b, near, out):
-    h = own_core()
+def k_residual_out(b, near, cm, twin, out, ct):
+    h = own_core()
+    for i in range(10):
+        ct[i] = 0.5 * (cm[i + 2] + twin[i])
 
     def rows(mirror):
         for x in range(16):
             row = 15 - x if mirror else x
-            out[:, x, :] = b[h, row + 2] if row < 8 else near[1 - h, 2 + 15 - row]
+            out[:, x, :] = b[h, row + 2] if row < 8 else near[1 - h, 16 - row]
 
     pl.when(h == 0)(lambda: rows(False))
     pl.when(h == 1)(lambda: rows(True))
 
 
-def store_half(u, add, out, buf, sems, start, row_of):
-    copies = []
-    for j in range(2):
-        part = pl.ds(8 * j, 8)
-        for x in range(8):
-            buf[part, x, :] = u[part, start + x, :] + add[row_of(x), part, :]
-        copies.append(
-            pltpu.make_async_copy(buf.at[part], out.at[part, pl.ds(start, 8)], sems.at[j])
-        )
-        copies[-1].start()
-    for copy in copies:
-        copy.wait()
-
-
-def k_state_own(u, mine, out, buf, sems):
-    pl.when(own_core() == 0)(lambda: store_half(u, mine, out, buf, sems, 0, lambda x: x))
-    pl.when(own_core() == 1)(lambda: store_half(u, mine, out, buf, sems, 8, lambda x: 7 - x))
-
-
-def k_state_far(u, got, out0, out, buf, sems):
-    pl.when(own_core() == 0)(lambda: store_half(u, got, out, buf, sems, 8, lambda x: 7 - x))
-    pl.when(own_core() == 1)(lambda: store_half(u, got, out, buf, sems, 0, lambda x: x))
+def k_state(u, mine, got, out, buf, sems):
+    def store(mirror):
+        far = 0 if mirror else 8
+        copies = []
+        for start in (8 - far, far):
+            for j in range(2):
+                part = pl.ds(8 * j, 8)
+                for x in range(start, start + 8):
+                    row = 15 - x if mirror else x
+                    if row < 8:
+                        add = mine[row, part, :]
+                    else:
+                        add = got[1 - int(mirror), 15 - row, part, :]
+                    buf[part, x, :] = u[part, x, :] + add
+                where = (part, pl.ds(start, 8))
+                copies.append(
+                    pltpu.make_async_copy(buf.at[where], out.at[where], sems.at[len(copies)])
+                )
+                copies[-1].start()
+        for copy in copies:
+            copy.wait()
+
+    pl.when(own_core() == 0)(lambda: store(False))
+    pl.when(own_core() == 1)(lambda: store(True))
 
 
 VMEM = pl.BlockSpec(memory_space=pltpu.VMEM)
@@ -452,48 +446,42 @@
     def shards(iterate, source_term, conductivity):
         u_in = iterate[0, 0]
 
-        uo, pay = call(k_load_u, [(9,), (17,)], u_in)
-        fo, pay = call(k_load_f, [(8,), (17,)], source_term[0, 0], pay, alias=[(1, 1)])
-        (ko,) = call(k_load_k, [(9,)], conductivity[0])
+        uo, pay = call(k_load_u, [(11,), (21,)], u_in)
+        fo, pay = call(k_load_f, [(10,), (21,)], source_term[0, 0], pay, alias=[(1, 1)])
+        (ko,) = call(k_load_k, [(11,)], conductivity[0])
         got = send(pay, pair)
-        u, f, edge, zu = call(k_pack, [(2, 9), (2, 8), (13,), (8,)], uo, fo, ko, got)
+        u, f, edge, zu = call(k_pack, [(2, 11), (2, 10), (13,), (10,)], uo, fo, ko, got)
         edge = send(edge, outer)
         zu = send(zu, later)
-        fields = [(4, 2, 10), (2, 11), (2, 10), (2, 10), (2, 10), (2, 10), (12,)]
-        held = call(k_inner, fields, u, f, ko, scratch=[(2, 9)])
+        fields = [(4, 2, 12), (2, 13), (2, 12), (2, 12), (2, 12), (2, 12), (12,)]
+        held = call(k_inner, fields, u, f, ko, scratch=[(2, 11)])
         w, wx, diag, gain, b, e0, cm, zpay = call(
-            k_edge, fields + [(11,)], u, f, ko, edge, *held,
+            k_edge, fields + [(12,)], u, f, ko, edge, *held,
             scratch=[(2, 5)], alias=[(4 + i, i) for i in range(7)],
         )
         z = send(zpay, later)
-        b, e0, ipay = call(
-            k_prev, [(2, 10), (2, 10), (10,)], zu, gain, b, e0, alias=[(2, 0), (3, 1)]
-        )
-        near_b = gather(ipay, in_chip)
-        e1, zpay = call(k_fine, [(2, 9), (8,)], w, wx, gain, b, e0, near_b)
+        b, e0 = call(k_prev, [(2, 12), (2, 12)], zu, gain, b, e0, alias=[(2, 0), (3, 1)])
+        e1, zpay = call(k_fine, [(2, 10), (8,)], w, wx, gain, b, e0)
         z1 = send(zpay, later)
-        e1, ipay = call(
-            k_fine_prev, [(2, 9), (2,)], w, wx, gain, b, e0, z, e1, alias=[(6, 0)]
-        )
-        near = gather(ipay, in_chip)
-        (residual,) = call(k_residual_out, [(16,)], b, near_b)
-        (part,) = call(k_restrict, [(8,)], w, wx, diag, b, e1, near)
+        (e1,) = call(k_fine_prev, [(2, 10)], w, wx, gain, b, e0, z, e1, alias=[(6, 0)])
+        part, pay = call(k_restrict, [(8,), (10,)], w, wx, diag, b, e1, cm)
+        cm_twin = send(pay, twin)
         wm, wxm, diagm, gainm = call(k_mid_faces, [(4, 10), (11,), (10,), (10,)], cm)
         bm, m0, pay, ipay = call(
-            k_restrict_prev, [(8,), (8,), (2,), (1,)], part, z1, gainm
+            k_restrict_prev, [(8,), (8,), (2,), (9,)], part, z1, gainm, b
         )
         z = send(m0, later)
         edge = send(pay, outer)
         near = gather(ipay, in_chip)
-        m1, pay = call(k_mid, [(9,), (10,)], wm, wxm, gainm, bm, m0, near, cm)
-        cm_twin = send(pay, twin)
+        residual, ct = call(k_residual_out, [(16,), (10,)], b, near, cm, cm_twin)
+        (m1,) = call(k_mid, [(9,)], wm, wxm, gainm, bm, m0, near, cm_twin, far=(6,))
         m1, zpay, ipay = call(
             k_mid_prev, [(9,), (9,), (1,)], wm, wxm, gainm, bm, m0, edge, z, m1,
             alias=[(7, 0)],
         )
         z = send(zpay, later)
         near = gather(ipay, in_chip)
-        wt, wxt, gaint = call(k_top_faces, [(4, 8), (9,), (8,)], cm, cm_twin, residual, scratch=[(10,)], far=(2,))
+        wt, wxt, gaint = call(k_top_faces, [(4, 8), (9,), (8,)], ct)
         (rm,) = call(k_mid_left, [(8,)], wm, wxm, diagm, bm, m1, near)
         (rm,) = call(
             k_mid_left_prev, [(8,)], wm, wxm, diagm, gainm, bm, m1, z, rm, alias=[(7, 0)]
@@ -510,24 +498,19 @@
             k_top_prev, [(8,), (8,)], wt, wxt, gaint, bt, t0, edge, z, m1, e1, mine, other,
             alias=[(9, 0), (10, 1)],
         )
-        got = send(other, pair)
-        half = pltpu.VMEM((16, 8, 512), jnp.float32)
-        own_spec = dict(
+        got = gather(other, in_chip)
+        new = pl.pallas_call(
+            k_state,
             out_shape=jax.ShapeDtypeStruct((16, 16, 512), jnp.float32),
+            in_specs=[VMEM, VMEM, VMEM],
             out_specs=HBM,
-            scratch_shapes=[half, pltpu.SemaphoreType.DMA((2,))],
+            scratch_shapes=[
+                pltpu.VMEM((16, 16, 512), jnp.float32),
+                pltpu.SemaphoreType.DMA((4,)),
+            ],
             compiler_params=pltpu.CompilerParams(vmem_limit_bytes=24 * 2**20),
-        )
-        new = pl.pallas_call(
-            k_state_own, in_specs=[VMEM, VMEM], name="k_state_own", **own_spec
-        )(u_in, mine)
-        new = pl.pallas_call(
-            k_state_far,
-            in_specs=[VMEM, VMEM, HBM],
-            input_output_aliases={2: 0},
-            name="k_state_far",
-            **own_spec,
-        )(u_in, got, new)
+            name="k_state",
+        )(u_in, mine, got)
         return new[None, None], residual[None, None]
 
     spec = P("tm", "space", None, None, None)

time: 96.9 us -> 90.2 us (0.931)
  the two profiles are of different devices: /device:TPU:71 before, /device:TPU:189 now
where the time goes in v4:
time: 90.2 us; the launch traced here: 89.6 us
  starting transfers between devices  43.1 us (48%)
  blocking collectives  21.7 us (24%)
  waiting for transfers between devices  13.8 us (15%)
  Pallas kernels  7.05 us (8%)
  local copies, waits for them, and re-layouts  3.11 us (3%)
    ppermute x11, starting transfers between devices, send(): return lax.ppermute(x, axes, route)  43.1 us
    all_gather x5, blocking collectives, gather(): return lax.all_gather(x, axes, axis_index_groups=groups)  21.7 us
    ppermute x11, waiting for transfers between devices, send(): return lax.ppermute(x, axes, route)  13.8 us
    pallas_call x21, Pallas kernels, call(): pl.pallas_call(kernel, out_shape=[jax.ShapeDtypeStruct(s + (16, 512), jnp...  6.15 us
    unnamed x8, local copies, waits for them, and re-layouts  3.11 us
  transfers between devices with their start and end apart: 11, of which 6 were waited for; matrix products, arithmetic and copies ran while one was open for 0% of the time, Pallas kernels for 6%

profile of v4, /device:TPU:189, one launch (start us, length us, event | category | flops | bytes accessed | tf_op | source)
XLA Modules:
  0.0 89.6 jit_solution(16168071906789083773)
XLA Ops:
  0.6 1.0 %copy-done = f32[1,1,16,16,512]{4,3,2,1,0:T(8,128)S(1)} copy-done((f32[1,1,16,16,512]{4,3,2,1,0:T(8,128)S(1)}, f32[1,1,16,16,512]{4,3,2,1,0:T(8,128)}, u32[]{:S(2)}) %copy-start) | copy-done | bytes 524312
  1.7 0.1 k_load_u.1
  1.8 0.0 copy-start.2
  1.8 1.0 %copy-done.2 = f32[1,1,16,16,512]{4,3,2,1,0:T(8,128)S(1)} copy-done((f32[1,1,16,16,512]{4,3,2,1,0:T(8,128)S(1)}, f32[1,1,16,16,512]{4,3,2,1,0:T(8,128)}, u32[]{:S(2)}) %copy-start.2) | copy-done | bytes 524312
  2.8 0.1 k_load_f.1
  2.9 2.6 %collective-permute-start = (f32[21,16,512]{2,1,0:T(8,128)S(1)}, f32[21,16,512]{2,1,0:T(8,128)S(1)}, u32[]{:S(2)}, u32[]{:S(2)}) collective-permute-start(f32[21,16,512]{2,1,0:T(8,128)S(1)} %get-tuple-element.58), channel_id=1, source_target_pairs={{0,32},{1,33},{2,34},{3,35},{4,36},{5,37},{6,38},{7,39},{8,40},{9,... | collective-permute-start | bytes 2064392 | tf_op jit(solution)/shard_map/ppermute | solution.py:424
  5.5 0.0 copy-start.3
  5.5 1.0 %copy-done.3 = f32[1,16,16,512]{3,2,1,0:T(8,128)S(1)} copy-done((f32[1,16,16,512]{3,2,1,0:T(8,128)S(1)}, f32[1,16,16,512]{3,2,1,0:T(8,128)}, u32[]{:S(2)}) %copy-start.3) | copy-done | bytes 524312
  6.6 0.1 k_load_k.1.ko
  6.7 0.6 collective-permute-done.got
  7.3 0.2 k_pack.1
  7.4 2.3 %collective-permute-start.2 = (f32[13,16,512]{2,1,0:T(8,128)S(1)}, f32[13,16,512]{2,1,0:T(8,128)S(1)}, u32[]{:S(2)}, u32[]{:S(2)}) collective-permute-start(f32[13,16,512]{2,1,0:T(8,128)S(1)} %get-tuple-element.62), channel_id=1, source_target_pairs={{1,32},{2,33},{3,34},{4,35},{5,36},{6,37},{7,38},{8,39},{9,40},{10... | collective-permute-start | bytes 1277960 | tf_op jit(solution)/shard_map/ppermute | solution.py:424
  9.7 4.0 %collective-permute-start.1 = (f32[10,16,512]{2,1,0:T(8,128)S(1)}, f32[10,16,512]{2,1,0:T(8,128)S(1)}, u32[]{:S(2)}, u32[]{:S(2)}) collective-permute-start(f32[10,16,512]{2,1,0:T(8,128)S(1)} %get-tuple-element.59), channel_id=1, source_target_pairs={{0,64},{1,65},{2,66},{3,67},{4,68},{5,69},{6,70},{7,71},{8,72},{9,... | collective-permute-start | bytes 983048 | tf_op jit(solution)/shard_map/ppermute | solution.py:424
  13.7 1.2 %k_inner.1 = (f32[4,2,12,16,512]{4,3,2,1,0:T(8,128)S(1)}, f32[2,13,16,512]{3,2,1,0:T(8,128)S(1)}, f32[2,12,16,512]{3,2,1,0:T(8,128)S(1)}, f32[2,12,16,512]{3,2,1...) custom-call(f32[2,11,16,512]{3,2,1,0:T(8,128)S(1)} %get-tuple-element.60, ...), custom_call_target="tpu_custom_call" | custom-call | flops 2621440 | bytes 1736704 | tf_op jit(solution)/shard_map/k_inner/pallas_call | solution.py:434
  15.0 4.0 %collective-permute-done.2.edge = f32[13,16,512]{2,1,0:T(8,128)S(1)} collective-permute-done((f32[13,16,512]{2,1,0:T(8,128)S(1)}, f32[13,16,512]{2,1,0:T(8,128)S(1)}, u32[]{:S(2)}, u32[]{:S(2)}) %collective-permute-start.2) | collective-permute-done | bytes 426016 | tf_op jit(solution)/shard_map/ppermute | solution.py:424
  19.0 0.5 k_edge.1
  19.4 4.0 %collective-permute-start.3 = (f32[12,16,512]{2,1,0:T(8,128)S(1)}, f32[12,16,512]{2,1,0:T(8,128)S(1)}, u32[]{:S(2)}, u32[]{:S(2)}) collective-permute-start(f32[12,16,512]{2,1,0:T(8,128)S(1)} %get-tuple-element.78), channel_id=1, source_target_pairs={{0,64},{1,65},{2,66},{3,67},{4,68},{5,69},{6,70},{7,71},{8,72},{9,... | collective-permute-start | bytes 1179656 | tf_op jit(solution)/shard_map/ppermute | solution.py:424
  23.5 0.1 k_prev.1
  23.6 0.5 k_fine.1
  24.1 5.2 %collective-permute-start.4 = (f32[8,16,512]{2,1,0:T(8,128)S(1)}, f32[8,16,512]{2,1,0:T(8,128)S(1)}, u32[]{:S(2)}, u32[]{:S(2)}) collective-permute-start(f32[8,16,512]{2,1,0:T(8,128)S(1)} %get-tuple-element.82), channel_id=1, source_target_pairs={{0,64},{1,65},{2,66},{3,67},{4,68},{5,69},{6,70},{7,71},{8,72},{9,... | collective-permute-start | bytes 786440 | tf_op jit(solution)/shard_map/ppermute | solution.py:424
  29.3 3.2 %collective-permute-done.3.z = f32[12,16,512]{2,1,0:T(8,128)S(1)} collective-permute-done((f32[12,16,512]{2,1,0:T(8,128)S(1)}, f32[12,16,512]{2,1,0:T(8,128)S(1)}, u32[]{:S(2)}, u32[]{:S(2)}) %collective-permute-start.3) | collective-permute-done | bytes 393248 | tf_op jit(solution)/shard_map/ppermute | solution.py:424
  32.5 0.2 k_fine_prev.1.e1
  32.7 0.5 k_restrict.1
  33.2 5.1 %collective-permute-start.5 = (f32[10,16,512]{2,1,0:T(8,128)S(1)}, f32[10,16,512]{2,1,0:T(8,128)S(1)}, u32[]{:S(2)}, u32[]{:S(2)}) collective-permute-start(f32[10,16,512]{2,1,0:T(8,128)S(1)} %get-tuple-element.85), channel_id=1, source_target_pairs={{0,64},{1,65},{2,66},{3,67},{4,68},{5,69},{6,70},{7,71},{8,72},{9,... | collective-permute-start | bytes 983048 | tf_op jit(solution)/shard_map/ppermute | solution.py:424
  38.3 0.4 k_mid_faces.1
  38.7 0.1 k_restrict_prev.1
  38.8 3.2 %collective-permute-start.7 = (f32[8,16,512]{2,1,0:T(8,128)S(1)}, f32[8,16,512]{2,1,0:T(8,128)S(1)}, u32[]{:S(2)}, u32[]{:S(2)}) collective-permute-start(f32[8,16,512]{2,1,0:T(8,128)S(1)} %get-tuple-element.94.m0), channel_id=1, source_target_pairs={{0,64},{1,65},{2,66},{3,67},{4,68},{5,69},{6,70},{7,71},{8,72},{9,... | collective-permute-start | bytes 786440 | tf_op jit(solution)/shard_map/ppermute | solution.py:424
  42.0 2.8 %collective-permute-start.6 = (f32[2,16,512]{2,1,0:T(8,128)S(1)}, f32[2,16,512]{2,1,0:T(8,128)S(1)}, u32[]{:S(2)}, u32[]{:S(2)}) collective-permute-start(f32[2,16,512]{2,1,0:T(8,128)S(1)} %get-tuple-element.95), channel_id=1, source_target_pairs={{1,32},{2,33},{3,34},{4,35},{5,36},{6,37},{7,38},{8,39},{9,40},{10... | collective-permute-start | bytes 196616 | tf_op jit(solution)/shard_map/ppermute | solution.py:424
  44.8 2.2 %all-gather = f32[18,16,512]{2,1,0:T(8,128)S(1)} all-gather(f32[9,16,512]{2,1,0:T(8,128)S(1)} %get-tuple-element.84), channel_id=2, replica_groups={{0,32},{1,33},{2,34},{3,35},{4,36},{5,37},{6,38},{7,39},{8,40},{9,41},{..., dimensions={0}, use_global_device_ids=true | all-gather | bytes 884736 | tf_op jit(solution)/shard_map/all_gather | solution.py:427
  47.1 0.2 k_mid.1.m10
  47.3 2.4 %collective-permute-done.6.edge = f32[2,16,512]{2,1,0:T(8,128)S(1)} collective-permute-done((f32[2,16,512]{2,1,0:T(8,128)S(1)}, f32[2,16,512]{2,1,0:T(8,128)S(1)}, u32[]{:S(2)}, u32[]{:S(2)}) %collective-permute-start.6) | collective-permute-done | bytes 65568 | tf_op jit(solution)/shard_map/ppermute | solution.py:424
  49.7 0.1 k_mid_prev.1
  49.8 5.0 %collective-permute-start.8 = (f32[9,16,512]{2,1,0:T(8,128)S(1)}, f32[9,16,512]{2,1,0:T(8,128)S(1)}, u32[]{:S(2)}, u32[]{:S(2)}) collective-permute-start(f32[9,16,512]{2,1,0:T(8,128)S(1)} %get-tuple-element.97), channel_id=1, source_target_pairs={{0,64},{1,65},{2,66},{3,67},{4,68},{5,69},{6,70},{7,71},{8,72},{9,... | collective-permute-start | bytes 884744 | tf_op jit(solution)/shard_map/ppermute | solution.py:424
  54.9 1.0 %k_residual_out.1 = (f32[16,16,512]{2,1,0:T(8,128)}, f32[10,16,512]{2,1,0:T(8,128)S(1)}) custom-call(f32[2,12,16,512]{3,2,1,0:T(8,128)S(1)} %get-tuple-element.73.b, f32[2,9,16,512]{3,2,1,0:T(8,128)S(1)} %bitcast.11, f32[12,16,512]{2,1,0:T(8,128)S(1)} %get-tuple-element.80.cm, f32[10,16,512]{2,1,0:T(8,128)S(1)} %collective-permute-done.5.twin._), custom_call_target="tpu_custom_call" | custom-call | flops 2621440 | bytes 2097152 | tf_op jit(solution)/shard_map/k_residual_out/pallas_call | solution.py:434
  55.8 0.3 k_top_faces.1
  56.1 1.9 %all-gather.1 = f32[2,16,512]{2,1,0:T(8,128)S(1)} all-gather(f32[1,16,512]{2,1,0:T(8,128)S(1)} %get-tuple-element.98), channel_id=3, replica_groups={{0,32},{1,33},{2,34},{3,35},{4,36},{5,37},{6,38},{7,39},{8,40},{9,41},{..., dimensions={0}, use_global_device_ids=true | all-gather | bytes 98304 | tf_op jit(solution)/shard_map/all_gather | solution.py:427
  58.0 0.2 k_mid_left.1.rm0
  58.2 2.4 %collective-permute-done.8.z = f32[9,16,512]{2,1,0:T(8,128)S(1)} collective-permute-done((f32[9,16,512]{2,1,0:T(8,128)S(1)}, f32[9,16,512]{2,1,0:T(8,128)S(1)}, u32[]{:S(2)}, u32[]{:S(2)}) %collective-permute-start.8) | collective-permute-done | bytes 294944 | tf_op jit(solution)/shard_map/ppermute | solution.py:424
  60.6 0.1 k_mid_left_prev.1
  60.7 8.2 %all-gather.2 = f32[16,16,512]{2,1,0:T(8,128)S(1)} all-gather(f32[8,16,512]{2,1,0:T(8,128)S(1)} %k_mid_left_prev.1), channel_id=4, replica_groups={{0,64},{1,65},{2,66},{3,67},{4,68},{5,69},{6,70},{7,71},{8,72},{9,73},{..., dimensions={0}, use_global_device_ids=true | all-gather | bytes 786432 | tf_op jit(solution)/shard_map/all_gather | solution.py:427
  68.9 5.8 %collective-permute-start.10 = (f32[8,16,512]{2,1,0:T(8,128)S(1)}, f32[8,16,512]{2,1,0:T(8,128)S(1)}, u32[]{:S(2)}, u32[]{:S(2)}) collective-permute-start(f32[8,16,512]{2,1,0:T(8,128)S(1)} %get-tuple-element.100.t0), channel_id=1, source_target_pairs={{0,128},{1,129},{2,130},{3,131},{4,132},{5,133},{6,134},{7,135},{8... | collective-permute-start | bytes 786440 | tf_op jit(solution)/shard_map/ppermute | solution.py:424
  74.8 3.0 %collective-permute-start.9 = (f32[1,16,512]{2,1,0:T(8,128)S(1)}, f32[1,16,512]{2,1,0:T(8,128)S(1)}, u32[]{:S(2)}, u32[]{:S(2)}) collective-permute-start(f32[1,16,512]{2,1,0:T(8,128)S(1)} %get-tuple-element.101), channel_id=1, source_target_pairs={{1,32},{2,33},{3,34},{4,35},{5,36},{6,37},{7,38},{8,39},{9,40},{10... | collective-permute-start | bytes 98312 | tf_op jit(solution)/shard_map/ppermute | solution.py:424
  77.7 2.9 %all-gather.3 = f32[2,16,512]{2,1,0:T(8,128)S(1)} all-gather(f32[1,16,512]{2,1,0:T(8,128)S(1)} %get-tuple-element.102), channel_id=5, replica_groups={{0,32},{1,33},{2,34},{3,35},{4,36},{5,37},{6,38},{7,39},{8,40},{9,41},{..., dimensions={0}, use_global_device_ids=true | all-gather | bytes 98304 | tf_op jit(solution)/shard_map/all_gather | solution.py:427
  80.6 0.3 k_top.1
  80.9 1.2 %collective-permute-done.9.edge = f32[1,16,512]{2,1,0:T(8,128)S(1)} collective-permute-done((f32[1,16,512]{2,1,0:T(8,128)S(1)}, f32[1,16,512]{2,1,0:T(8,128)S(1)}, u32[]{:S(2)}, u32[]{:S(2)}) %collective-permute-start.9) | collective-permute-done | bytes 32800 | tf_op jit(solution)/shard_map/ppermute | solution.py:424
  82.1 0.1 k_top_prev.1
  82.2 6.5 %all-gather.4 = f32[16,16,512]{2,1,0:T(8,128)S(1)} all-gather(f32[8,16,512]{2,1,0:T(8,128)S(1)} %get-tuple-element.106), channel_id=6, replica_groups={{0,32},{1,33},{2,34},{3,35},{4,36},{5,37},{6,38},{7,39},{8,40},{9,41},{..., dimensions={0}, use_global_device_ids=true | all-gather | bytes 786432 | tf_op jit(solution)/shard_map/all_gather | solution.py:427
  88.8 0.9 %k_state.1 = f32[16,16,512]{2,1,0:T(8,128)} custom-call(f32[16,16,512]{2,1,0:T(8,128)S(1)} %bitcast.13, f32[8,16,512]{2,1,0:T(8,128)S(1)} %get-tuple-element.105.mine, f32[2,8,16,512]{3,2,1,0:T(8,128)S(1)} %bitcast.14), custom_call_target="tpu_custom_call" | custom-call | tf_op jit(solution)/shard_map/k_state/pallas_call | solution.py:502
  (9 shorter events, 0.1 us)
Async XLA Ops:
  0.6 1.0 %copy-start = (f32[1,1,16,16,512]{4,3,2,1,0:T(8,128)S(1)}, f32[1,1,16,16,512]{4,3,2,1,0:T(8,128)}, u32[]{:S(2)}) copy-start(f32[1,1,16,16,512]{4,3,2,1,0:T(8,128)} %param.3) | copy-start | bytes 1572868
  1.8 1.0 %copy-start.2 = (f32[1,1,16,16,512]{4,3,2,1,0:T(8,128)S(1)}, f32[1,1,16,16,512]{4,3,2,1,0:T(8,128)}, u32[]{:S(2)}) copy-start(f32[1,1,16,16,512]{4,3,2,1,0:T(8,128)} %param.4) | copy-start | bytes 1572868
  2.9 4.3 %collective-permute-start = (f32[21,16,512]{2,1,0:T(8,128)S(1)}, f32[21,16,512]{2,1,0:T(8,128)S(1)}, u32[]{:S(2)}, u32[]{:S(2)}) collective-permute-start(f32[21,16,512]{2,1,0:T(8,128)S(1)} %get-tuple-element.58), channel_id=1, source_target_pairs={{0,32},{1,33},{2,34},{3,35},{4,36},{5,37},{6,38},{7,39},{8,40},{9,... | collective-permute-start | bytes 2064392 | tf_op jit(solution)/shard_map/ppermute | solution.py:424
  5.5 1.0 %copy-start.3 = (f32[1,16,16,512]{3,2,1,0:T(8,128)S(1)}, f32[1,16,16,512]{3,2,1,0:T(8,128)}, u32[]{:S(2)}) copy-start(f32[1,16,16,512]{3,2,1,0:T(8,128)} %param.5) | copy-start | bytes 1572868
  7.4 11.6 %collective-permute-start.2 = (f32[13,16,512]{2,1,0:T(8,128)S(1)}, f32[13,16,512]{2,1,0:T(8,128)S(1)}, u32[]{:S(2)}, u32[]{:S(2)}) collective-permute-start(f32[13,16,512]{2,1,0:T(8,128)S(1)} %get-tuple-element.62), channel_id=1, source_target_pairs={{1,32},{2,33},{3,34},{4,35},{5,36},{6,37},{7,38},{8,39},{9,40},{10... | collective-permute-start | bytes 1277960 | tf_op jit(solution)/shard_map/ppermute | solution.py:424
  9.7 13.7 %collective-permute-start.1 = (f32[10,16,512]{2,1,0:T(8,128)S(1)}, f32[10,16,512]{2,1,0:T(8,128)S(1)}, u32[]{:S(2)}, u32[]{:S(2)}) collective-permute-start(f32[10,16,512]{2,1,0:T(8,128)S(1)} %get-tuple-element.59), channel_id=1, source_target_pairs={{0,64},{1,65},{2,66},{3,67},{4,68},{5,69},{6,70},{7,71},{8,72},{9,... | collective-permute-start | bytes 983048 | tf_op jit(solution)/shard_map/ppermute | solution.py:424
  19.4 13.1 %collective-permute-start.3 = (f32[12,16,512]{2,1,0:T(8,128)S(1)}, f32[12,16,512]{2,1,0:T(8,128)S(1)}, u32[]{:S(2)}, u32[]{:S(2)}) collective-permute-start(f32[12,16,512]{2,1,0:T(8,128)S(1)} %get-tuple-element.78), channel_id=1, source_target_pairs={{0,64},{1,65},{2,66},{3,67},{4,68},{5,69},{6,70},{7,71},{8,72},{9,... | collective-permute-start | bytes 1179656 | tf_op jit(solution)/shard_map/ppermute | solution.py:424
  24.1 14.6 %collective-permute-start.4 = (f32[8,16,512]{2,1,0:T(8,128)S(1)}, f32[8,16,512]{2,1,0:T(8,128)S(1)}, u32[]{:S(2)}, u32[]{:S(2)}) collective-permute-start(f32[8,16,512]{2,1,0:T(8,128)S(1)} %get-tuple-element.82), channel_id=1, source_target_pairs={{0,64},{1,65},{2,66},{3,67},{4,68},{5,69},{6,70},{7,71},{8,72},{9,... | collective-permute-start | bytes 786440 | tf_op jit(solution)/shard_map/ppermute | solution.py:424
  33.2 13.9 %collective-permute-start.5 = (f32[10,16,512]{2,1,0:T(8,128)S(1)}, f32[10,16,512]{2,1,0:T(8,128)S(1)}, u32[]{:S(2)}, u32[]{:S(2)}) collective-permute-start(f32[10,16,512]{2,1,0:T(8,128)S(1)} %get-tuple-element.85), channel_id=1, source_target_pairs={{0,64},{1,65},{2,66},{3,67},{4,68},{5,69},{6,70},{7,71},{8,72},{9,... | collective-permute-start | bytes 983048 | tf_op jit(solution)/shard_map/ppermute | solution.py:424
  38.8 10.9 %collective-permute-start.7 = (f32[8,16,512]{2,1,0:T(8,128)S(1)}, f32[8,16,512]{2,1,0:T(8,128)S(1)}, u32[]{:S(2)}, u32[]{:S(2)}) collective-permute-start(f32[8,16,512]{2,1,0:T(8,128)S(1)} %get-tuple-element.94.m0), channel_id=1, source_target_pairs={{0,64},{1,65},{2,66},{3,67},{4,68},{5,69},{6,70},{7,71},{8,72},{9,... | collective-permute-start | bytes 786440 | tf_op jit(solution)/shard_map/ppermute | solution.py:424
  42.0 7.7 %collective-permute-start.6 = (f32[2,16,512]{2,1,0:T(8,128)S(1)}, f32[2,16,512]{2,1,0:T(8,128)S(1)}, u32[]{:S(2)}, u32[]{:S(2)}) collective-permute-start(f32[2,16,512]{2,1,0:T(8,128)S(1)} %get-tuple-element.95), channel_id=1, source_target_pairs={{1,32},{2,33},{3,34},{4,35},{5,36},{6,37},{7,38},{8,39},{9,40},{10... | collective-permute-start | bytes 196616 | tf_op jit(solution)/shard_map/ppermute | solution.py:424
  49.8 10.8 %collective-permute-start.8 = (f32[9,16,512]{2,1,0:T(8,128)S(1)}, f32[9,16,512]{2,1,0:T(8,128)S(1)}, u32[]{:S(2)}, u32[]{:S(2)}) collective-permute-start(f32[9,16,512]{2,1,0:T(8,128)S(1)} %get-tuple-element.97), channel_id=1, source_target_pairs={{0,64},{1,65},{2,66},{3,67},{4,68},{5,69},{6,70},{7,71},{8,72},{9,... | collective-permute-start | bytes 884744 | tf_op jit(solution)/shard_map/ppermute | solution.py:424
  68.9 13.2 %collective-permute-start.10 = (f32[8,16,512]{2,1,0:T(8,128)S(1)}, f32[8,16,512]{2,1,0:T(8,128)S(1)}, u32[]{:S(2)}, u32[]{:S(2)}) collective-permute-start(f32[8,16,512]{2,1,0:T(8,128)S(1)} %get-tuple-element.100.t0), channel_id=1, source_target_pairs={{0,128},{1,129},{2,130},{3,131},{4,132},{5,133},{6,134},{7,135},{8... | collective-permute-start | bytes 786440 | tf_op jit(solution)/shard_map/ppermute | solution.py:424
  74.8 7.3 %collective-permute-start.9 = (f32[1,16,512]{2,1,0:T(8,128)S(1)}, f32[1,16,512]{2,1,0:T(8,128)S(1)}, u32[]{:S(2)}, u32[]{:S(2)}) collective-permute-start(f32[1,16,512]{2,1,0:T(8,128)S(1)} %get-tuple-element.101), channel_id=1, source_target_pairs={{1,32},{2,33},{3,34},{4,35},{5,36},{6,37},{7,38},{8,39},{9,40},{10... | collective-permute-start | bytes 98312 | tf_op jit(solution)/shard_map/ppermute | solution.py:424
  80.6 8.1 %copy-start.1 = (f32[1,1,16,16,512]{4,3,2,1,0:T(8,128)S(1)}, f32[1,1,16,16,512]{4,3,2,1,0:T(8,128)}, u32[]{:S(2)}) copy-start(f32[1,1,16,16,512]{4,3,2,1,0:T(8,128)} %param.3) | copy-start | bytes 1572868

commit v5 on v4

--- a/solution.py
+++ b/solution.py
@@ -269,13 +269,11 @@
         cpay[x] = cm[x + 2]
 
 
-def k_restrict_prev(part, z, gain, b, bm, m0, edge, ipay):
-    h = own_core()
+def k_restrict_prev(part, z, gain, bm, m0, edge, ipay):
     for x in range(8):
         value = part[x] + z[x]
         bm[x] = value
         m0[x] = gain[x + 2] * value
-        ipay[1 + x] = b[1 - h, x + 2]
     edge[0] = bm[0]
     edge[1] = bm[1]
     ipay[0] = m0[7]
@@ -294,7 +292,10 @@
         m1[x + 1] = smoothed_mid(m0[x], m0[x - 1], high, w, wx, gain, x + 2, bm[x])
 
 
-def k_mid_prev(w, wx, gain, bm, m0, edge, z, m10, m1, zpay, ipay):
+def k_mid_prev(w, wx, gain, bm, m0, edge, z, m10, b, m1, zpay, ipay):
+    h = own_core()
+    for x in range(8):
+        ipay[1 + x] = b[1 - h, x + 2]
     real = has_outer()
     far, near = gain[0] * edge[1], gain[1] * edge[0]
     for x in range(1, 8):
@@ -468,19 +469,19 @@
         cm_twin = send(pay, twin)
         wm, wxm, diagm, gainm = call(k_mid_faces, [(4, 10), (11,), (10,), (10,)], cm)
         bm, m0, pay, ipay = call(
-            k_restrict_prev, [(8,), (8,), (2,), (9,)], part, z1, gainm, b
+            k_restrict_prev, [(8,), (8,), (2,), (1,)], part, z1, gainm
         )
         z = send(m0, later)
         edge = send(pay, outer)
         near = gather(ipay, in_chip)
-        residual, ct = call(k_residual_out, [(16,), (10,)], b, near, cm, cm_twin)
         (m1,) = call(k_mid, [(9,)], wm, wxm, gainm, bm, m0, near, cm_twin, far=(6,))
         m1, zpay, ipay = call(
-            k_mid_prev, [(9,), (9,), (1,)], wm, wxm, gainm, bm, m0, edge, z, m1,
+            k_mid_prev, [(9,), (9,), (9,)], wm, wxm, gainm, bm, m0, edge, z, m1, b,
             alias=[(7, 0)],
         )
         z = send(zpay, later)
         near = gather(ipay, in_chip)
+        residual, ct = call(k_residual_out, [(16,), (10,)], b, near, cm, cm_twin)
         wt, wxt, gaint = call(k_top_faces, [(4, 8), (9,), (8,)], ct)
         (rm,) = call(k_mid_left, [(8,)], wm, wxm, diagm, bm, m1, near)
         (rm,) = call(

time: 90.2 us -> 90.2 us (level)
  no operation moved by 1% of the time
where the time goes in v5:
time: 90.2 us; the launch traced here: 89.6 us
  starting transfers between devices  42.7 us (47%)
  blocking collectives  22.1 us (25%)
  waiting for transfers between devices  13.8 us (15%)
  Pallas kernels  7.05 us (8%)
  local copies, waits for them, and re-layouts  3.11 us (3%)
    ppermute x11, starting transfers between devices, send(): return lax.ppermute(x, axes, route)  42.7 us
    all_gather x5, blocking collectives, gather(): return lax.all_gather(x, axes, axis_index_groups=groups)  22.1 us
    ppermute x11, waiting for transfers between devices, send(): return lax.ppermute(x, axes, route)  13.8 us
    pallas_call x21, Pallas kernels, call(): pl.pallas_call(kernel, out_shape=[jax.ShapeDtypeStruct(s + (16, 512), jnp...  6.15 us
    unnamed x8, local copies, waits for them, and re-layouts  3.11 us
  transfers between devices with their start and end apart: 11, of which 6 were waited for; matrix products, arithmetic and copies ran while one was open for 0% of the time, Pallas kernels for 6%

profile of v5, /device:TPU:189, one launch (start us, length us, event | category | flops | bytes accessed | tf_op | source)
XLA Modules:
  0.0 89.6 jit_solution(11875363147691715137)
XLA Ops:
  0.6 0.0 copy-start
  0.6 1.0 %copy-done = f32[1,1,16,16,512]{4,3,2,1,0:T(8,128)S(1)} copy-done((f32[1,1,16,16,512]{4,3,2,1,0:T(8,128)S(1)}, f32[1,1,16,16,512]{4,3,2,1,0:T(8,128)}, u32[]{:S(2)}) %copy-start) | copy-done | bytes 524312
  1.7 0.1 k_load_u.1
  1.8 0.0 copy-start.2
  1.8 1.0 %copy-done.2 = f32[1,1,16,16,512]{4,3,2,1,0:T(8,128)S(1)} copy-done((f32[1,1,16,16,512]{4,3,2,1,0:T(8,128)S(1)}, f32[1,1,16,16,512]{4,3,2,1,0:T(8,128)}, u32[]{:S(2)}) %copy-start.2) | copy-done | bytes 524312
  2.8 0.1 k_load_f.1
  2.9 2.6 %collective-permute-start = (f32[21,16,512]{2,1,0:T(8,128)S(1)}, f32[21,16,512]{2,1,0:T(8,128)S(1)}, u32[]{:S(2)}, u32[]{:S(2)}) collective-permute-start(f32[21,16,512]{2,1,0:T(8,128)S(1)} %get-tuple-element.58), channel_id=1, source_target_pairs={{0,32},{1,33},{2,34},{3,35},{4,36},{5,37},{6,38},{7,39},{8,40},{9,... | collective-permute-start | bytes 2064392 | tf_op jit(solution)/shard_map/ppermute | solution.py:425
  5.5 1.0 %copy-done.3 = f32[1,16,16,512]{3,2,1,0:T(8,128)S(1)} copy-done((f32[1,16,16,512]{3,2,1,0:T(8,128)S(1)}, f32[1,16,16,512]{3,2,1,0:T(8,128)}, u32[]{:S(2)}) %copy-start.3) | copy-done | bytes 524312
  6.6 0.1 k_load_k.1.ko
  6.7 0.6 collective-permute-done.got
  7.3 0.2 k_pack.1
  7.4 2.3 %collective-permute-start.2 = (f32[13,16,512]{2,1,0:T(8,128)S(1)}, f32[13,16,512]{2,1,0:T(8,128)S(1)}, u32[]{:S(2)}, u32[]{:S(2)}) collective-permute-start(f32[13,16,512]{2,1,0:T(8,128)S(1)} %get-tuple-element.62), channel_id=1, source_target_pairs={{1,32},{2,33},{3,34},{4,35},{5,36},{6,37},{7,38},{8,39},{9,40},{10... | collective-permute-start | bytes 1277960 | tf_op jit(solution)/shard_map/ppermute | solution.py:425
  9.7 4.0 %collective-permute-start.1 = (f32[10,16,512]{2,1,0:T(8,128)S(1)}, f32[10,16,512]{2,1,0:T(8,128)S(1)}, u32[]{:S(2)}, u32[]{:S(2)}) collective-permute-start(f32[10,16,512]{2,1,0:T(8,128)S(1)} %get-tuple-element.59), channel_id=1, source_target_pairs={{0,64},{1,65},{2,66},{3,67},{4,68},{5,69},{6,70},{7,71},{8,72},{9,... | collective-permute-start | bytes 983048 | tf_op jit(solution)/shard_map/ppermute | solution.py:425
  13.7 1.2 %k_inner.1 = (f32[4,2,12,16,512]{4,3,2,1,0:T(8,128)S(1)}, f32[2,13,16,512]{3,2,1,0:T(8,128)S(1)}, f32[2,12,16,512]{3,2,1,0:T(8,128)S(1)}, f32[2,12,16,512]{3,2,1...) custom-call(f32[2,11,16,512]{3,2,1,0:T(8,128)S(1)} %get-tuple-element.60, ...), custom_call_target="tpu_custom_call" | custom-call | flops 2621440 | bytes 1736704 | tf_op jit(solution)/shard_map/k_inner/pallas_call | solution.py:435
  15.0 4.0 %collective-permute-done.2.edge = f32[13,16,512]{2,1,0:T(8,128)S(1)} collective-permute-done((f32[13,16,512]{2,1,0:T(8,128)S(1)}, f32[13,16,512]{2,1,0:T(8,128)S(1)}, u32[]{:S(2)}, u32[]{:S(2)}) %collective-permute-start.2) | collective-permute-done | bytes 426016 | tf_op jit(solution)/shard_map/ppermute | solution.py:425
  19.0 0.5 k_edge.1
  19.4 4.0 %collective-permute-start.3 = (f32[12,16,512]{2,1,0:T(8,128)S(1)}, f32[12,16,512]{2,1,0:T(8,128)S(1)}, u32[]{:S(2)}, u32[]{:S(2)}) collective-permute-start(f32[12,16,512]{2,1,0:T(8,128)S(1)} %get-tuple-element.82), channel_id=1, source_target_pairs={{0,64},{1,65},{2,66},{3,67},{4,68},{5,69},{6,70},{7,71},{8,72},{9,... | collective-permute-start | bytes 1179656 | tf_op jit(solution)/shard_map/ppermute | solution.py:425
  23.5 0.1 k_prev.1
  23.6 0.5 k_fine.1
  24.1 5.2 %collective-permute-start.4 = (f32[8,16,512]{2,1,0:T(8,128)S(1)}, f32[8,16,512]{2,1,0:T(8,128)S(1)}, u32[]{:S(2)}, u32[]{:S(2)}) collective-permute-start(f32[8,16,512]{2,1,0:T(8,128)S(1)} %get-tuple-element.85), channel_id=1, source_target_pairs={{0,64},{1,65},{2,66},{3,67},{4,68},{5,69},{6,70},{7,71},{8,72},{9,... | collective-permute-start | bytes 786440 | tf_op jit(solution)/shard_map/ppermute | solution.py:425
  29.3 3.2 %collective-permute-done.3.z = f32[12,16,512]{2,1,0:T(8,128)S(1)} collective-permute-done((f32[12,16,512]{2,1,0:T(8,128)S(1)}, f32[12,16,512]{2,1,0:T(8,128)S(1)}, u32[]{:S(2)}, u32[]{:S(2)}) %collective-permute-start.3) | collective-permute-done | bytes 393248 | tf_op jit(solution)/shard_map/ppermute | solution.py:425
  32.5 0.2 k_fine_prev.1.e1
  32.7 0.5 k_restrict.1
  33.2 5.1 %collective-permute-start.7 = (f32[10,16,512]{2,1,0:T(8,128)S(1)}, f32[10,16,512]{2,1,0:T(8,128)S(1)}, u32[]{:S(2)}, u32[]{:S(2)}) collective-permute-start(f32[10,16,512]{2,1,0:T(8,128)S(1)} %get-tuple-element.90), channel_id=1, source_target_pairs={{0,64},{1,65},{2,66},{3,67},{4,68},{5,69},{6,70},{7,71},{8,72},{9,... | collective-permute-start | bytes 983048 | tf_op jit(solution)/shard_map/ppermute | solution.py:425
  38.3 0.4 k_mid_faces.1
  38.7 0.1 k_restrict_prev.1
  38.7 3.2 %collective-permute-start.6 = (f32[8,16,512]{2,1,0:T(8,128)S(1)}, f32[8,16,512]{2,1,0:T(8,128)S(1)}, u32[]{:S(2)}, u32[]{:S(2)}) collective-permute-start(f32[8,16,512]{2,1,0:T(8,128)S(1)} %get-tuple-element.87.m0), channel_id=1, source_target_pairs={{0,64},{1,65},{2,66},{3,67},{4,68},{5,69},{6,70},{7,71},{8,72},{9,... | collective-permute-start | bytes 786440 | tf_op jit(solution)/shard_map/ppermute | solution.py:425
  42.0 2.8 %collective-permute-start.5 = (f32[2,16,512]{2,1,0:T(8,128)S(1)}, f32[2,16,512]{2,1,0:T(8,128)S(1)}, u32[]{:S(2)}, u32[]{:S(2)}) collective-permute-start(f32[2,16,512]{2,1,0:T(8,128)S(1)} %get-tuple-element.88), channel_id=1, source_target_pairs={{1,32},{2,33},{3,34},{4,35},{5,36},{6,37},{7,38},{8,39},{9,40},{10... | collective-permute-start | bytes 196616 | tf_op jit(solution)/shard_map/ppermute | solution.py:425
  44.8 1.9 %all-gather = f32[2,16,512]{2,1,0:T(8,128)S(1)} all-gather(f32[1,16,512]{2,1,0:T(8,128)S(1)} %get-tuple-element.89), channel_id=2, replica_groups={{0,32},{1,33},{2,34},{3,35},{4,36},{5,37},{6,38},{7,39},{8,40},{9,41},{..., dimensions={0}, use_global_device_ids=true | all-gather | bytes 98304 | tf_op jit(solution)/shard_map/all_gather | solution.py:428
  46.7 0.2 k_mid.1.m10
  46.9 2.8 %collective-permute-done.5.edge = f32[2,16,512]{2,1,0:T(8,128)S(1)} collective-permute-done((f32[2,16,512]{2,1,0:T(8,128)S(1)}, f32[2,16,512]{2,1,0:T(8,128)S(1)}, u32[]{:S(2)}, u32[]{:S(2)}) %collective-permute-start.5) | collective-permute-done | bytes 65568 | tf_op jit(solution)/shard_map/ppermute | solution.py:425
  49.7 0.1 k_mid_prev.1
  49.8 5.0 %collective-permute-start.8 = (f32[9,16,512]{2,1,0:T(8,128)S(1)}, f32[9,16,512]{2,1,0:T(8,128)S(1)}, u32[]{:S(2)}, u32[]{:S(2)}) collective-permute-start(f32[9,16,512]{2,1,0:T(8,128)S(1)} %get-tuple-element.98), channel_id=1, source_target_pairs={{0,64},{1,65},{2,66},{3,67},{4,68},{5,69},{6,70},{7,71},{8,72},{9,... | collective-permute-start | bytes 884744 | tf_op jit(solution)/shard_map/ppermute | solution.py:425
  54.9 2.2 %all-gather.1 = f32[18,16,512]{2,1,0:T(8,128)S(1)} all-gather(f32[9,16,512]{2,1,0:T(8,128)S(1)} %get-tuple-element.91), channel_id=3, replica_groups={{0,32},{1,33},{2,34},{3,35},{4,36},{5,37},{6,38},{7,39},{8,40},{9,41},{..., dimensions={0}, use_global_device_ids=true | all-gather | bytes 884736 | tf_op jit(solution)/shard_map/all_gather | solution.py:428
  57.1 0.9 %k_residual_out.1 = (f32[16,16,512]{2,1,0:T(8,128)}, f32[10,16,512]{2,1,0:T(8,128)S(1)}) custom-call(f32[2,12,16,512]{3,2,1,0:T(8,128)S(1)} %get-tuple-element.73.b, f32[2,9,16,512]{3,2,1,0:T(8,128)S(1)} %bitcast.10, f32[12,16,512]{2,1,0:T(8,128)S(1)} %get-tuple-element.74.cm, f32[10,16,512]{2,1,0:T(8,128)S(1)} %collective-permute-done.7._.twin), custom_call_target="tpu_custom_call" | custom-call | flops 2621440 | bytes 2097152 | tf_op jit(solution)/shard_map/k_residual_out/pallas_call | solution.py:435
  58.0 0.3 k_top_faces.1
  58.3 0.2 k_mid_left.1.rm0
  58.6 2.0 %collective-permute-done.8.z = f32[9,16,512]{2,1,0:T(8,128)S(1)} collective-permute-done((f32[9,16,512]{2,1,0:T(8,128)S(1)}, f32[9,16,512]{2,1,0:T(8,128)S(1)}, u32[]{:S(2)}, u32[]{:S(2)}) %collective-permute-start.8) | collective-permute-done | bytes 294944 | tf_op jit(solution)/shard_map/ppermute | solution.py:425
  60.6 0.1 k_mid_left_prev.1
  60.7 8.2 %all-gather.2 = f32[16,16,512]{2,1,0:T(8,128)S(1)} all-gather(f32[8,16,512]{2,1,0:T(8,128)S(1)} %k_mid_left_prev.1), channel_id=4, replica_groups={{0,64},{1,65},{2,66},{3,67},{4,68},{5,69},{6,70},{7,71},{8,72},{9,73},{..., dimensions={0}, use_global_device_ids=true | all-gather | bytes 786432 | tf_op jit(solution)/shard_map/all_gather | solution.py:428
  68.9 5.8 %collective-permute-start.10 = (f32[8,16,512]{2,1,0:T(8,128)S(1)}, f32[8,16,512]{2,1,0:T(8,128)S(1)}, u32[]{:S(2)}, u32[]{:S(2)}) collective-permute-start(f32[8,16,512]{2,1,0:T(8,128)S(1)} %get-tuple-element.100.t0), channel_id=1, source_target_pairs={{0,128},{1,129},{2,130},{3,131},{4,132},{5,133},{6,134},{7,135},{8... | collective-permute-start | bytes 786440 | tf_op jit(solution)/shard_map/ppermute | solution.py:425
  74.7 2.6 %collective-permute-start.9 = (f32[1,16,512]{2,1,0:T(8,128)S(1)}, f32[1,16,512]{2,1,0:T(8,128)S(1)}, u32[]{:S(2)}, u32[]{:S(2)}) collective-permute-start(f32[1,16,512]{2,1,0:T(8,128)S(1)} %get-tuple-element.101), channel_id=1, source_target_pairs={{1,32},{2,33},{3,34},{4,35},{5,36},{6,37},{7,38},{8,39},{9,40},{10... | collective-permute-start | bytes 98312 | tf_op jit(solution)/shard_map/ppermute | solution.py:425
  77.4 3.3 %all-gather.3 = f32[2,16,512]{2,1,0:T(8,128)S(1)} all-gather(f32[1,16,512]{2,1,0:T(8,128)S(1)} %get-tuple-element.102), channel_id=5, replica_groups={{0,32},{1,33},{2,34},{3,35},{4,36},{5,37},{6,38},{7,39},{8,40},{9,41},{..., dimensions={0}, use_global_device_ids=true | all-gather | bytes 98304 | tf_op jit(solution)/shard_map/all_gather | solution.py:428
  80.6 0.3 k_top.1
  80.9 1.2 %collective-permute-done.9.edge = f32[1,16,512]{2,1,0:T(8,128)S(1)} collective-permute-done((f32[1,16,512]{2,1,0:T(8,128)S(1)}, f32[1,16,512]{2,1,0:T(8,128)S(1)}, u32[]{:S(2)}, u32[]{:S(2)}) %collective-permute-start.9) | collective-permute-done | bytes 32800 | tf_op jit(solution)/shard_map/ppermute | solution.py:425
  82.1 0.1 k_top_prev.1
  82.2 6.5 %all-gather.4 = f32[16,16,512]{2,1,0:T(8,128)S(1)} all-gather(f32[8,16,512]{2,1,0:T(8,128)S(1)} %get-tuple-element.106), channel_id=6, replica_groups={{0,32},{1,33},{2,34},{3,35},{4,36},{5,37},{6,38},{7,39},{8,40},{9,41},{..., dimensions={0}, use_global_device_ids=true | all-gather | bytes 786432 | tf_op jit(solution)/shard_map/all_gather | solution.py:428
  88.7 0.9 %k_state.1 = f32[16,16,512]{2,1,0:T(8,128)} custom-call(f32[16,16,512]{2,1,0:T(8,128)S(1)} %bitcast.13, f32[8,16,512]{2,1,0:T(8,128)S(1)} %get-tuple-element.105.mine, f32[2,8,16,512]{3,2,1,0:T(8,128)S(1)} %bitcast.14), custom_call_target="tpu_custom_call" | custom-call | tf_op jit(solution)/shard_map/k_state/pallas_call | solution.py:503
  (9 shorter events, 0.1 us)
Async XLA Ops:
  0.6 1.0 %copy-start = (f32[1,1,16,16,512]{4,3,2,1,0:T(8,128)S(1)}, f32[1,1,16,16,512]{4,3,2,1,0:T(8,128)}, u32[]{:S(2)}) copy-start(f32[1,1,16,16,512]{4,3,2,1,0:T(8,128)} %param.3) | copy-start | bytes 1572868
  1.8 1.0 %copy-start.2 = (f32[1,1,16,16,512]{4,3,2,1,0:T(8,128)S(1)}, f32[1,1,16,16,512]{4,3,2,1,0:T(8,128)}, u32[]{:S(2)}) copy-start(f32[1,1,16,16,512]{4,3,2,1,0:T(8,128)} %param.4) | copy-start | bytes 1572868
  2.9 4.3 %collective-permute-start = (f32[21,16,512]{2,1,0:T(8,128)S(1)}, f32[21,16,512]{2,1,0:T(8,128)S(1)}, u32[]{:S(2)}, u32[]{:S(2)}) collective-permute-start(f32[21,16,512]{2,1,0:T(8,128)S(1)} %get-tuple-element.58), channel_id=1, source_target_pairs={{0,32},{1,33},{2,34},{3,35},{4,36},{5,37},{6,38},{7,39},{8,40},{9,... | collective-permute-start | bytes 2064392 | tf_op jit(solution)/shard_map/ppermute | solution.py:425
  5.5 1.0 %copy-start.3 = (f32[1,16,16,512]{3,2,1,0:T(8,128)S(1)}, f32[1,16,16,512]{3,2,1,0:T(8,128)}, u32[]{:S(2)}) copy-start(f32[1,16,16,512]{3,2,1,0:T(8,128)} %param.5) | copy-start | bytes 1572868
  7.4 11.6 %collective-permute-start.2 = (f32[13,16,512]{2,1,0:T(8,128)S(1)}, f32[13,16,512]{2,1,0:T(8,128)S(1)}, u32[]{:S(2)}, u32[]{:S(2)}) collective-permute-start(f32[13,16,512]{2,1,0:T(8,128)S(1)} %get-tuple-element.62), channel_id=1, source_target_pairs={{1,32},{2,33},{3,34},{4,35},{5,36},{6,37},{7,38},{8,39},{9,40},{10... | collective-permute-start | bytes 1277960 | tf_op jit(solution)/shard_map/ppermute | solution.py:425
  9.7 13.7 %collective-permute-start.1 = (f32[10,16,512]{2,1,0:T(8,128)S(1)}, f32[10,16,512]{2,1,0:T(8,128)S(1)}, u32[]{:S(2)}, u32[]{:S(2)}) collective-permute-start(f32[10,16,512]{2,1,0:T(8,128)S(1)} %get-tuple-element.59), channel_id=1, source_target_pairs={{0,64},{1,65},{2,66},{3,67},{4,68},{5,69},{6,70},{7,71},{8,72},{9,... | collective-permute-start | bytes 983048 | tf_op jit(solution)/shard_map/ppermute | solution.py:425
  19.4 13.1 %collective-permute-start.3 = (f32[12,16,512]{2,1,0:T(8,128)S(1)}, f32[12,16,512]{2,1,0:T(8,128)S(1)}, u32[]{:S(2)}, u32[]{:S(2)}) collective-permute-start(f32[12,16,512]{2,1,0:T(8,128)S(1)} %get-tuple-element.82), channel_id=1, source_target_pairs={{0,64},{1,65},{2,66},{3,67},{4,68},{5,69},{6,70},{7,71},{8,72},{9,... | collective-permute-start | bytes 1179656 | tf_op jit(solution)/shard_map/ppermute | solution.py:425
  24.1 14.6 %collective-permute-start.4 = (f32[8,16,512]{2,1,0:T(8,128)S(1)}, f32[8,16,512]{2,1,0:T(8,128)S(1)}, u32[]{:S(2)}, u32[]{:S(2)}) collective-permute-start(f32[8,16,512]{2,1,0:T(8,128)S(1)} %get-tuple-element.85), channel_id=1, source_target_pairs={{0,64},{1,65},{2,66},{3,67},{4,68},{5,69},{6,70},{7,71},{8,72},{9,... | collective-permute-start | bytes 786440 | tf_op jit(solution)/shard_map/ppermute | solution.py:425
  33.2 13.5 %collective-permute-start.7 = (f32[10,16,512]{2,1,0:T(8,128)S(1)}, f32[10,16,512]{2,1,0:T(8,128)S(1)}, u32[]{:S(2)}, u32[]{:S(2)}) collective-permute-start(f32[10,16,512]{2,1,0:T(8,128)S(1)} %get-tuple-element.90), channel_id=1, source_target_pairs={{0,64},{1,65},{2,66},{3,67},{4,68},{5,69},{6,70},{7,71},{8,72},{9,... | collective-permute-start | bytes 983048 | tf_op jit(solution)/shard_map/ppermute | solution.py:425
  38.7 10.9 %collective-permute-start.6 = (f32[8,16,512]{2,1,0:T(8,128)S(1)}, f32[8,16,512]{2,1,0:T(8,128)S(1)}, u32[]{:S(2)}, u32[]{:S(2)}) collective-permute-start(f32[8,16,512]{2,1,0:T(8,128)S(1)} %get-tuple-element.87.m0), channel_id=1, source_target_pairs={{0,64},{1,65},{2,66},{3,67},{4,68},{5,69},{6,70},{7,71},{8,72},{9,... | collective-permute-start | bytes 786440 | tf_op jit(solution)/shard_map/ppermute | solution.py:425
  42.0 7.7 %collective-permute-start.5 = (f32[2,16,512]{2,1,0:T(8,128)S(1)}, f32[2,16,512]{2,1,0:T(8,128)S(1)}, u32[]{:S(2)}, u32[]{:S(2)}) collective-permute-start(f32[2,16,512]{2,1,0:T(8,128)S(1)} %get-tuple-element.88), channel_id=1, source_target_pairs={{1,32},{2,33},{3,34},{4,35},{5,36},{6,37},{7,38},{8,39},{9,40},{10... | collective-permute-start | bytes 196616 | tf_op jit(solution)/shard_map/ppermute | solution.py:425
  49.8 10.8 %collective-permute-start.8 = (f32[9,16,512]{2,1,0:T(8,128)S(1)}, f32[9,16,512]{2,1,0:T(8,128)S(1)}, u32[]{:S(2)}, u32[]{:S(2)}) collective-permute-start(f32[9,16,512]{2,1,0:T(8,128)S(1)} %get-tuple-element.98), channel_id=1, source_target_pairs={{0,64},{1,65},{2,66},{3,67},{4,68},{5,69},{6,70},{7,71},{8,72},{9,... | collective-permute-start | bytes 884744 | tf_op jit(solution)/shard_map/ppermute | solution.py:425
  68.9 13.2 %collective-permute-start.10 = (f32[8,16,512]{2,1,0:T(8,128)S(1)}, f32[8,16,512]{2,1,0:T(8,128)S(1)}, u32[]{:S(2)}, u32[]{:S(2)}) collective-permute-start(f32[8,16,512]{2,1,0:T(8,128)S(1)} %get-tuple-element.100.t0), channel_id=1, source_target_pairs={{0,128},{1,129},{2,130},{3,131},{4,132},{5,133},{6,134},{7,135},{8... | collective-permute-start | bytes 786440 | tf_op jit(solution)/shard_map/ppermute | solution.py:425
  74.7 7.3 %collective-permute-start.9 = (f32[1,16,512]{2,1,0:T(8,128)S(1)}, f32[1,16,512]{2,1,0:T(8,128)S(1)}, u32[]{:S(2)}, u32[]{:S(2)}) collective-permute-start(f32[1,16,512]{2,1,0:T(8,128)S(1)} %get-tuple-element.101), channel_id=1, source_target_pairs={{1,32},{2,33},{3,34},{4,35},{5,36},{6,37},{7,38},{8,39},{9,40},{10... | collective-permute-start | bytes 98312 | tf_op jit(solution)/shard_map/ppermute | solution.py:425
  80.6 8.1 %copy-start.1 = (f32[1,1,16,16,512]{4,3,2,1,0:T(8,128)S(1)}, f32[1,1,16,16,512]{4,3,2,1,0:T(8,128)}, u32[]{:S(2)}) copy-start(f32[1,1,16,16,512]{4,3,2,1,0:T(8,128)} %param.3) | copy-start | bytes 1572868
